TPU v7x, 256 devices: a whole 4x4x8 slice. The times are simulated.
256 devices in a mesh: blk: 32 (over z, x_hi, core), tp: 8 (over x_lo, y).
Axes of the slice: x: 4 (x_hi: 2, x_lo: 2; x = x_hi * 2 + x_lo), y: 4, z: 8, core: 2. Of those that a mesh axis runs over, the one named last changes fastest.
Arguments:
- queries: bfloat16 [16384, 8192], P('blk', 'tp'), may hold values from -6 to 6
- key_matrix: bfloat16 [16384, 1024], P('blk', 'tp'), may hold values from -6 to 6
- value_matrix: bfloat16 [16384, 1024], P('blk', 'tp'), may hold values from -6 to 6
- attention_output: bfloat16 [16384, 8192], P('blk', 'tp'), may hold values from -1.5 to 1.5
- output_gradient: bfloat16 [16384, 8192], P('blk', 'tp'), may hold values from -24 to 24
- softmax_log_total: float32 [64, 16384], P('tp', 'blk'), may hold values from 5 to 7.5
- positions: int32 [16384], P(('blk', 'tp')), may hold values from 0 to 16383, as said below
Outputs:
- query_grad: bfloat16 [16384, 8192], P('blk', 'tp')
- key_gradient: bfloat16 [16384, 1024], P('blk', 'tp')
- value_gradient: bfloat16 [16384, 1024], P('blk', 'tp')
Inputs may be any that keep to these rules, and one draw needn't show every extreme that they name: Every position occurs once. Block b (tokens b * 512 to b * 512 + 511) holds two runs of 256 consecutive positions in rising order: first piece c, then piece 2 * 32 - 1 - c, where piece m is positions m * 256 to (m + 1) * 256 - 1, and the c of the blocks are distinct.
All inputs are finite; a program needn't handle non-finite values.
Results may differ from a plain program's by a relative error of at most 0.0051.
Values may be sent and summed in bfloat16 or wider, within the bound.
No kernel may reach another device: no remote copies, remote signals or barrier semaphores. Data moves between devices by JAX's collectives and lax.ppermute only.
A program may use at most 64 MiB of HBM per device.

v0:
```python
import math

import jax
import jax.numpy as jnp
from jax import lax
from jax.sharding import PartitionSpec as P

HEAD_SIZE = 128
STEPS = 2


def passed_along(value, axis, steps):
    count = lax.axis_size(axis)
    pairs = [(source, (source + steps) % count) for source in range(count)]
    return lax.ppermute(value, axis, pairs)


def attend(query_four, grad_four, norm_rows, row_dot, key_block, value_block, allowed):
    score_scale = 1.0 / math.sqrt(HEAD_SIZE)
    scores = (
        jnp.einsum("ikgd,jkd->kgij", query_four, key_block, preferred_element_type=jnp.float32)
        * score_scale
    )
    weights = jnp.exp(scores - norm_rows[..., None])
    weights = jnp.where(allowed, weights, 0.0)
    rounded = weights.astype(jnp.bfloat16)
    value_part = jnp.einsum(
        "kgij,ikgd->jkd", rounded, grad_four, preferred_element_type=jnp.float32
    )
    grad_weights = jnp.einsum(
        "ikgd,jkd->kgij", grad_four, value_block, preferred_element_type=jnp.float32
    )
    grad_scores = (weights * (grad_weights - row_dot[..., None])).astype(jnp.bfloat16)
    query_part = (
        jnp.einsum("kgij,jkd->ikgd", grad_scores, key_block, preferred_element_type=jnp.float32)
        * score_scale
    )
    key_part = (
        jnp.einsum("kgij,ikgd->jkd", grad_scores, query_four, preferred_element_type=jnp.float32)
        * score_scale
    )
    return (query_part, key_part, value_part)


def on_device(
    queries,
    key_matrix,
    value_matrix,
    attention_output,
    output_gradient,
    softmax_log_total,
    positions,
):
    tokens = queries.shape[0]
    half_len = tokens // 2
    kv_heads = key_matrix.shape[1] // HEAD_SIZE
    q_heads = queries.shape[1] // HEAD_SIZE
    query_group_width = q_heads // kv_heads
    own_pos = lax.all_gather(positions, "tp", axis=0, tiled=True)
    query_four = queries.reshape(tokens, kv_heads, query_group_width, HEAD_SIZE)
    grad_four = output_gradient.reshape(tokens, kv_heads, query_group_width, HEAD_SIZE)
    norm_rows = softmax_log_total.reshape(kv_heads, query_group_width, tokens)
    products = output_gradient.astype(jnp.float32) * attention_output.astype(jnp.float32)
    row_dot = jnp.sum(
        products.reshape(tokens, kv_heads, query_group_width, HEAD_SIZE), axis=3
    ).transpose(1, 2, 0)
    own_ids = jnp.stack([own_pos[0] // half_len, own_pos[half_len] // half_len]).astype(
        jnp.bfloat16
    )
    key_three = key_matrix.reshape(tokens, kv_heads, HEAD_SIZE)
    value_three = value_matrix.reshape(tokens, kv_heads, HEAD_SIZE)
    local_allowed = own_pos[None, :] <= own_pos[:, None]
    query_total, key_total, value_total = attend(
        query_four, grad_four, norm_rows, row_dot, key_three, value_three, local_allowed
    )
    moving = (key_matrix, value_matrix, own_ids)
    key_parts = []
    value_parts = []
    for offset in range(STEPS):
        moving = passed_along((moving[0], moving[1], moving[2]), "blk", 1)
        key_block = moving[0].reshape(tokens, kv_heads, HEAD_SIZE)
        value_block = moving[1].reshape(tokens, kv_heads, HEAD_SIZE)
        their_ids = moving[2].astype(jnp.int32)
        within = jnp.arange(half_len, dtype=jnp.int32)
        key_pos = jnp.concatenate(
            [their_ids[0] * half_len + within, their_ids[1] * half_len + within]
        )
        allowed = key_pos[None, :] <= own_pos[:, None]
        query_part, key_part, value_part = attend(
            query_four, grad_four, norm_rows, row_dot, key_block, value_block, allowed
        )
        query_total = query_total + query_part
        key_parts.append(key_part)
        value_parts.append(value_part)
    carried = (jnp.zeros_like(key_total), jnp.zeros_like(value_total))
    for offset in range(STEPS, 0, -1):
        summed = (carried[0] + key_parts[offset - 1], carried[1] + value_parts[offset - 1])
        carried = passed_along((summed[0], summed[1]), "blk", -1)
    key_total = key_total + carried[0]
    value_total = value_total + carried[1]
    query_grad = query_total.reshape(tokens, q_heads * HEAD_SIZE).astype(jnp.bfloat16)
    key_gradient = key_total.reshape(tokens, kv_heads * HEAD_SIZE).astype(jnp.bfloat16)
    value_gradient = value_total.reshape(tokens, kv_heads * HEAD_SIZE).astype(jnp.bfloat16)
    return (query_grad, key_gradient, value_gradient)


def solution(mesh):
    in_specs = (
        P("blk", "tp"),
        P("blk", "tp"),
        P("blk", "tp"),
        P("blk", "tp"),
        P("blk", "tp"),
        P("tp", "blk"),
        P(("blk", "tp")),
    )
    out_specs = (P("blk", "tp"), P("blk", "tp"), P("blk", "tp"))
    return jax.shard_map(
        on_device, mesh=mesh, in_specs=in_specs, out_specs=out_specs, check_vma=False
    )
```

profile of v0, /device:TPU:101, one launch (start us, length us, event | category | flops | bytes accessed | tf_op | source)
XLA Modules:
  0.0 90.3 jit_solution(4462790095112876925)
XLA Ops:
  0.6 0.0 copy-start
  0.6 0.0 copy-start.4
  0.7 1.4 %dynamic-slice = u32[1]{0:T(128)} dynamic-slice(u32[256]{0:T(256)} %constant.37, u32[]{:T(128)S(6)} %add.71), dynamic_slice_sizes={1} | dynamic-slice | bytes 12
  2.7 0.9 dynamic-update-slice
  3.5 9.2 %all-reduce = s32[512]{0:T(512)S(1)} all-reduce(s32[512]{0:T(512)S(1)} %dynamic-update-slice), channel_id=1, replica_groups=mesh['blk'=32,'tp'=8] {'tp'}, use_global_device_ids=true, to_apply=%add | all-reduce | flops 512 | bytes 4096
  12.8 0.5 fusion.95
  18.5 0.1 pad_maximum_fusion
  18.6 6.3 %collective-permute-start = (bf16[2]{0:T(256)(128)(2,1)S(1)}, bf16[2]{0:T(256)(128)(2,1)S(1)}, u32[]{:S(2)}, u32[]{:S(2)}) collective-permute-start(bf16[2]{0:T(256)(128)(2,1)S(1)} %pad_maximum_fusion), channel_id=1, source_target_pairs={{0,8},{8,16},{16,24},{24,32},{32,40},{40,48},{48,56},{56,64},{64,7... | collective-permute-start | bytes 20 | tf_op jit(solution)/shard_map/ppermute | solution.py:15
  24.8 0.1 collective-permute-start.2
  24.9 2.8 %collective-permute-start.1 = (bf16[512,128]{1,0:T(8,128)(2,1)}, bf16[512,128]{1,0:T(8,128)(2,1)}, u32[]{:S(2)}, u32[]{:S(2)}) collective-permute-start(bf16[512,128]{1,0:T(8,128)(2,1)} %param.8), channel_id=1, source_target_pairs={{0,8},{8,16},{16,24},{24,32},{32,40},{40,48},{48,56},{56,64},{64,7... | collective-permute-start | bytes 393224 | tf_op jit(solution)/shard_map/ppermute | solution.py:15
  27.7 1.9 %multiply_bitcast_fusion = f32[64,8,8,128]{3,1,2,0:T(8,128)S(1)} fusion(bf16[512,1024]{1,0:T(8,128)(2,1)} %param.10, bf16[512,1024]{1,0:T(8,128)(2,1)} %param.11), kind=kLoop, calls=%fused_computation.34 | loop fusion | flops 1572864 | bytes 4194304
  29.6 0.5 copy.60
  30.1 0.6 reduce_sum.11
  30.7 0.0 copy-start.3
  30.7 0.7 copy.31
  31.4 1.3 %fusion.62 = f32[512,512,8]{1,0,2:T(8,128)S(1)} fusion(bf16[512,128]{1,0:T(8,128)(2,1)S(1)} %copy-done.4, bf16[512,1024]{1,0:T(8,128)(2,1)S(1)} %copy-done), kind=kOutput, calls=%fused_computation.62 | convolution fusion | flops 536870912 | bytes 9568256 | tf_op jit(solution)/shard_map/ikgd,jkd->kgij/dot_general | solution.py:21
  32.7 0.0 copy-start.5
  32.7 0.0 copy-start.6
  32.8 0.6 fusion.97
  34.7 0.2 collective-permute-start.3
  34.8 1.0 %collective-permute-done.3 = bf16[2]{0:T(256)(128)(2,1)S(1)} collective-permute-done((bf16[2]{0:T(256)(128)(2,1)S(1)}, bf16[2]{0:T(256)(128)(2,1)S(1)}, u32[]{:S(2)}, u32[]{:S(2)}) %collective-permute-start.3) | collective-permute-done | bytes 36 | tf_op jit(solution)/shard_map/ppermute | solution.py:15
  35.9 0.6 fusion.96
  37.8 0.5 broadcast_compare_fusion
  38.3 1.6 %fusion.42 = f32[512,1,128]{2,0,1:T(8,128)S(1)} fusion(f32[512,512,8]{1,0,2:T(8,128)S(1)} %fusion.62, f32[8,512]{1,0:T(8,128)S(1)} %copy-done.7, pred[512,512]{0,1:T(8,128)(4,1)S(1)} %get-tuple-element.10, bf16[512,1024]{1,0:T(8,128)(2,1)S(1)} %copy-done.3), kind=kOutput, calls=%fused_computation.46 | convolution fusion | flops 545259520 | bytes 9977856 | tf_op jit(solution)/shard_map/kgij,ikgd->jkd/dot_general | solution.py:27
  40.0 3.0 %fusion.18 = bf16[8,512,512]{1,2,0:T(8,128)(2,1)S(1)} fusion(f32[512,512,8]{1,0,2:T(8,128)S(1)} %fusion.62, f32[8,512]{1,0:T(8,128)S(1)} %copy-done.5, f32[8,512]{1,0:T(8,128)S(1)} %copy-done.7, pred[512,512]{0,1:T(8,128)(4,1)S(1)} %get-tuple-element.10, bf16[512,128]{1,0:T(8,128)(2,1)S(1)} %copy-done.6, bf16[512,1024]{1,0:T(8,128)(2,1)S(1)} %copy-done.3), kind=kOutput, calls=%fused_computation.24 | convolution fusion | flops 549453824 | bytes 14057472 | tf_op jit(solution)/shard_map/ikgd,jkd->kgij/dot_general | solution.py:30
  42.9 1.3 %fusion.35 = f32[512,1,128]{2,0,1:T(8,128)S(1)} fusion(bf16[8,512,512]{1,2,0:T(8,128)(2,1)S(1)} %fusion.18, bf16[512,1024]{1,0:T(8,128)(2,1)S(1)} %copy-done), kind=kOutput, calls=%fused_computation.43 | convolution fusion | flops 536936448 | bytes 5505024 | tf_op jit(solution)/shard_map/kgij,ikgd->jkd/dot_general | solution.py:39
  44.2 0.8 fusion.86
  45.0 5.8 %collective-permute-start.4 = (bf16[512,128]{1,0:T(8,128)(2,1)}, bf16[512,128]{1,0:T(8,128)(2,1)S(1)}, u32[]{:S(2)}, u32[]{:S(2)}) collective-permute-start(bf16[512,128]{1,0:T(8,128)(2,1)} %collective-permute-done.1), channel_id=1, source_target_pairs={{0,8},{8,16},{16,24},{24,32},{32,40},{40,48},{48,56},{56,64},{64,7... | collective-permute-start | bytes 393224 | tf_op jit(solution)/shard_map/ppermute | solution.py:15
  50.8 2.2 %fusion.60 = f32[512,512,8]{1,0,2:T(8,128)S(1)} fusion(bf16[512,128]{1,0:T(8,128)(2,1)} %collective-permute-done.1, bf16[512,1024]{1,0:T(8,128)(2,1)S(1)} %copy-done), kind=kOutput, calls=%fused_computation.60 | convolution fusion | flops 536870912 | bytes 9568256 | tf_op jit(solution)/shard_map/ikgd,jkd->kgij/dot_general | solution.py:21
  53.0 0.1 collective-permute-start.5
  53.1 3.9 %fusion.19 = bf16[8,512,512]{1,2,0:T(8,128)(2,1)S(1)} fusion(f32[512,512,8]{1,0,2:T(8,128)S(1)} %fusion.60, f32[8,512]{1,0:T(8,128)S(1)} %copy-done.5, f32[8,512]{1,0:T(8,128)S(1)} %copy-done.7, pred[512,512]{0,1:T(8,128)(4,1)S(1)} %get-tuple-element.11, bf16[512,128]{1,0:T(8,128)(2,1)} %collective-permute-done.2, bf16[512,1024]{1,0:T(8,128)(2,1)S(1)} %copy-done.3), kind=kOutput, calls=%fused_computation.25 | convolution fusion | flops 549453824 | bytes 14057472 | tf_op jit(solution)/shard_map/ikgd,jkd->kgij/dot_general | solution.py:30
  57.0 1.8 %fusion.82 = f32[8,512,128]{1,2,0:T(8,128)S(1)} fusion(bf16[8,512,512]{1,2,0:T(8,128)(2,1)S(1)} %fusion.19, bf16[512,128]{1,0:T(8,128)(2,1)} %collective-permute-done.1), kind=kOutput, calls=%fused_computation.87 | convolution fusion | flops 536870912 | bytes 6422528 | tf_op jit(solution)/shard_map/kgij,jkd->ikgd/dot_general | solution.py:35
  58.8 1.3 %fusion.58 = f32[512,512,8]{1,0,2:T(8,128)S(1)} fusion(bf16[512,128]{1,0:T(8,128)(2,1)S(1)} %collective-permute-done.4, bf16[512,1024]{1,0:T(8,128)(2,1)S(1)} %copy-done), kind=kOutput, calls=%fused_computation.58 | convolution fusion | flops 536870912 | bytes 9568256 | tf_op jit(solution)/shard_map/ikgd,jkd->kgij/dot_general | solution.py:21
  60.1 3.0 %fusion.20 = bf16[8,512,512]{1,2,0:T(8,128)(2,1)S(1)} fusion(f32[512,512,8]{1,0,2:T(8,128)S(1)} %fusion.58, f32[8,512]{1,0:T(8,128)S(1)} %copy-done.5, f32[8,512]{1,0:T(8,128)S(1)} %copy-done.7, pred[512,512]{0,1:T(8,128)(4,1)S(1)} %get-tuple-element.9, bf16[512,128]{1,0:T(8,128)(2,1)S(1)} %collective-permute-done.5, bf16[512,1024]{1,0:T(8,128)(2,1)S(1)} %copy-done.3), kind=kOutput, calls=%fused_computation.26 | convolution fusion | flops 549453824 | bytes 14057472 | tf_op jit(solution)/shard_map/ikgd,jkd->kgij/dot_general | solution.py:30
  63.1 1.3 %fusion.34 = f32[512,1,128]{2,0,1:T(8,128)S(1)} fusion(bf16[8,512,512]{1,2,0:T(8,128)(2,1)S(1)} %fusion.20, bf16[512,1024]{1,0:T(8,128)(2,1)S(1)} %copy-done), kind=kOutput, calls=%fused_computation.42 | convolution fusion | flops 536936448 | bytes 5505024 | tf_op jit(solution)/shard_map/kgij,ikgd->jkd/dot_general | solution.py:39
  64.4 0.5 collective-permute-start.6
  64.9 1.6 %fusion.36 = f32[512,1,128]{2,0,1:T(8,128)S(1)} fusion(f32[512,512,8]{1,0,2:T(8,128)S(1)} %fusion.58, f32[8,512]{1,0:T(8,128)S(1)} %copy-done.7, pred[512,512]{0,1:T(8,128)(4,1)S(1)} %get-tuple-element.9, bf16[512,1024]{1,0:T(8,128)(2,1)S(1)} %copy-done.3), kind=kOutput, calls=%fused_computation.44 | convolution fusion | flops 545259520 | bytes 9977856 | tf_op jit(solution)/shard_map/kgij,ikgd->jkd/dot_general | solution.py:27
  66.6 0.1 collective-permute-start.8
  66.7 7.2 %collective-permute-done.6 = f32[512,1,128]{2,0,1:T(8,128)S(1)} collective-permute-done((f32[512,1,128]{2,0,1:T(8,128)S(1)}, f32[512,1,128]{2,0,1:T(8,128)S(1)}, u32[]{:S(2)}, u32[]{:S(2)}) %collective-permute-start.6) | collective-permute-done | bytes 262176 | tf_op jit(solution)/shard_map/ppermute | solution.py:15
  73.9 1.2 %fusion.48 = f32[512,1,128]{2,0,1:T(8,128)S(1)} fusion(f32[512,1,128]{2,0,1:T(8,128)S(1)} %collective-permute-done.6, bf16[8,512,512]{1,2,0:T(8,128)(2,1)S(1)} %copy-done.2, bf16[512,1024]{1,0:T(8,128)(2,1)S(1)} %copy-done), kind=kOutput, calls=%fused_computation.48 | convolution fusion | flops 537001984 | bytes 5767168 | tf_op jit(solution)/shard_map/kgij,ikgd->jkd/dot_general | solution.py:39
  75.1 0.3 collective-permute-start.7
  75.5 1.2 %collective-permute-done.8 = f32[512,1,128]{2,0,1:T(8,128)S(1)} collective-permute-done((f32[512,1,128]{2,0,1:T(8,128)S(1)}, f32[512,1,128]{2,0,1:T(8,128)S(1)}, u32[]{:S(2)}, u32[]{:S(2)}) %collective-permute-start.8) | collective-permute-done | bytes 262176 | tf_op jit(solution)/shard_map/ppermute | solution.py:15
  76.7 2.6 %fusion.45 = f32[512,1,128]{2,0,1:T(8,128)} fusion(f32[512,1,128]{2,0,1:T(8,128)S(1)} %collective-permute-done.8, f32[512,512,8]{1,0,2:T(8,128)S(1)} %fusion.60, f32[8,512]{1,0:T(8,128)S(1)} %copy-done.7, pred[512,512]{0,1:T(8,128)(4,1)S(1)} %get-tuple-element.11, bf16[512,1024]{1,0:T(8,128)(2,1)S(1)} %copy-done.3), kind=kOutput, calls=%fused_computation.47 | convolution fusion | flops 545325056 | bytes 10240000 | tf_op jit(solution)/shard_map/kgij,ikgd->jkd/dot_general | solution.py:27
  79.3 1.2 %multiply_convert_fusion = bf16[8,512,128]{1,2,0:T(8,128)(2,1)S(1)} fusion(f32[8,512,128]{1,2,0:T(8,128)S(1)} %fusion.86, f32[8,512,128]{1,2,0:T(8,128)S(1)} %fusion.82, bf16[8,512,512]{1,2,0:T(8,128)(2,1)S(1)} %fusion.20, bf16[512,128]{1,0:T(8,128)(2,1)S(1)} %collective-permute-done.4), kind=kOutput, calls=%fused_computation.33 | convolution fusion | flops 538968064 | bytes 9568256 | tf_op jit(solution)/shard_map/kgij,jkd->ikgd/dot_general | solution.py:35
  80.5 1.3 %copy.48 = bf16[512,1024]{1,0:T(8,128)(2,1)} copy(bf16[512,1024]{0,1:T(8,128)(2,1)S(1)} %bitcast.304) | data formatting | bytes 2097152
  81.8 7.1 %collective-permute-done.9 = f32[512,1,128]{2,0,1:T(8,128)S(1)} collective-permute-done((f32[512,1,128]{2,0,1:T(8,128)}, f32[512,1,128]{2,0,1:T(8,128)S(1)}, u32[]{:S(2)}, u32[]{:S(2)}) %collective-permute-start.9) | collective-permute-done | bytes 262176 | tf_op jit(solution)/shard_map/ppermute | solution.py:15
  88.9 0.7 fusion.77
  89.6 0.7 fusion.76
  (25 shorter events, 0.1 us)
Async XLA Ops:
  0.6 30.8 %copy-start = (bf16[512,1024]{1,0:T(8,128)(2,1)S(1)}, bf16[512,1024]{1,0:T(8,128)(2,1)}, u32[]{:S(2)}) copy-start(bf16[512,1024]{1,0:T(8,128)(2,1)} %param.7) | copy-start | bytes 3145732
  0.6 30.8 %copy-start.4 = (bf16[512,128]{1,0:T(8,128)(2,1)S(1)}, bf16[512,128]{1,0:T(8,128)(2,1)}, u32[]{:S(2)}) copy-start(bf16[512,128]{1,0:T(8,128)(2,1)} %param.8) | copy-start | bytes 393220
  18.6 14.1 %collective-permute-start = (bf16[2]{0:T(256)(128)(2,1)S(1)}, bf16[2]{0:T(256)(128)(2,1)S(1)}, u32[]{:S(2)}, u32[]{:S(2)}) collective-permute-start(bf16[2]{0:T(256)(128)(2,1)S(1)} %pad_maximum_fusion), channel_id=1, source_target_pairs={{0,8},{8,16},{16,24},{24,32},{32,40},{40,48},{48,56},{56,64},{64,7... | collective-permute-start | bytes 20 | tf_op jit(solution)/shard_map/ppermute | solution.py:15
  24.8 28.2 %collective-permute-start.2 = (bf16[512,128]{1,0:T(8,128)(2,1)}, bf16[512,128]{1,0:T(8,128)(2,1)}, u32[]{:S(2)}, u32[]{:S(2)}) collective-permute-start(bf16[512,128]{1,0:T(8,128)(2,1)} %param.9), channel_id=1, source_target_pairs={{0,8},{8,16},{16,24},{24,32},{32,40},{40,48},{48,56},{56,64},{64,7... | collective-permute-start | bytes 393224 | tf_op jit(solution)/shard_map/ppermute | solution.py:15
  24.9 20.1 %collective-permute-start.1 = (bf16[512,128]{1,0:T(8,128)(2,1)}, bf16[512,128]{1,0:T(8,128)(2,1)}, u32[]{:S(2)}, u32[]{:S(2)}) collective-permute-start(bf16[512,128]{1,0:T(8,128)(2,1)} %param.8), channel_id=1, source_target_pairs={{0,8},{8,16},{16,24},{24,32},{32,40},{40,48},{48,56},{56,64},{64,7... | collective-permute-start | bytes 393224 | tf_op jit(solution)/shard_map/ppermute | solution.py:15
  30.7 7.6 %copy-start.3 = (bf16[512,1024]{1,0:T(8,128)(2,1)S(1)}, bf16[512,1024]{1,0:T(8,128)(2,1)}, u32[]{:S(2)}) copy-start(bf16[512,1024]{1,0:T(8,128)(2,1)} %param.11) | copy-start | bytes 3145732
  31.4 6.9 %copy-start.7 = (f32[8,512]{1,0:T(8,128)S(1)}, f32[8,512]{1,0:T(8,128)}, u32[]{:S(2)}) copy-start(f32[8,512]{1,0:T(8,128)} %param.12) | copy-start | bytes 49156
  32.7 7.3 %copy-start.5 = (f32[8,512]{1,0:T(8,128)S(1)}, f32[8,512]{1,0:T(8,128)}, u32[]{:S(2)}) copy-start(f32[8,512]{1,0:T(8,128)} %copy.31) | copy-start | bytes 49156
  32.7 7.3 %copy-start.6 = (bf16[512,128]{1,0:T(8,128)(2,1)S(1)}, bf16[512,128]{1,0:T(8,128)(2,1)}, u32[]{:S(2)}) copy-start(bf16[512,128]{1,0:T(8,128)(2,1)} %param.9) | copy-start | bytes 393220
  34.7 1.2 %collective-permute-start.3 = (bf16[2]{0:T(256)(128)(2,1)S(1)}, bf16[2]{0:T(256)(128)(2,1)S(1)}, u32[]{:S(2)}, u32[]{:S(2)}) collective-permute-start(bf16[2]{0:T(256)(128)(2,1)S(1)} %collective-permute-done), channel_id=1, source_target_pairs={{0,8},{8,16},{16,24},{24,32},{32,40},{40,48},{48,56},{56,64},{64,7... | collective-permute-start | bytes 20 | tf_op jit(solution)/shard_map/ppermute | solution.py:15
  45.0 13.8 %collective-permute-start.4 = (bf16[512,128]{1,0:T(8,128)(2,1)}, bf16[512,128]{1,0:T(8,128)(2,1)S(1)}, u32[]{:S(2)}, u32[]{:S(2)}) collective-permute-start(bf16[512,128]{1,0:T(8,128)(2,1)} %collective-permute-done.1), channel_id=1, source_target_pairs={{0,8},{8,16},{16,24},{24,32},{32,40},{40,48},{48,56},{56,64},{64,7... | collective-permute-start | bytes 393224 | tf_op jit(solution)/shard_map/ppermute | solution.py:15
  53.0 7.1 %collective-permute-start.5 = (bf16[512,128]{1,0:T(8,128)(2,1)}, bf16[512,128]{1,0:T(8,128)(2,1)S(1)}, u32[]{:S(2)}, u32[]{:S(2)}) collective-permute-start(bf16[512,128]{1,0:T(8,128)(2,1)} %collective-permute-done.2), channel_id=1, source_target_pairs={{0,8},{8,16},{16,24},{24,32},{32,40},{40,48},{48,56},{56,64},{64,7... | collective-permute-start | bytes 393224 | tf_op jit(solution)/shard_map/ppermute | solution.py:15
  57.0 3.1 %copy-start.1 = (bf16[8,512,512]{1,2,0:T(8,128)(2,1)}, bf16[8,512,512]{1,2,0:T(8,128)(2,1)S(1)}, u32[]{:S(2)}) copy-start(bf16[8,512,512]{1,2,0:T(8,128)(2,1)S(1)} %fusion.19) | copy-start | bytes 12582916
  64.4 9.5 %copy-start.2 = (bf16[8,512,512]{1,2,0:T(8,128)(2,1)S(1)}, bf16[8,512,512]{1,2,0:T(8,128)(2,1)}, u32[]{:S(2)}) copy-start(bf16[8,512,512]{1,2,0:T(8,128)(2,1)} %copy-done.1) | copy-start | bytes 12582916
  64.4 9.5 %collective-permute-start.6 = (f32[512,1,128]{2,0,1:T(8,128)S(1)}, f32[512,1,128]{2,0,1:T(8,128)S(1)}, u32[]{:S(2)}, u32[]{:S(2)}) collective-permute-start(f32[512,1,128]{2,0,1:T(8,128)S(1)} %fusion.34), channel_id=1, source_target_pairs={{0,248},{8,0},{16,8},{24,16},{32,24},{40,32},{48,40},{56,48},{64,5... | collective-permute-start | bytes 786440 | tf_op jit(solution)/shard_map/ppermute | solution.py:15
  66.6 10.1 %collective-permute-start.8 = (f32[512,1,128]{2,0,1:T(8,128)S(1)}, f32[512,1,128]{2,0,1:T(8,128)S(1)}, u32[]{:S(2)}, u32[]{:S(2)}) collective-permute-start(f32[512,1,128]{2,0,1:T(8,128)S(1)} %fusion.36), channel_id=1, source_target_pairs={{0,248},{8,0},{16,8},{24,16},{32,24},{40,32},{48,40},{56,48},{64,5... | collective-permute-start | bytes 786440 | tf_op jit(solution)/shard_map/ppermute | solution.py:15
  75.1 14.4 %collective-permute-start.7 = (f32[512,1,128]{2,0,1:T(8,128)S(1)}, f32[512,1,128]{2,0,1:T(8,128)S(1)}, u32[]{:S(2)}, u32[]{:S(2)}) collective-permute-start(f32[512,1,128]{2,0,1:T(8,128)S(1)} %fusion.48), channel_id=1, source_target_pairs={{0,248},{8,0},{16,8},{24,16},{32,24},{40,32},{48,40},{56,48},{64,5... | collective-permute-start | bytes 786440 | tf_op jit(solution)/shard_map/ppermute | solution.py:15
  79.3 9.6 %collective-permute-start.9 = (f32[512,1,128]{2,0,1:T(8,128)}, f32[512,1,128]{2,0,1:T(8,128)S(1)}, u32[]{:S(2)}, u32[]{:S(2)}) collective-permute-start(f32[512,1,128]{2,0,1:T(8,128)} %fusion.45), channel_id=1, source_target_pairs={{0,248},{8,0},{16,8},{24,16},{32,24},{40,32},{48,40},{56,48},{64,5... | collective-permute-start | bytes 786440 | tf_op jit(solution)/shard_map/ppermute | solution.py:15
where the time goes:
time: 90.6 us; the launch traced here: 90.3 us
  matrix products  28 us (31%)
  waiting for transfers between devices  16.6 us (18%)
  starting transfers between devices  16.1 us (18%)
  between operations  9.44 us (10%)
  blocking collectives  9.24 us (10%)
  local copies, waits for them, and re-layouts  6.44 us (7%)
  other arithmetic  4.52 us (5%)
    ppermute x10, waiting for transfers between devices, passed_along(): return lax.ppermute(value, axis, pairs)  16.6 us
    ppermute x10, starting transfers between devices, passed_along(): return lax.ppermute(value, axis, pairs)  16.1 us
    dot_general x3, matrix products, attend(): jnp.einsum('ikgd,jkd->kgij', grad_four, value_block, preferred_element_ty...  9.81 us
    unnamed x1, blocking collectives  9.24 us
    dot_general x3, matrix products, attend(): jnp.einsum('kgij,ikgd->jkd', rounded, grad_four, preferred_element_type=j...  5.86 us
    dot_general x3, matrix products, attend(): jnp.einsum('ikgd,jkd->kgij', query_four, key_block, preferred_element_typ...  4.71 us
    unnamed x21, local copies, waits for them, and re-layouts  4.05 us
    dot_general x3, matrix products, attend(): jnp.einsum('kgij,jkd->ikgd', grad_scores, key_block, preferred_element_ty...  3.82 us
  transfers between devices with their start and end apart: 10, of which 4 were waited for; matrix products, arithmetic and copies ran while one was open for 34% of the time, Pallas kernels for 0%

commit v1 on v0

v1 whole, which is shorter than its diff:
```python
import functools
import math

import jax
import jax.numpy as jnp
from jax import lax
from jax.experimental import pallas as pl
from jax.experimental.pallas import tpu as pltpu
from jax.sharding import PartitionSpec as P

D = 128
H = 8
T = 512
HALF = T // 2
PIECES = 64
GROUP = 4
SCALE = 1.0 / math.sqrt(D)
LOG2E = math.log2(math.e)
SCORE_SCALE = SCALE * LOG2E
F32 = jnp.float32
BF16 = jnp.bfloat16


def dot(a, b):
    return lax.dot_general(a, b, (((1,), (0,)), ((), ())), preferred_element_type=F32)


def dot_t(a, b):
    return lax.dot_general(a, b, (((1,), (1,)), ((), ())), preferred_element_type=F32)


def cat(parts, axis):
    return parts[0] if len(parts) == 1 else jnp.concatenate(parts, axis)


def add(total, part):
    return part if total is None else total + part


def weights_of(q, g, k_t, v_t, log_total, row_dot, mask):
    p = jnp.exp2(dot(q, k_t) * SCORE_SCALE - log_total)
    if mask is not None:
        p = jnp.where(mask, p, 0.0)
    ds = p * (dot(g, v_t) - row_dot)
    return p.astype(BF16), ds.astype(BF16)


def own_kernel(off, q_ref, g_ref, o_ref, l_ref, k_ref, v_ref, dq_ref, dkv_ref, stat_ref, stat_t):
    ql = pl.multiple_of(off[0], HALF)
    qh = pl.multiple_of(HALF - off[0], HALF)
    rows = lax.broadcasted_iota(jnp.int32, (H, 2 * D), 0)
    row_dot = jnp.zeros((H, T), F32)
    for h in range(H):
        cols = slice(h * D, (h + 1) * D)
        prod = g_ref[:, cols].astype(F32) * o_ref[:, cols].astype(F32)
        top = prod.astype(BF16)
        rest = (prod - top.astype(F32)).astype(BF16)
        pick = jnp.where(rows == h, 1.0, 0.0).astype(BF16)
        row_dot += dot_t(pick, jnp.concatenate([top, rest], 1))
    stat = jnp.concatenate([l_ref[...] * LOG2E, row_dot], 0)
    stat_ref[...] = stat
    stat_t[...] = stat.T
    mask = lax.broadcasted_iota(jnp.int32, (HALF, HALF), 1) <= lax.broadcasted_iota(
        jnp.int32, (HALF, HALF), 0
    )
    kl, kh = k_ref[pl.ds(ql, HALF), :], k_ref[pl.ds(qh, HALF), :]
    vl, vh = v_ref[pl.ds(ql, HALF), :], v_ref[pl.ds(qh, HALF), :]
    kl_t, kh_t, vl_t, vh_t = kl.T, kh.T, vl.T, vh.T
    k_both = jnp.concatenate([kl, kh], 0)
    dk_l = dk_h = dv_l = dv_h = None
    for h0 in range(0, H, GROUP):
        p_l, p_h, d_l, d_h, g_l, g_h, q_l, q_h = [], [], [], [], [], [], [], []
        for h in range(h0, h0 + GROUP):
            cols = slice(h * D, (h + 1) * D)
            q0, q1 = q_ref[pl.ds(ql, HALF), cols], q_ref[pl.ds(qh, HALF), cols]
            g0, g1 = g_ref[pl.ds(ql, HALF), cols], g_ref[pl.ds(qh, HALF), cols]
            l0, l1 = stat_t[pl.ds(ql, HALF), h : h + 1], stat_t[pl.ds(qh, HALF), h : h + 1]
            r0 = stat_t[pl.ds(ql, HALF), H + h : H + h + 1]
            r1 = stat_t[pl.ds(qh, HALF), H + h : H + h + 1]
            p00, d00 = weights_of(q0, g0, kl_t, vl_t, l0, r0, mask)
            p10, d10 = weights_of(q1, g1, kl_t, vl_t, l1, r1, None)
            p11, d11 = weights_of(q1, g1, kh_t, vh_t, l1, r1, mask)
            q0_t, q1_t, g0_t, g1_t = q0.T, q1.T, g0.T, g1.T
            p_l += [p00, p10]
            d_l += [d00, d10]
            p_h += [p11]
            d_h += [d11]
            g_l += [g0_t, g1_t]
            q_l += [q0_t, q1_t]
            g_h += [g1_t]
            q_h += [q1_t]
            dq_ref[pl.ds(ql, HALF), cols] = dot(d00, kl)
            dq_ref[pl.ds(qh, HALF), cols] = dot(jnp.concatenate([d10, d11], 1), k_both)
        dv_l = add(dv_l, dot(cat(g_l, 1), cat(p_l, 0)))
        dv_h = add(dv_h, dot(cat(g_h, 1), cat(p_h, 0)))
        dk_l = add(dk_l, dot(cat(q_l, 1), cat(d_l, 0)))
        dk_h = add(dk_h, dot(cat(q_h, 1), cat(d_h, 0)))
    dkv_ref[pl.ds(ql, HALF), :] = (dk_l * SCALE).T
    dkv_ref[pl.ds(qh, HALF), :] = (dk_h * SCALE).T
    dkv_ref[pl.ds(pl.multiple_of(T + ql, HALF), HALF), :] = dv_l.T
    dkv_ref[pl.ds(pl.multiple_of(T + qh, HALF), HALF), :] = dv_h.T


def other_kernel(last, ids, q_ref, g_ref, stat_ref, k_ref, v_ref, part_ref, dq_ref, dkv_ref, stat_t):
    ql = pl.multiple_of(ids[0], HALF)
    qh = pl.multiple_of(HALF - ids[0], HALF)
    kl = pl.multiple_of(ids[1], HALF)
    kh = pl.multiple_of(HALF - ids[1], HALF)
    lows = ids[2]
    q2 = pl.multiple_of(jnp.where(lows == 1, ql, qh), HALF)
    k2 = pl.multiple_of(jnp.where(lows == 1, kl, kh), HALF)
    in_low = lows.astype(F32)
    in_high = 1.0 - in_low
    stat_t[...] = stat_ref[...].T
    ka, kb = k_ref[pl.ds(kl, HALF), :], k_ref[pl.ds(k2, HALF), :]
    va, vb = v_ref[pl.ds(kl, HALF), :], v_ref[pl.ds(k2, HALF), :]
    ka_t, kb_t, va_t, vb_t = ka.T, kb.T, va.T, vb.T
    dk_a = dk_b = dv_a = dv_b = None
    for h0 in range(0, H, GROUP):
        p_a, p_b, d_a, d_b, g_a, g_b, q_a, q_b = [], [], [], [], [], [], [], []
        for h in range(h0, h0 + GROUP):
            cols = slice(h * D, (h + 1) * D)

            def quadrant(rows, k_t, v_t, h=h, cols=cols):
                q, g = q_ref[pl.ds(rows, HALF), cols], g_ref[pl.ds(rows, HALF), cols]
                log_total = stat_t[pl.ds(rows, HALF), h : h + 1]
                row_dot = stat_t[pl.ds(rows, HALF), H + h : H + h + 1]
                p, ds = weights_of(q, g, k_t, v_t, log_total, row_dot, None)
                return p, ds, q.T, g.T

            p, da, q, g = quadrant(qh, ka_t, va_t)
            p_a, d_a, q_a, g_a = p_a + [p], d_a + [da], q_a + [q], g_a + [g]
            p, db, q, g = quadrant(q2, kb_t, vb_t)
            p_b, d_b, q_b, g_b = p_b + [p], d_b + [db], q_b + [q], g_b + [g]
            x1, x2 = dot(da, ka), dot(db, kb)
            high = part_ref[pl.ds(qh, HALF), cols] + (x1 + in_high * x2)
            low = part_ref[pl.ds(ql, HALF), cols] + in_low * x2
            if last:
                high, low = (high * SCALE).astype(BF16), (low * SCALE).astype(BF16)
            dq_ref[pl.ds(qh, HALF), cols] = high
            dq_ref[pl.ds(ql, HALF), cols] = low
        dv_a = add(dv_a, dot(cat(g_a, 1), cat(p_a, 0)))
        dv_b = add(dv_b, dot(cat(g_b, 1), cat(p_b, 0)))
        dk_a = add(dk_a, dot(cat(q_a, 1), cat(d_a, 0)))
        dk_b = add(dk_b, dot(cat(q_b, 1), cat(d_b, 0)))
    dk_a, dk_b = dk_a * SCALE, dk_b * SCALE
    dkv_ref[pl.ds(kl, HALF), :] = (dk_a + in_low * dk_b).T.astype(BF16)
    dkv_ref[pl.ds(kh, HALF), :] = (in_high * dk_b).T.astype(BF16)
    dkv_ref[pl.ds(pl.multiple_of(T + kl, HALF), HALF), :] = (dv_a + in_low * dv_b).T.astype(BF16)
    dkv_ref[pl.ds(pl.multiple_of(T + kh, HALF), HALF), :] = (in_high * dv_b).T.astype(BF16)


def vmem():
    return pl.BlockSpec(memory_space=pltpu.VMEM)


def smem():
    return pl.BlockSpec(memory_space=pltpu.SMEM)


def cost(quadrants, size):
    return pl.CostEstimate(
        flops=quadrants * H * 20 * HALF * HALF * D,
        bytes_accessed=size,
        transcendentals=quadrants * H * HALF * HALF,
    )


def own_block(off, q, g, o, l, k, v):
    return pl.pallas_call(
        own_kernel,
        in_specs=[smem()] + [vmem()] * 6,
        out_specs=[vmem()] * 3,
        out_shape=[
            jax.ShapeDtypeStruct((T, H * D), F32),
            jax.ShapeDtypeStruct((2 * T, D), F32),
            jax.ShapeDtypeStruct((2 * H, T), F32),
        ],
        scratch_shapes=[pltpu.VMEM((T, 2 * H), F32)],
        compiler_params=pltpu.CompilerParams(vmem_limit_bytes=24 << 20),
        cost_estimate=cost(3, 6 << 20),
        name="own_block",
    )(off, q, g, o, l, k, v)


def other_block(last, ids, q, g, stat, k, v, part):
    return pl.pallas_call(
        functools.partial(other_kernel, last),
        in_specs=[smem()] + [vmem()] * 6,
        out_specs=[vmem()] * 2,
        out_shape=[
            jax.ShapeDtypeStruct((T, H * D), BF16 if last else F32),
            jax.ShapeDtypeStruct((2 * T, D), BF16),
        ],
        scratch_shapes=[pltpu.VMEM((T, 2 * H), F32)],
        compiler_params=pltpu.CompilerParams(vmem_limit_bytes=24 << 20),
        cost_estimate=cost(2, 6 << 20),
        name="other_block",
    )(ids, q, g, stat, k, v, part)


def passed_along(value, steps):
    count = lax.axis_size("blk")
    pairs = [(source, (source + steps) % count) for source in range(count)]
    return lax.ppermute(value, "blk", pairs)


def swapped(value):
    count = lax.axis_size("blk")
    return lax.ppermute(value, "blk", [(source, source ^ 1) for source in range(count)])


def first_piece(positions):
    piece = positions[0] // HALF
    in_first = lax.axis_index("tp") < lax.axis_size("tp") // 2
    return jnp.where(in_first, piece, PIECES - 1 - piece)


def low_row(first):
    return jnp.where(first < PIECES // 2, 0, HALF).astype(jnp.int32)


def low_piece(first):
    return jnp.minimum(first, PIECES - 1 - first)


def on_device(q, k, v, o, g, log_total, positions):
    k_two, v_two, pos_two = passed_along(k, 2), passed_along(v, 2), passed_along(positions, 2)
    first = first_piece(positions)
    off = low_row(first)
    dq, dkv, stat = own_block(off.reshape(1), q, g, o, log_total, k, v)
    even = lax.axis_index("blk") % 2 == 0
    k_one, v_one, pos_one = (
        swapped(jnp.where(even, a, b))
        for a, b in ((k, k_two), (v, v_two), (positions, pos_two))
    )

    def ids(pos):
        theirs = first_piece(pos)
        lows = (low_piece(first) > low_piece(theirs)).astype(jnp.int32)
        return jnp.stack([off, low_row(theirs), lows])

    dq, dkv_two = other_block(False, ids(pos_two), q, g, stat, k_two, v_two, dq)
    back_two = passed_along(dkv_two, -2)
    dq, dkv_one = other_block(True, ids(pos_one), q, g, stat, k_one, v_one, dq)
    back_one = passed_along(dkv_one, -1)
    total = (dkv + back_two.astype(F32) + back_one.astype(F32)).astype(BF16)
    return dq, total[:T], total[T:]


def solution(mesh):
    in_specs = (
        P("blk", "tp"),
        P("blk", "tp"),
        P("blk", "tp"),
        P("blk", "tp"),
        P("blk", "tp"),
        P("tp", "blk"),
        P(("blk", "tp")),
    )
    out_specs = (P("blk", "tp"), P("blk", "tp"), P("blk", "tp"))
    return jax.shard_map(
        on_device, mesh=mesh, in_specs=in_specs, out_specs=out_specs, check_vma=False
    )
```

time: 90.6 us -> 48.2 us (0.53)
  the two profiles are of different devices: /device:TPU:101 before, /device:TPU:1 now
where the time goes in v1:
time: 48.2 us; the launch traced here: 47.5 us
  starting transfers between devices  13.4 us (28%)
  Pallas kernels  12.7 us (26%)
  local copies, waits for them, and re-layouts  9.85 us (20%)
  waiting for transfers between devices  7.47 us (15%)
  between operations  3.69 us (8%)
    ppermute x5, starting transfers between devices, passed_along(): return lax.ppermute(value, 'blk', pairs)  11.2 us
    unnamed x26, local copies, waits for them, and re-layouts  9.14 us
    pallas_call x2, Pallas kernels, other_block(): pl.pallas_call(functools.partial(other_kernel, last), in_specs=[smem()] +...  8.13 us
    ppermute x5, waiting for transfers between devices, passed_along(): return lax.ppermute(value, 'blk', pairs)  6.72 us
    pallas_call x1, Pallas kernels, own_block(): pl.pallas_call(own_kernel, in_specs=[smem()] + [vmem()] * 6, out_specs=[v...  4.61 us
    ppermute x3, starting transfers between devices, swapped(): lax.ppermute(value, 'blk', [(source, source ^ 1) for source in range(coun...  2.28 us
  transfers between devices with their start and end apart: 8, of which 3 were waited for; matrix products, arithmetic and copies ran while one was open for 0% of the time, Pallas kernels for 27%

profile of v1, /device:TPU:1, one launch (start us, length us, event | category | flops | bytes accessed | tf_op | source)
XLA Modules:
  0.0 47.5 jit_solution(14902287327797254008)
XLA Ops:
  0.6 3.6 %collective-permute-start = (s32[64]{0:T(128)}, s32[64]{0:T(128)S(1)}, u32[]{:S(2)}, u32[]{:S(2)}) collective-permute-start(s32[64]{0:T(128)} %param.13), channel_id=1, source_target_pairs={{0,16},{8,24},{16,32},{24,40},{32,48},{40,56},{48,64},{56,72},{64,... | collective-permute-start | bytes 776 | tf_op jit(solution)/shard_map/ppermute | solution.py:205
  4.3 1.6 %collective-permute-start.2 = (bf16[512,128]{1,0:T(8,128)(2,1)}, bf16[512,128]{1,0:T(8,128)(2,1)S(1)}, u32[]{:S(2)}, u32[]{:S(2)}) collective-permute-start(bf16[512,128]{1,0:T(8,128)(2,1)} %k_ref.1), channel_id=1, source_target_pairs={{0,16},{8,24},{16,32},{24,40},{32,48},{40,56},{48,64},{56,72},{64,... | collective-permute-start | bytes 393224 | tf_op jit(solution)/shard_map/ppermute | solution.py:205
  5.9 2.7 %collective-permute-start.4 = (bf16[512,128]{1,0:T(8,128)(2,1)}, bf16[512,128]{1,0:T(8,128)(2,1)S(1)}, u32[]{:S(2)}, u32[]{:S(2)}) collective-permute-start(bf16[512,128]{1,0:T(8,128)(2,1)} %v_ref.1), channel_id=1, source_target_pairs={{0,16},{8,24},{16,32},{24,40},{32,48},{40,56},{48,64},{56,72},{64,... | collective-permute-start | bytes 393224 | tf_op jit(solution)/shard_map/ppermute | solution.py:205
  11.2 0.0 copy-start
  11.2 0.9 %copy-done = bf16[512,128]{1,0:T(8,128)(2,1)S(1)} copy-done((bf16[512,128]{1,0:T(8,128)(2,1)S(1)}, bf16[512,128]{1,0:T(8,128)(2,1)}, u32[]{:S(2)}) %copy-start) | copy-done | bytes 131096
  12.1 0.0 copy-start.2
  12.1 0.9 %copy-done.2 = bf16[512,128]{1,0:T(8,128)(2,1)S(1)} copy-done((bf16[512,128]{1,0:T(8,128)(2,1)S(1)}, bf16[512,128]{1,0:T(8,128)(2,1)}, u32[]{:S(2)}) %copy-start.2) | copy-done | bytes 131096
  13.0 0.0 copy-start.4
  13.0 1.2 %copy-done.4 = bf16[512,1024]{1,0:T(8,128)(2,1)S(1)} copy-done((bf16[512,1024]{1,0:T(8,128)(2,1)S(1)}, bf16[512,1024]{1,0:T(8,128)(2,1)}, u32[]{:S(2)}) %copy-start.4) | copy-done | bytes 1048600
  14.3 0.0 copy-start.5
  14.3 1.2 %copy-done.5 = bf16[512,1024]{1,0:T(8,128)(2,1)S(1)} copy-done((bf16[512,1024]{1,0:T(8,128)(2,1)S(1)}, bf16[512,1024]{1,0:T(8,128)(2,1)}, u32[]{:S(2)}) %copy-start.5) | copy-done | bytes 1048600
  15.5 0.0 copy-start.7
  15.5 1.2 %copy-done.7 = bf16[512,1024]{1,0:T(8,128)(2,1)S(1)} copy-done((bf16[512,1024]{1,0:T(8,128)(2,1)S(1)}, bf16[512,1024]{1,0:T(8,128)(2,1)}, u32[]{:S(2)}) %copy-start.7) | copy-done | bytes 1048600
  16.7 0.0 copy-start.9
  16.7 0.7 %copy-done.9 = f32[8,512]{1,0:T(8,128)S(1)} copy-done((f32[8,512]{1,0:T(8,128)S(1)}, f32[8,512]{1,0:T(8,128)}, u32[]{:S(2)}) %copy-start.9) | copy-done | bytes 16408
  17.4 0.0 copy-start.12
  17.4 0.0 copy-start.1
  17.4 0.0 copy-start.3
  17.4 0.0 copy-start.6
  17.4 0.0 copy-start.8
  17.5 4.6 %own_block.1 = (f32[512,1024]{1,0:T(8,128)S(1)}, f32[1024,128]{1,0:T(8,128)S(1)}, f32[16,512]{1,0:T(8,128)S(1)}) custom-call(s32[1]{0:T(128)} %bitcast.1.off, bf16[512,1024]{1,0:T(8,128)(2,1)S(1)} %copy-done.5, bf16[512,1024]{1,0:T(8,128)(2,1)S(1)} %copy-done.7, bf16[512,1024]{1,0:T(8,128)(2,1)S(1)} %copy-done.4, f32[8,512]{1,0:T(8,128)S(1)} %copy-done.9, ...), custom_call_target="tpu_custom_call" | custom-call | flops 4026531840 | bytes 6291456 | tf_op jit(solution)/shard_map/own_block/pallas_call | solution.py:170
  22.1 0.0 copy-start.10
  22.1 1.3 %copy-done.10 = f32[512,1024]{1,0:T(8,128)} copy-done((f32[512,1024]{1,0:T(8,128)}, f32[512,1024]{1,0:T(8,128)S(1)}, u32[]{:S(2)}) %copy-start.10) | copy-done | bytes 2097176
  23.4 0.0 collective-permute-done
  23.6 0.0 copy-done.12
  23.6 1.6 %collective-permute-start.1 = (s32[64]{0:T(128)S(1)}, s32[64]{0:T(128)S(1)}, u32[]{:S(2)}, u32[]{:S(2)}) collective-permute-start(s32[64]{0:T(128)S(1)} %broadcast_select_fusion.2), channel_id=1, source_target_pairs={{0,8},{8,0},{16,24},{24,16},{32,40},{40,32},{48,56},{56,48},{64,72... | collective-permute-start | bytes 776 | tf_op jit(solution)/shard_map/ppermute | solution.py:210
  25.2 0.1 pad_add_fusion.1.ids
  25.3 0.7 %collective-permute-done.1 = s32[64]{0:T(128)S(1)} collective-permute-done((s32[64]{0:T(128)S(1)}, s32[64]{0:T(128)S(1)}, u32[]{:S(2)}, u32[]{:S(2)}) %collective-permute-start.1) | collective-permute-done | bytes 288 | tf_op jit(solution)/shard_map/ppermute | solution.py:210
  26.2 0.1 pad_add_fusion.ids
  26.3 0.0 collective-permute-done.2.k_ref
  26.3 0.0 copy-done.1
  26.3 0.4 collective-permute-start.3
  26.7 0.0 collective-permute-done.4.v_ref
  26.7 0.0 copy-done.3
  26.7 0.3 collective-permute-start.5
  27.0 0.0 copy-done.6
  27.0 0.0 copy-done.8
  27.0 1.6 %copy-done.11 = f32[512,1024]{1,0:T(8,128)S(1)} copy-done((f32[512,1024]{1,0:T(8,128)S(1)}, f32[512,1024]{1,0:T(8,128)}, u32[]{:S(2)}) %copy-start.11) | copy-done | bytes 2097176
  28.6 3.9 %other_block.2 = (f32[512,1024]{1,0:T(8,128)S(1)}, bf16[1024,128]{1,0:T(8,128)(2,1)S(1)}) custom-call(s32[3]{0:T(128)S(1)} %pad_add_fusion.1.ids, bf16[512,1024]{1,0:T(8,128)(2,1)S(1)} %copy-done.6, bf16[512,1024]{1,0:T(8,128)(2,1)S(1)} %copy-done.8, f32[16,512]{1,0:T(8,128)S(1)} %get-tuple-element.10.stat_ref, ...), custom_call_target="tpu_custom_call" | custom-call | flops 2684354560 | bytes 6291456 | tf_op jit(solution)/shard_map/other_block/pallas_call | solution.py:187
  32.5 2.6 %collective-permute-start.6 = (bf16[1024,128]{1,0:T(8,128)(2,1)S(1)}, bf16[1024,128]{1,0:T(8,128)(2,1)S(1)}, u32[]{:S(2)}, u32[]{:S(2)}) collective-permute-start(bf16[1024,128]{1,0:T(8,128)(2,1)S(1)} %get-tuple-element.15), channel_id=1, source_target_pairs={{0,240},{8,248},{16,0},{24,8},{32,16},{40,24},{48,32},{56,40},{64,... | collective-permute-start | bytes 786440 | tf_op jit(solution)/shard_map/ppermute | solution.py:205
  35.1 0.0 collective-permute-done.3.k_ref
  35.1 0.0 collective-permute-done.5.v_ref
  35.1 4.2 %other_block.3 = (bf16[512,1024]{1,0:T(8,128)(2,1)}, bf16[1024,128]{1,0:T(8,128)(2,1)S(1)}) custom-call(s32[3]{0:T(128)S(1)} %pad_add_fusion.ids, bf16[512,1024]{1,0:T(8,128)(2,1)S(1)} %copy-done.6, bf16[512,1024]{1,0:T(8,128)(2,1)S(1)} %copy-done.8, f32[16,512]{1,0:T(8,128)S(1)} %get-tuple-element.10.stat_ref, ...), custom_call_target="tpu_custom_call" | custom-call | flops 2684354560 | bytes 6291456 | tf_op jit(solution)/shard_map/other_block/pallas_call | solution.py:187
  39.3 0.6 %collective-permute-start.7 = (bf16[1024,128]{1,0:T(8,128)(2,1)S(1)}, bf16[1024,128]{1,0:T(8,128)(2,1)S(1)}, u32[]{:S(2)}, u32[]{:S(2)}) collective-permute-start(bf16[1024,128]{1,0:T(8,128)(2,1)S(1)} %get-tuple-element.16), channel_id=1, source_target_pairs={{0,248},{8,0},{16,8},{24,16},{32,24},{40,32},{48,40},{56,48},{64,5... | collective-permute-start | bytes 786440 | tf_op jit(solution)/shard_map/ppermute | solution.py:205
  39.9 1.9 %collective-permute-done.6 = bf16[1024,128]{1,0:T(8,128)(2,1)S(1)} collective-permute-done((bf16[1024,128]{1,0:T(8,128)(2,1)S(1)}, bf16[1024,128]{1,0:T(8,128)(2,1)S(1)}, u32[]{:S(2)}, u32[]{:S(2)}) %collective-permute-start.6) | collective-permute-done | bytes 262176 | tf_op jit(solution)/shard_map/ppermute | solution.py:205
  41.9 4.8 %collective-permute-done.7 = bf16[1024,128]{1,0:T(8,128)(2,1)S(1)} collective-permute-done((bf16[1024,128]{1,0:T(8,128)(2,1)S(1)}, bf16[1024,128]{1,0:T(8,128)(2,1)S(1)}, u32[]{:S(2)}, u32[]{:S(2)}) %collective-permute-start.7) | collective-permute-done | bytes 262176 | tf_op jit(solution)/shard_map/ppermute | solution.py:205
  46.7 0.1 add_convert_fusion
  46.8 0.7 %fusion = (bf16[512,128]{1,0:T(8,128)(2,1)}, bf16[512,128]{1,0:T(8,128)(2,1)}) fusion(bf16[1024,128]{1,0:T(8,128)(2,1)S(1)} %add_convert_fusion), kind=kLoop, calls=%fused_computation.6 | loop fusion | bytes 524288 | tf_op jit(solution)/shard_map/slice | solution.py:248
  (4 shorter events, 0.0 us)
Async XLA Ops:
  0.6 22.8 %collective-permute-start = (s32[64]{0:T(128)}, s32[64]{0:T(128)S(1)}, u32[]{:S(2)}, u32[]{:S(2)}) collective-permute-start(s32[64]{0:T(128)} %param.13), channel_id=1, source_target_pairs={{0,16},{8,24},{16,32},{24,40},{32,48},{40,56},{48,64},{56,72},{64,... | collective-permute-start | bytes 776 | tf_op jit(solution)/shard_map/ppermute | solution.py:205
  4.3 22.0 %collective-permute-start.2 = (bf16[512,128]{1,0:T(8,128)(2,1)}, bf16[512,128]{1,0:T(8,128)(2,1)S(1)}, u32[]{:S(2)}, u32[]{:S(2)}) collective-permute-start(bf16[512,128]{1,0:T(8,128)(2,1)} %k_ref.1), channel_id=1, source_target_pairs={{0,16},{8,24},{16,32},{24,40},{32,48},{40,56},{48,64},{56,72},{64,... | collective-permute-start | bytes 393224 | tf_op jit(solution)/shard_map/ppermute | solution.py:205
  5.9 20.8 %collective-permute-start.4 = (bf16[512,128]{1,0:T(8,128)(2,1)}, bf16[512,128]{1,0:T(8,128)(2,1)S(1)}, u32[]{:S(2)}, u32[]{:S(2)}) collective-permute-start(bf16[512,128]{1,0:T(8,128)(2,1)} %v_ref.1), channel_id=1, source_target_pairs={{0,16},{8,24},{16,32},{24,40},{32,48},{40,56},{48,64},{56,72},{64,... | collective-permute-start | bytes 393224 | tf_op jit(solution)/shard_map/ppermute | solution.py:205
  11.2 0.9 %copy-start = (bf16[512,128]{1,0:T(8,128)(2,1)S(1)}, bf16[512,128]{1,0:T(8,128)(2,1)}, u32[]{:S(2)}) copy-start(bf16[512,128]{1,0:T(8,128)(2,1)} %k_ref.1) | copy-start | bytes 393220
  12.1 0.9 %copy-start.2 = (bf16[512,128]{1,0:T(8,128)(2,1)S(1)}, bf16[512,128]{1,0:T(8,128)(2,1)}, u32[]{:S(2)}) copy-start(bf16[512,128]{1,0:T(8,128)(2,1)} %v_ref.1) | copy-start | bytes 393220
  13.0 1.2 %copy-start.4 = (bf16[512,1024]{1,0:T(8,128)(2,1)S(1)}, bf16[512,1024]{1,0:T(8,128)(2,1)}, u32[]{:S(2)}) copy-start(bf16[512,1024]{1,0:T(8,128)(2,1)} %o_ref.1) | copy-start | bytes 3145732
  14.3 1.2 %copy-start.5 = (bf16[512,1024]{1,0:T(8,128)(2,1)S(1)}, bf16[512,1024]{1,0:T(8,128)(2,1)}, u32[]{:S(2)}) copy-start(bf16[512,1024]{1,0:T(8,128)(2,1)} %q_ref.5) | copy-start | bytes 3145732
  15.5 1.2 %copy-start.7 = (bf16[512,1024]{1,0:T(8,128)(2,1)S(1)}, bf16[512,1024]{1,0:T(8,128)(2,1)}, u32[]{:S(2)}) copy-start(bf16[512,1024]{1,0:T(8,128)(2,1)} %g_ref.5) | copy-start | bytes 3145732
  16.7 0.7 %copy-start.9 = (f32[8,512]{1,0:T(8,128)S(1)}, f32[8,512]{1,0:T(8,128)}, u32[]{:S(2)}) copy-start(f32[8,512]{1,0:T(8,128)} %l_ref.1) | copy-start | bytes 49156
  17.4 6.2 %copy-start.12 = (s32[64]{0:T(128)S(1)}, s32[64]{0:T(128)}, u32[]{:S(2)}) copy-start(s32[64]{0:T(128)} %param.13) | copy-start | bytes 772
  17.4 8.9 %copy-start.1 = (bf16[512,128]{1,0:T(8,128)(2,1)S(1)}, bf16[512,128]{1,0:T(8,128)(2,1)}, u32[]{:S(2)}) copy-start(bf16[512,128]{1,0:T(8,128)(2,1)} %k_ref.1) | copy-start | bytes 393220
  17.4 9.3 %copy-start.3 = (bf16[512,128]{1,0:T(8,128)(2,1)S(1)}, bf16[512,128]{1,0:T(8,128)(2,1)}, u32[]{:S(2)}) copy-start(bf16[512,128]{1,0:T(8,128)(2,1)} %v_ref.1) | copy-start | bytes 393220
  17.4 9.6 %copy-start.6 = (bf16[512,1024]{1,0:T(8,128)(2,1)S(1)}, bf16[512,1024]{1,0:T(8,128)(2,1)}, u32[]{:S(2)}) copy-start(bf16[512,1024]{1,0:T(8,128)(2,1)} %q_ref.5) | copy-start | bytes 3145732
  17.4 9.6 %copy-start.8 = (bf16[512,1024]{1,0:T(8,128)(2,1)S(1)}, bf16[512,1024]{1,0:T(8,128)(2,1)}, u32[]{:S(2)}) copy-start(bf16[512,1024]{1,0:T(8,128)(2,1)} %g_ref.5) | copy-start | bytes 3145732
  22.1 1.3 %copy-start.10 = (f32[512,1024]{1,0:T(8,128)}, f32[512,1024]{1,0:T(8,128)S(1)}, u32[]{:S(2)}) copy-start(f32[512,1024]{1,0:T(8,128)S(1)} %get-tuple-element.11.part_ref) | copy-start | bytes 6291460
  23.6 2.4 %collective-permute-start.1 = (s32[64]{0:T(128)S(1)}, s32[64]{0:T(128)S(1)}, u32[]{:S(2)}, u32[]{:S(2)}) collective-permute-start(s32[64]{0:T(128)S(1)} %broadcast_select_fusion.2), channel_id=1, source_target_pairs={{0,8},{8,0},{16,24},{24,16},{32,40},{40,32},{48,56},{56,48},{64,72... | collective-permute-start | bytes 776 | tf_op jit(solution)/shard_map/ppermute | solution.py:210
  26.3 8.8 %collective-permute-start.3 = (bf16[512,128]{1,0:T(8,128)(2,1)S(1)}, bf16[512,128]{1,0:T(8,128)(2,1)S(1)}, u32[]{:S(2)}, u32[]{:S(2)}) collective-permute-start(bf16[512,128]{1,0:T(8,128)(2,1)S(1)} %broadcast_select_fusion.1), channel_id=1, source_target_pairs={{0,8},{8,0},{16,24},{24,16},{32,40},{40,32},{48,56},{56,48},{64,72... | collective-permute-start | bytes 393224 | tf_op jit(solution)/shard_map/ppermute | solution.py:210
  26.7 8.4 %collective-permute-start.5 = (bf16[512,128]{1,0:T(8,128)(2,1)S(1)}, bf16[512,128]{1,0:T(8,128)(2,1)S(1)}, u32[]{:S(2)}, u32[]{:S(2)}) collective-permute-start(bf16[512,128]{1,0:T(8,128)(2,1)S(1)} %broadcast_select_fusion), channel_id=1, source_target_pairs={{0,8},{8,0},{16,24},{24,16},{32,40},{40,32},{48,56},{56,48},{64,72... | collective-permute-start | bytes 393224 | tf_op jit(solution)/shard_map/ppermute | solution.py:210
  27.0 1.6 %copy-start.11 = (f32[512,1024]{1,0:T(8,128)S(1)}, f32[512,1024]{1,0:T(8,128)}, u32[]{:S(2)}) copy-start(f32[512,1024]{1,0:T(8,128)} %copy-done.10) | copy-start | bytes 6291460
  32.5 9.4 %collective-permute-start.6 = (bf16[1024,128]{1,0:T(8,128)(2,1)S(1)}, bf16[1024,128]{1,0:T(8,128)(2,1)S(1)}, u32[]{:S(2)}, u32[]{:S(2)}) collective-permute-start(bf16[1024,128]{1,0:T(8,128)(2,1)S(1)} %get-tuple-element.15), channel_id=1, source_target_pairs={{0,240},{8,248},{16,0},{24,8},{32,16},{40,24},{48,32},{56,40},{64,... | collective-permute-start | bytes 786440 | tf_op jit(solution)/shard_map/ppermute | solution.py:205
  39.3 7.3 %collective-permute-start.7 = (bf16[1024,128]{1,0:T(8,128)(2,1)S(1)}, bf16[1024,128]{1,0:T(8,128)(2,1)S(1)}, u32[]{:S(2)}, u32[]{:S(2)}) collective-permute-start(bf16[1024,128]{1,0:T(8,128)(2,1)S(1)} %get-tuple-element.16), channel_id=1, source_target_pairs={{0,248},{8,0},{16,8},{24,16},{32,24},{40,32},{48,40},{56,48},{64,5... | collective-permute-start | bytes 786440 | tf_op jit(solution)/shard_map/ppermute | solution.py:205

commit v2 on v1

--- a/solution.py
+++ b/solution.py
@@ -13,6 +13,7 @@
 T = 512
 HALF = T // 2
 PIECES = 64
+IDS = 16
 GROUP = 4
 SCALE = 1.0 / math.sqrt(D)
 LOG2E = math.log2(math.e)
@@ -45,21 +46,56 @@
     return p.astype(BF16), ds.astype(BF16)
 
 
-def own_kernel(off, q_ref, g_ref, o_ref, l_ref, k_ref, v_ref, dq_ref, dkv_ref, stat_ref, stat_t):
-    ql = pl.multiple_of(off[0], HALF)
-    qh = pl.multiple_of(HALF - off[0], HALF)
+def piece_of(message):
+    return jnp.max(message[2 * T :, :].astype(F32)).astype(jnp.int32)
+
+
+def low_row(first):
+    return pl.multiple_of(jnp.where(first < PIECES // 2, 0, HALF), HALF)
+
+
+def low_piece(first):
+    return jnp.minimum(first, PIECES - 1 - first)
+
+
+def pack_kernel(k_hbm, v_hbm, pos_hbm, message, pos, sems):
+    copies = [
+        pltpu.make_async_copy(pos_hbm, pos, sems.at[0]),
+        pltpu.make_async_copy(k_hbm, message.at[pl.ds(0, T), :], sems.at[1]),
+        pltpu.make_async_copy(v_hbm, message.at[pl.ds(T, T), :], sems.at[2]),
+    ]
+    for copy in copies:
+        copy.start()
+    copies[0].wait()
+    piece = pos[0] // HALF
+    in_first = lax.axis_index("tp") < lax.axis_size("tp") // 2
+    first = jnp.where(in_first, piece, PIECES - 1 - piece)
+    message[2 * T :, :] = jnp.full((IDS, D), first.astype(F32), F32).astype(BF16)
+    copies[1].wait()
+    copies[2].wait()
+
+
+def own_kernel(q_hbm, g_hbm, o_hbm, l_hbm, message, dq_ref, dkv_ref, stat_ref, q_ref, g_ref, o_ref, l_ref, stat_t, sems):
+    loads = []
+    for n, h0 in enumerate(range(0, H, GROUP)):
+        cols = pl.ds(h0 * D, GROUP * D)
+        loads.append(
+            [
+                pltpu.make_async_copy(source.at[:, cols], target.at[:, cols], sems.at[n, i])
+                for i, (source, target) in enumerate(
+                    ((g_hbm, g_ref), (o_hbm, o_ref), (q_hbm, q_ref))
+                )
+            ]
+        )
+    load_l = pltpu.make_async_copy(l_hbm, l_ref, sems.at[0, 3])
+    load_l.start()
+    for load in loads:
+        for copy in load:
+            copy.start()
+    k_ref, v_ref = message.at[pl.ds(0, T), :], message.at[pl.ds(T, T), :]
+    ql = low_row(piece_of(message))
+    qh = pl.multiple_of(HALF - ql, HALF)
     rows = lax.broadcasted_iota(jnp.int32, (H, 2 * D), 0)
-    row_dot = jnp.zeros((H, T), F32)
-    for h in range(H):
-        cols = slice(h * D, (h + 1) * D)
-        prod = g_ref[:, cols].astype(F32) * o_ref[:, cols].astype(F32)
-        top = prod.astype(BF16)
-        rest = (prod - top.astype(F32)).astype(BF16)
-        pick = jnp.where(rows == h, 1.0, 0.0).astype(BF16)
-        row_dot += dot_t(pick, jnp.concatenate([top, rest], 1))
-    stat = jnp.concatenate([l_ref[...] * LOG2E, row_dot], 0)
-    stat_ref[...] = stat
-    stat_t[...] = stat.T
     mask = lax.broadcasted_iota(jnp.int32, (HALF, HALF), 1) <= lax.broadcasted_iota(
         jnp.int32, (HALF, HALF), 0
     )
@@ -68,15 +104,29 @@
     kl_t, kh_t, vl_t, vh_t = kl.T, kh.T, vl.T, vh.T
     k_both = jnp.concatenate([kl, kh], 0)
     dk_l = dk_h = dv_l = dv_h = None
-    for h0 in range(0, H, GROUP):
+    load_l.wait()
+    for n, h0 in enumerate(range(0, H, GROUP)):
+        for copy in loads[n]:
+            copy.wait()
+        row_dot = jnp.zeros((2 * GROUP, T), F32)
+        for h in range(h0, h0 + GROUP):
+            cols = slice(h * D, (h + 1) * D)
+            prod = g_ref[:, cols].astype(F32) * o_ref[:, cols].astype(F32)
+            top = prod.astype(BF16)
+            rest = (prod - top.astype(F32)).astype(BF16)
+            pick = jnp.where(rows == GROUP + h - h0, 1.0, 0.0).astype(BF16)
+            row_dot += dot_t(pick, jnp.concatenate([top, rest], 1))
+        stat = jnp.concatenate([l_ref[h0 : h0 + GROUP, :] * LOG2E, row_dot[GROUP:, :]], 0)
+        stat_ref[2 * h0 : 2 * (h0 + GROUP), :] = stat
+        stat_t[:, 2 * h0 : 2 * (h0 + GROUP)] = stat.T
         p_l, p_h, d_l, d_h, g_l, g_h, q_l, q_h = [], [], [], [], [], [], [], []
         for h in range(h0, h0 + GROUP):
             cols = slice(h * D, (h + 1) * D)
             q0, q1 = q_ref[pl.ds(ql, HALF), cols], q_ref[pl.ds(qh, HALF), cols]
             g0, g1 = g_ref[pl.ds(ql, HALF), cols], g_ref[pl.ds(qh, HALF), cols]
-            l0, l1 = stat_t[pl.ds(ql, HALF), h : h + 1], stat_t[pl.ds(qh, HALF), h : h + 1]
-            r0 = stat_t[pl.ds(ql, HALF), H + h : H + h + 1]
-            r1 = stat_t[pl.ds(qh, HALF), H + h : H + h + 1]
+            at, to = h0 + h, h0 + h + GROUP
+            l0, l1 = stat_t[pl.ds(ql, HALF), at : at + 1], stat_t[pl.ds(qh, HALF), at : at + 1]
+            r0, r1 = stat_t[pl.ds(ql, HALF), to : to + 1], stat_t[pl.ds(qh, HALF), to : to + 1]
             p00, d00 = weights_of(q0, g0, kl_t, vl_t, l0, r0, mask)
             p10, d10 = weights_of(q1, g1, kl_t, vl_t, l1, r1, None)
             p11, d11 = weights_of(q1, g1, kh_t, vh_t, l1, r1, mask)
@@ -101,12 +151,12 @@
     dkv_ref[pl.ds(pl.multiple_of(T + qh, HALF), HALF), :] = dv_h.T
 
 
-def other_kernel(last, ids, q_ref, g_ref, stat_ref, k_ref, v_ref, part_ref, dq_ref, dkv_ref, stat_t):
-    ql = pl.multiple_of(ids[0], HALF)
-    qh = pl.multiple_of(HALF - ids[0], HALF)
-    kl = pl.multiple_of(ids[1], HALF)
-    kh = pl.multiple_of(HALF - ids[1], HALF)
-    lows = ids[2]
+def other_kernel(last, q_ref, g_ref, stat_ref, message, theirs, part_ref, dq_ref, dkv_ref, stat_t):
+    own_first, their_first = piece_of(message), piece_of(theirs)
+    k_ref, v_ref = theirs.at[pl.ds(0, T), :], theirs.at[pl.ds(T, T), :]
+    ql, kl = low_row(own_first), low_row(their_first)
+    qh, kh = pl.multiple_of(HALF - ql, HALF), pl.multiple_of(HALF - kl, HALF)
+    lows = (low_piece(own_first) > low_piece(their_first)).astype(jnp.int32)
     q2 = pl.multiple_of(jnp.where(lows == 1, ql, qh), HALF)
     k2 = pl.multiple_of(jnp.where(lows == 1, kl, kh), HALF)
     in_low = lows.astype(F32)
@@ -123,8 +173,9 @@
 
             def quadrant(rows, k_t, v_t, h=h, cols=cols):
                 q, g = q_ref[pl.ds(rows, HALF), cols], g_ref[pl.ds(rows, HALF), cols]
-                log_total = stat_t[pl.ds(rows, HALF), h : h + 1]
-                row_dot = stat_t[pl.ds(rows, HALF), H + h : H + h + 1]
+                at, to = h0 + h, h0 + h + GROUP
+                log_total = stat_t[pl.ds(rows, HALF), at : at + 1]
+                row_dot = stat_t[pl.ds(rows, HALF), to : to + 1]
                 p, ds = weights_of(q, g, k_t, v_t, log_total, row_dot, None)
                 return p, ds, q.T, g.T
 
@@ -154,10 +205,6 @@
     return pl.BlockSpec(memory_space=pltpu.VMEM)
 
 
-def smem():
-    return pl.BlockSpec(memory_space=pltpu.SMEM)
-
-
 def cost(quadrants, size):
     return pl.CostEstimate(
         flops=quadrants * H * 20 * HALF * HALF * D,
@@ -166,27 +213,49 @@
     )
 
 
-def own_block(off, q, g, o, l, k, v):
+def hbm():
+    return pl.BlockSpec(memory_space=pltpu.HBM)
+
+
+def pack(k, v, positions):
+    return pl.pallas_call(
+        pack_kernel,
+        in_specs=[hbm()] * 3,
+        out_specs=vmem(),
+        out_shape=jax.ShapeDtypeStruct((2 * T + IDS, D), BF16),
+        scratch_shapes=[pltpu.SMEM(positions.shape, jnp.int32), pltpu.SemaphoreType.DMA((3,))],
+        name="pack",
+    )(k, v, positions)
+
+
+def own_block(q, g, o, l, message):
     return pl.pallas_call(
         own_kernel,
-        in_specs=[smem()] + [vmem()] * 6,
-        out_specs=[vmem()] * 3,
+        in_specs=[hbm()] * 4 + [vmem()],
+        out_specs=[vmem()] * 5,
         out_shape=[
             jax.ShapeDtypeStruct((T, H * D), F32),
             jax.ShapeDtypeStruct((2 * T, D), F32),
             jax.ShapeDtypeStruct((2 * H, T), F32),
+            jax.ShapeDtypeStruct((T, H * D), BF16),
+            jax.ShapeDtypeStruct((T, H * D), BF16),
         ],
-        scratch_shapes=[pltpu.VMEM((T, 2 * H), F32)],
+        scratch_shapes=[
+            pltpu.VMEM((T, H * D), BF16),
+            pltpu.VMEM((H, T), F32),
+            pltpu.VMEM((T, 2 * H), F32),
+            pltpu.SemaphoreType.DMA((H // GROUP, 4)),
+        ],
         compiler_params=pltpu.CompilerParams(vmem_limit_bytes=24 << 20),
         cost_estimate=cost(3, 6 << 20),
         name="own_block",
-    )(off, q, g, o, l, k, v)
-
-
-def other_block(last, ids, q, g, stat, k, v, part):
+    )(q, g, o, l, message)
+
+
+def other_block(last, q, g, stat, message, theirs, part):
     return pl.pallas_call(
         functools.partial(other_kernel, last),
-        in_specs=[smem()] + [vmem()] * 6,
+        in_specs=[vmem()] * 6,
         out_specs=[vmem()] * 2,
         out_shape=[
             jax.ShapeDtypeStruct((T, H * D), BF16 if last else F32),
@@ -196,7 +265,7 @@
         compiler_params=pltpu.CompilerParams(vmem_limit_bytes=24 << 20),
         cost_estimate=cost(2, 6 << 20),
         name="other_block",
-    )(ids, q, g, stat, k, v, part)
+    )(q, g, stat, message, theirs, part)
 
 
 def passed_along(value, steps):
@@ -210,39 +279,18 @@
     return lax.ppermute(value, "blk", [(source, source ^ 1) for source in range(count)])
 
 
-def first_piece(positions):
-    piece = positions[0] // HALF
-    in_first = lax.axis_index("tp") < lax.axis_size("tp") // 2
-    return jnp.where(in_first, piece, PIECES - 1 - piece)
-
-
-def low_row(first):
-    return jnp.where(first < PIECES // 2, 0, HALF).astype(jnp.int32)
-
-
-def low_piece(first):
-    return jnp.minimum(first, PIECES - 1 - first)
-
-
 def on_device(q, k, v, o, g, log_total, positions):
-    k_two, v_two, pos_two = passed_along(k, 2), passed_along(v, 2), passed_along(positions, 2)
-    first = first_piece(positions)
-    off = low_row(first)
-    dq, dkv, stat = own_block(off.reshape(1), q, g, o, log_total, k, v)
-    even = lax.axis_index("blk") % 2 == 0
-    k_one, v_one, pos_one = (
-        swapped(jnp.where(even, a, b))
-        for a, b in ((k, k_two), (v, v_two), (positions, pos_two))
-    )
-
-    def ids(pos):
-        theirs = first_piece(pos)
-        lows = (low_piece(first) > low_piece(theirs)).astype(jnp.int32)
-        return jnp.stack([off, low_row(theirs), lows])
-
-    dq, dkv_two = other_block(False, ids(pos_two), q, g, stat, k_two, v_two, dq)
+    q, k, v, o, g, log_total, positions = (
+        pltpu.with_memory_space_constraint(x, pltpu.HBM) for x in (q, k, v, o, g, log_total, positions)
+    )
+    message = pack(k, v, positions)
+    two = passed_along(message, 2)
+    dq, dkv, stat, q, g = own_block(q, g, o, log_total, message)
+    two, dq = lax.optimization_barrier((two, dq))
+    one = swapped(jnp.where(lax.axis_index("blk") % 2 == 0, message, two))
+    dq, dkv_two = other_block(False, q, g, stat, message, two, dq)
     back_two = passed_along(dkv_two, -2)
-    dq, dkv_one = other_block(True, ids(pos_one), q, g, stat, k_one, v_one, dq)
+    dq, dkv_one = other_block(True, q, g, stat, message, one, dq)
     back_one = passed_along(dkv_one, -1)
     total = (dkv + back_two.astype(F32) + back_one.astype(F32)).astype(BF16)
     return dq, total[:T], total[T:]

time: 48.2 us -> 37.3 us (0.77); the launches traced: 47.5 us -> 37.1 us
  local copies, waits for them, and re-layouts: 9.85 us -> 1.7 us
  starting transfers between devices: 13.4 us -> 8.48 us
  waiting for transfers between devices: 7.47 us -> 11.1 us
  between operations: 3.69 us -> 0.67 us
  Pallas kernels: 12.7 us -> 15.1 us
    unnamed x26 -> x4, local copies, waits for them, and re-layouts: 9.14 us -> 0.99 us
    ppermute x5 -> x3, waiting for transfers between devices: 6.72 us -> 11.1 us  [passed_along(): return lax.ppermute(value, 'blk', pairs)]
    ppermute x5 -> x3, starting transfers between devices: 11.2 us -> 7.17 us  [passed_along(): return lax.ppermute(value, 'blk', pairs)]
    pallas_call x3 -> x4, Pallas kernels: 12.7 us -> 15.1 us  [the longest x2 6.81 us: other_block(): pl.pallas_call(functools.partial(other_kernel, last), in_specs=[vmem()] *...]
    ppermute x3 -> x1, starting transfers between devices: 2.28 us -> 1.32 us  [swapped(): lax.ppermute(value, 'blk', [(source, source ^ 1) for source in range(coun...]
    ppermute x3 -> x1, waiting for transfers between devices: 0.75 us -> 0.01 us  [swapped(): lax.ppermute(value, 'blk', [(source, source ^ 1) for source in range(coun...]
  transfers between devices with their start and end apart: 8 -> 4, of which waited for: 3 -> 3; matrix products, arithmetic and copies ran while one was open for 0% -> 0% of each run, Pallas kernels for 27% -> 36%
where the time goes in v2:
time: 37.3 us; the launch traced here: 37.1 us
  Pallas kernels  15.1 us (40%)
  waiting for transfers between devices  11.1 us (30%)
  starting transfers between devices  8.48 us (23%)
  local copies, waits for them, and re-layouts  1.7 us (5%)
  between operations  0.67 us (2%)
    ppermute x3, waiting for transfers between devices, passed_along(): return lax.ppermute(value, 'blk', pairs)  11.1 us
    ppermute x3, starting transfers between devices, passed_along(): return lax.ppermute(value, 'blk', pairs)  7.17 us
    pallas_call x2, Pallas kernels, other_block(): pl.pallas_call(functools.partial(other_kernel, last), in_specs=[vmem()] *...  6.81 us
    pallas_call x1, Pallas kernels, own_block(): pl.pallas_call(own_kernel, in_specs=[hbm()] * 4 + [vmem()], out_specs=[vm...  6.55 us
    pallas_call x1, Pallas kernels, pack(): pl.pallas_call(pack_kernel, in_specs=[hbm()] * 3, out_specs=vmem(), out_s...  1.7 us
    ppermute x1, starting transfers between devices, swapped(): lax.ppermute(value, 'blk', [(source, source ^ 1) for source in range(coun...  1.32 us
    unnamed x4, local copies, waits for them, and re-layouts  0.99 us
  transfers between devices with their start and end apart: 4, of which 3 were waited for; matrix products, arithmetic and copies ran while one was open for 0% of the time, Pallas kernels for 36%

profile of v2, /device:TPU:1, one launch (start us, length us, event | category | flops | bytes accessed | tf_op | source)
XLA Modules:
  0.0 37.1 jit_solution(17316466618248646593)
XLA Ops:
  0.6 1.7 %pack.1.message = bf16[1040,128]{1,0:T(8,128)(2,1)} custom-call(bf16[512,128]{1,0:T(8,128)(2,1)} %k_hbm.1, bf16[512,128]{1,0:T(8,128)(2,1)} %v_hbm.1, s32[64]{0:T(128)} %pos_hbm.1), custom_call_target="tpu_custom_call" | custom-call | tf_op jit(solution)/shard_map/pack/pallas_call | solution.py:221
  2.3 3.7 %collective-permute-start = (bf16[1040,128]{1,0:T(8,128)(2,1)}, bf16[1040,128]{1,0:T(8,128)(2,1)S(1)}, u32[]{:S(2)}, u32[]{:S(2)}) collective-permute-start(bf16[1040,128]{1,0:T(8,128)(2,1)} %pack.1.message), channel_id=1, source_target_pairs={{0,16},{8,24},{16,32},{24,40},{32,48},{40,56},{48,64},{56,72},{64,... | collective-permute-start | bytes 798728 | tf_op jit(solution)/shard_map/ppermute | solution.py:274
  6.0 0.0 copy-start
  6.0 1.0 %copy-done = bf16[1040,128]{1,0:T(8,128)(2,1)S(1)} copy-done((bf16[1040,128]{1,0:T(8,128)(2,1)S(1)}, bf16[1040,128]{1,0:T(8,128)(2,1)}, u32[]{:S(2)}) %copy-start) | copy-done | bytes 266264
  7.0 0.0 copy-start.1
  7.0 6.5 %own_block.1 = (f32[512,1024]{1,0:T(8,128)S(1)}, f32[1024,128]{1,0:T(8,128)S(1)}, f32[16,512]{1,0:T(8,128)S(1)}, bf16[512,1024]{1,0:T(8,128)(2,1)S(1)}, bf16[512,1024]{1,0:T(8,128)(2,1)S(1)}) custom-call(bf16[512,1024]{1,0:T(8,128)(2,1)} %q_hbm.1, bf16[512,1024]{1,0:T(8,128)(2,1)} %g_hbm.1, bf16[512,1024]{1,0:T(8,128)(2,1)} %o_hbm.1, f32[8,512]{1,0:T(8,128)} %l_hbm.1, ...), custom_call_target="tpu_custom_call" | custom-call | flops 4026531840 | bytes 6291456 | tf_op jit(solution)/shard_map/own_block/pallas_call | solution.py:232
  13.5 4.1 %collective-permute-done.theirs = bf16[1040,128]{1,0:T(8,128)(2,1)S(1)} collective-permute-done((bf16[1040,128]{1,0:T(8,128)(2,1)}, bf16[1040,128]{1,0:T(8,128)(2,1)S(1)}, u32[]{:S(2)}, u32[]{:S(2)}) %collective-permute-start) | collective-permute-done | bytes 266272 | tf_op jit(solution)/shard_map/ppermute | solution.py:274
  17.6 1.3 %collective-permute-start.1 = (bf16[1040,128]{1,0:T(8,128)(2,1)S(1)}, bf16[1040,128]{1,0:T(8,128)(2,1)S(1)}, u32[]{:S(2)}, u32[]{:S(2)}) collective-permute-start(bf16[1040,128]{1,0:T(8,128)(2,1)S(1)} %broadcast_select_fusion), channel_id=1, source_target_pairs={{0,8},{8,0},{16,24},{24,16},{32,40},{40,32},{48,56},{56,48},{64,72... | collective-permute-start | bytes 798728 | tf_op jit(solution)/shard_map/ppermute | solution.py:279
  19.0 0.0 copy-done.1
  19.0 3.2 %other_block.2 = (f32[512,1024]{1,0:T(8,128)S(1)}, bf16[1024,128]{1,0:T(8,128)(2,1)S(1)}) custom-call(bf16[512,1024]{1,0:T(8,128)(2,1)S(1)} %get-tuple-element.14.q_ref, bf16[512,1024]{1,0:T(8,128)(2,1)S(1)} %get-tuple-element.15.g_ref, f32[16,512]{1,0:T(8,128)S(1)} %get-tuple-element.16.stat_ref, bf16[1040,128]{1,0:T(8,128)(2,1)S(1)} %copy-done.1, ...), custom_call_target="tpu_custom_call" | custom-call | flops 2684354560 | bytes 6291456 | tf_op jit(solution)/shard_map/other_block/pallas_call | solution.py:256
  22.2 3.2 %collective-permute-start.2 = (bf16[1024,128]{1,0:T(8,128)(2,1)S(1)}, bf16[1024,128]{1,0:T(8,128)(2,1)S(1)}, u32[]{:S(2)}, u32[]{:S(2)}) collective-permute-start(bf16[1024,128]{1,0:T(8,128)(2,1)S(1)} %get-tuple-element.23), channel_id=1, source_target_pairs={{0,240},{8,248},{16,0},{24,8},{32,16},{40,24},{48,32},{56,40},{64,... | collective-permute-start | bytes 786440 | tf_op jit(solution)/shard_map/ppermute | solution.py:274
  25.4 0.0 collective-permute-done.1.theirs
  25.4 3.6 %other_block.3 = (bf16[512,1024]{1,0:T(8,128)(2,1)}, bf16[1024,128]{1,0:T(8,128)(2,1)S(1)}) custom-call(bf16[512,1024]{1,0:T(8,128)(2,1)S(1)} %get-tuple-element.14.q_ref, bf16[512,1024]{1,0:T(8,128)(2,1)S(1)} %get-tuple-element.15.g_ref, f32[16,512]{1,0:T(8,128)S(1)} %get-tuple-element.16.stat_ref, bf16[1040,128]{1,0:T(8,128)(2,1)S(1)} %copy-done.1, ...), custom_call_target="tpu_custom_call" | custom-call | flops 2684354560 | bytes 6291456 | tf_op jit(solution)/shard_map/other_block/pallas_call | solution.py:256
  29.0 0.3 collective-permute-start.3
  29.3 2.6 %collective-permute-done.2 = bf16[1024,128]{1,0:T(8,128)(2,1)S(1)} collective-permute-done((bf16[1024,128]{1,0:T(8,128)(2,1)S(1)}, bf16[1024,128]{1,0:T(8,128)(2,1)S(1)}, u32[]{:S(2)}, u32[]{:S(2)}) %collective-permute-start.2) | collective-permute-done | bytes 262176 | tf_op jit(solution)/shard_map/ppermute | solution.py:274
  31.9 4.4 %collective-permute-done.3 = bf16[1024,128]{1,0:T(8,128)(2,1)S(1)} collective-permute-done((bf16[1024,128]{1,0:T(8,128)(2,1)S(1)}, bf16[1024,128]{1,0:T(8,128)(2,1)S(1)}, u32[]{:S(2)}, u32[]{:S(2)}) %collective-permute-start.3) | collective-permute-done | bytes 262176 | tf_op jit(solution)/shard_map/ppermute | solution.py:274
  36.3 0.1 add_convert_fusion
  36.4 0.7 %fusion = (bf16[512,128]{1,0:T(8,128)(2,1)}, bf16[512,128]{1,0:T(8,128)(2,1)}) fusion(bf16[1024,128]{1,0:T(8,128)(2,1)S(1)} %add_convert_fusion), kind=kLoop, calls=%fused_computation.2 | loop fusion | bytes 524288 | tf_op jit(solution)/shard_map/slice | solution.py:296
  (1 shorter events, 0.0 us)
Async XLA Ops:
  2.3 15.3 %collective-permute-start = (bf16[1040,128]{1,0:T(8,128)(2,1)}, bf16[1040,128]{1,0:T(8,128)(2,1)S(1)}, u32[]{:S(2)}, u32[]{:S(2)}) collective-permute-start(bf16[1040,128]{1,0:T(8,128)(2,1)} %pack.1.message), channel_id=1, source_target_pairs={{0,16},{8,24},{16,32},{24,40},{32,48},{40,56},{48,64},{56,72},{64,... | collective-permute-start | bytes 798728 | tf_op jit(solution)/shard_map/ppermute | solution.py:274
  6.0 1.0 %copy-start = (bf16[1040,128]{1,0:T(8,128)(2,1)S(1)}, bf16[1040,128]{1,0:T(8,128)(2,1)}, u32[]{:S(2)}) copy-start(bf16[1040,128]{1,0:T(8,128)(2,1)} %pack.1.message) | copy-start | bytes 798724
  7.0 12.0 %copy-start.1 = (bf16[1040,128]{1,0:T(8,128)(2,1)S(1)}, bf16[1040,128]{1,0:T(8,128)(2,1)}, u32[]{:S(2)}) copy-start(bf16[1040,128]{1,0:T(8,128)(2,1)} %pack.1.message) | copy-start | bytes 798724
  17.6 7.8 %collective-permute-start.1 = (bf16[1040,128]{1,0:T(8,128)(2,1)S(1)}, bf16[1040,128]{1,0:T(8,128)(2,1)S(1)}, u32[]{:S(2)}, u32[]{:S(2)}) collective-permute-start(bf16[1040,128]{1,0:T(8,128)(2,1)S(1)} %broadcast_select_fusion), channel_id=1, source_target_pairs={{0,8},{8,0},{16,24},{24,16},{32,40},{40,32},{48,56},{56,48},{64,72... | collective-permute-start | bytes 798728 | tf_op jit(solution)/shard_map/ppermute | solution.py:279
  22.2 9.7 %collective-permute-start.2 = (bf16[1024,128]{1,0:T(8,128)(2,1)S(1)}, bf16[1024,128]{1,0:T(8,128)(2,1)S(1)}, u32[]{:S(2)}, u32[]{:S(2)}) collective-permute-start(bf16[1024,128]{1,0:T(8,128)(2,1)S(1)} %get-tuple-element.23), channel_id=1, source_target_pairs={{0,240},{8,248},{16,0},{24,8},{32,16},{40,24},{48,32},{56,40},{64,... | collective-permute-start | bytes 786440 | tf_op jit(solution)/shard_map/ppermute | solution.py:274
  29.0 7.3 %collective-permute-start.3 = (bf16[1024,128]{1,0:T(8,128)(2,1)S(1)}, bf16[1024,128]{1,0:T(8,128)(2,1)S(1)}, u32[]{:S(2)}, u32[]{:S(2)}) collective-permute-start(bf16[1024,128]{1,0:T(8,128)(2,1)S(1)} %get-tuple-element.24), channel_id=1, source_target_pairs={{0,248},{8,0},{16,8},{24,16},{32,24},{40,32},{48,40},{56,48},{64,5... | collective-permute-start | bytes 786440 | tf_op jit(solution)/shard_map/ppermute | solution.py:274

commit v3 on v2

v3 whole, which is shorter than its diff:
```python
import functools
import math

import jax
import jax.numpy as jnp
from jax import lax
from jax.experimental import pallas as pl
from jax.experimental.pallas import tpu as pltpu
from jax.sharding import PartitionSpec as P

D = 128
H = 8
T = 512
HALF = T // 2
PIECES = 64
IDS = 16
GROUP = 4
SCALE = 1.0 / math.sqrt(D)
LOG2E = math.log2(math.e)
SCORE_SCALE = SCALE * LOG2E
F32 = jnp.float32
BF16 = jnp.bfloat16


def dot(a, b):
    return lax.dot_general(a, b, (((1,), (0,)), ((), ())), preferred_element_type=F32)


def dot_t(a, b):
    return lax.dot_general(a, b, (((1,), (1,)), ((), ())), preferred_element_type=F32)


def cat(parts, axis):
    return parts[0] if len(parts) == 1 else jnp.concatenate(parts, axis)


def products(parts, matrix):
    whole = dot(cat(parts, 0), matrix)
    return [whole[n * HALF : (n + 1) * HALF, :] for n in range(len(parts))]


def weights_of(scores, grads, log_total, row_dot, mask):
    p = jnp.exp2(scores * SCORE_SCALE - log_total)
    if mask is not None:
        p = jnp.where(mask, p, 0.0)
    ds = p * (grads - row_dot)
    return p.astype(BF16), ds.astype(BF16)


def piece_of(message):
    return jnp.max(message[T:, :].astype(F32)).astype(jnp.int32)


def low_row(first):
    return pl.multiple_of(jnp.where(first < PIECES // 2, 0, HALF), HALF)


def low_piece(first):
    return jnp.minimum(first, PIECES - 1 - first)


def pack_kernel(k_hbm, v_hbm, pos_hbm, low, high, pos, k_ref, v_ref, sems):
    copies = [
        pltpu.make_async_copy(source, target, sems.at[i])
        for i, (source, target) in enumerate(((pos_hbm, pos), (k_hbm, k_ref), (v_hbm, v_ref)))
    ]
    for copy in copies:
        copy.start()
    copies[0].wait()
    piece = pos[0] // HALF
    in_first = lax.axis_index("tp") < lax.axis_size("tp") // 2
    first = jnp.where(in_first, piece, PIECES - 1 - piece)
    low[T:, :] = jnp.full((IDS, D), first.astype(F32), F32).astype(BF16)
    ql = low_row(first)
    qh = pl.multiple_of(HALF - ql, HALF)
    for copy, source, at in ((copies[1], k_ref, 0), (copies[2], v_ref, HALF)):
        copy.wait()
        low[at : at + HALF, :] = source[pl.ds(ql, HALF), :]
        high[at : at + HALF, :] = source[pl.ds(qh, HALF), :]


def transposed_stat(stat_ref, stat_t):
    stat_t[...] = stat_ref[...].T


def stat_of(stat_t, rows, h):
    return stat_t[pl.ds(rows, HALF), h : h + 1], stat_t[pl.ds(rows, HALF), H + h : H + h + 1]


def stat_kernel(q_hbm, g_hbm, o_hbm, l_hbm, message, q_ref, g_ref, stat_ref, o_ref, l_ref, sems):
    load_l = pltpu.make_async_copy(l_hbm, l_ref, sems.at[0, 2])
    load_q = pltpu.make_async_copy(q_hbm, q_ref, sems.at[1, 2])
    loads = []
    for n, h0 in enumerate(range(0, H, GROUP)):
        cols = pl.ds(h0 * D, GROUP * D)
        loads.append(
            [
                pltpu.make_async_copy(source.at[:, cols], target.at[:, cols], sems.at[n, i])
                for i, (source, target) in enumerate(((g_hbm, g_ref), (o_hbm, o_ref)))
            ]
        )
        for load in loads[n]:
            load.start()
    load_l.start()
    load_q.start()
    rows = lax.broadcasted_iota(jnp.int32, (H, 2 * D), 0)
    row_dot = jnp.zeros((H, T), F32)
    for n, h0 in enumerate(range(0, H, GROUP)):
        for load in loads[n]:
            load.wait()
        for h in range(h0, h0 + GROUP):
            cols = slice(h * D, (h + 1) * D)
            prod = g_ref[:, cols].astype(F32) * o_ref[:, cols].astype(F32)
            top = prod.astype(BF16)
            rest = (prod - top.astype(F32)).astype(BF16)
            pick = jnp.where(rows == h, 1.0, 0.0).astype(BF16)
            row_dot += dot_t(pick, jnp.concatenate([top, rest], 1))
    load_l.wait()
    stat_ref[0:H, :] = l_ref[...] * LOG2E
    stat_ref[H : 2 * H, :] = row_dot
    stat_ref[2 * H :, :] = jnp.full((H, T), piece_of(message).astype(F32), F32)
    load_q.wait()


def own_kernel(q_ref, g_ref, stat_ref, low_ref, high_ref, keep_ref, keep_h, x_low, x_high, dq_ref, low_total, high_total, stat_t):
    transposed_stat(stat_ref, stat_t)
    ql = low_row(piece_of(low_ref))
    qh = pl.multiple_of(HALF - ql, HALF)
    mask = lax.broadcasted_iota(jnp.int32, (HALF, HALF), 1) <= lax.broadcasted_iota(
        jnp.int32, (HALF, HALF), 0
    )
    kl, vl = low_ref[:HALF, :], low_ref[HALF:T, :]
    kh, vh = high_ref[:HALF, :], high_ref[HALF:, :]
    sums = None
    for h0 in (0, GROUP):
        heads = [slice(h * D, (h + 1) * D) for h in range(h0, h0 + GROUP)]
        q0, q1 = ([q_ref[pl.ds(rows, HALF), cols] for cols in heads] for rows in (ql, qh))
        g0, g1 = ([g_ref[pl.ds(rows, HALF), cols] for cols in heads] for rows in (ql, qh))
        scores_l, grads_l = products(q0 + q1, kl.T), products(g0 + g1, vl.T)
        scores_h, grads_h = products(q1, kh.T), products(g1, vh.T)
        p_l, d_l, p_h, d_h = [], [], [], []
        for n in range(2 * GROUP):
            rows, masked = (ql, mask) if n < GROUP else (qh, None)
            stat = stat_of(stat_t, rows, h0 + n % GROUP)
            p, d = weights_of(scores_l[n], grads_l[n], *stat, masked)
            p_l, d_l = p_l + [p], d_l + [d]
        for n in range(GROUP):
            p, d = weights_of(scores_h[n], grads_h[n], *stat_of(stat_t, qh, h0 + n), mask)
            p_h, d_h = p_h + [p], d_h + [d]
        lows = products(d_l[:GROUP], kl)
        highs = products(
            [jnp.concatenate([d_l[GROUP + n], d_h[n]], 1) for n in range(GROUP)],
            jnp.concatenate([kl, kh], 0),
        )
        for n, cols in enumerate(heads):
            dq_ref[pl.ds(ql, HALF), cols] = keep_ref[pl.ds(ql, HALF), cols].astype(F32) + lows[n]
            kept = keep_ref[pl.ds(qh, HALF), cols].astype(F32) + keep_h[:, cols].astype(F32)
            dq_ref[pl.ds(qh, HALF), cols] = kept + highs[n]
        g0_t, g1_t = cat([g.T for g in g0], 1), cat([g.T for g in g1], 1)
        q0_t, q1_t = cat([q.T for q in q0], 1), cat([q.T for q in q1], 1)
        dv_l, dv_h = dot(cat([g0_t, g1_t], 1), cat(p_l, 0)), dot(g1_t, cat(p_h, 0))
        dk_l, dk_h = dot(cat([q0_t, q1_t], 1), cat(d_l, 0)), dot(q1_t, cat(d_h, 0))
        part = (dk_l, dv_l, dk_h, dv_h)
        sums = part if sums is None else tuple(x + y for x, y in zip(sums, part))
    dk_l, dv_l, dk_h, dv_h = sums
    even = is_even()
    for total, more, dk, dv in ((low_total, x_low, dk_l, dv_l), (high_total, x_high, dk_h, dv_h)):
        total[:HALF, :] = (dk * SCALE).T + jnp.where(even, more[:HALF, :], 0.0)
        total[HALF:, :] = dv.T + jnp.where(even, more[HALF:, :], 0.0)


class Queries:

    def __init__(self, q_ref, g_ref, stat_ref, theirs_low, stat_t):
        transposed_stat(stat_ref, stat_t)
        self.q_ref, self.g_ref, self.stat_t = q_ref, g_ref, stat_t
        first = jnp.max(stat_ref[2 * H :, :]).astype(jnp.int32)
        self.low = low_row(first)
        self.high = pl.multiple_of(HALF - self.low, HALF)
        self.lows = low_piece(first) > low_piece(piece_of(theirs_low))

    def quadrant(self, rows, keys, dq_ref, at):
        k, v = keys[:HALF, :], keys[HALF:T, :]
        k_t, v_t = k.T, v.T
        heads = [slice(h * D, (h + 1) * D) for h in range(H)]
        qs = [self.q_ref[pl.ds(rows, HALF), cols] for cols in heads]
        gs = [self.g_ref[pl.ds(rows, HALF), cols] for cols in heads]
        scores, grads = products(qs, k_t), products(gs, v_t)
        ps, ds = [], []
        for h in range(H):
            p, d = weights_of(scores[h], grads[h], *stat_of(self.stat_t, rows, h), None)
            ps, ds = ps + [p], ds + [d]
        for h, x in enumerate(products(ds, k)):
            dq_ref[pl.ds(at, HALF), heads[h]] = x.astype(BF16)
        dv = dot(cat([g.T for g in gs], 1), cat(ps, 0))
        dk = dot(cat([q.T for q in qs], 1), cat(ds, 0))
        return (dk * SCALE).T, dv.T

    def low_keys(self, keys, dq_ref, total):
        dk, dv = self.quadrant(self.high, keys, dq_ref, self.high)
        total[:HALF, :] = dk
        total[HALF:, :] = dv

        @pl.when(self.lows)
        def _():
            dk, dv = self.quadrant(self.low, keys, dq_ref, self.low)
            total[:HALF, :] += dk
            total[HALF:, :] += dv

        @pl.when(jnp.logical_not(self.lows))
        def _():
            dq_ref[pl.ds(self.low, HALF), :] = jnp.zeros((HALF, H * D), BF16)

    def high_keys(self, keys, dq_ref, total, adds):
        @pl.when(jnp.logical_not(self.lows))
        def _():
            dk, dv = self.quadrant(self.high, keys, dq_ref, 0)
            if adds:
                total[:HALF, :] += dk
                total[HALF:, :] += dv
            else:
                total[:HALF, :] = dk
                total[HALF:, :] = dv

        @pl.when(self.lows)
        def _():
            dq_ref[...] = jnp.zeros((HALF, H * D), BF16)
            if not adds:
                total[...] = jnp.zeros((T, D), F32)


def is_even():
    return lax.axis_index("blk") % 2 == 0


def first_kernel(q_ref, g_ref, stat_ref, theirs_low, dq_ref, low_total, stat_t):
    queries = Queries(q_ref, g_ref, stat_ref, theirs_low, stat_t)
    queries.low_keys(theirs_low, dq_ref, low_total)


def second_kernel(q2_ref, g2_ref, stat2_ref, own_low, own_high, theirs_low, dq_ref, dq_h, x_low, x_high, stat_t):
    even = is_even()

    @pl.when(even)
    def _():
        queries = Queries(q2_ref, g2_ref, stat2_ref, own_low, stat_t)
        queries.low_keys(own_low, dq_ref, x_low)
        queries.high_keys(own_high, dq_h, x_high, False)

    @pl.when(jnp.logical_not(even))
    def _():
        Queries(q2_ref, g2_ref, stat2_ref, theirs_low, stat_t).low_keys(theirs_low, dq_ref, x_low)


def send_whole(stat2_ref, dq_ref, dq_h, out_ref):
    high = pl.multiple_of(HALF - low_row(jnp.max(stat2_ref[2 * H :, :]).astype(jnp.int32)), HALF)
    low = pl.multiple_of(HALF - high, HALF)
    total = dq_ref[pl.ds(high, HALF), :].astype(F32) + dq_h[...].astype(F32)
    out_ref[pl.ds(high, HALF), :] = total.astype(BF16)
    out_ref[pl.ds(low, HALF), :] = dq_ref[pl.ds(low, HALF), :]


def third_kernel(q_ref, g_ref, stat_ref, q2_ref, g2_ref, stat2_ref, theirs_low, theirs_high, low_total, x_low, x_dq, x_dq_h, keep_h, send, back, high_total, dq_h, stat_t):
    even = is_even()
    queries = Queries(q_ref, g_ref, stat_ref, theirs_low, stat_t)
    queries.high_keys(theirs_high, keep_h, high_total, False)

    @pl.when(even)
    def _():
        send_whole(stat2_ref, x_dq, x_dq_h, send)
        back[:T, :] = low_total[...].astype(BF16)

    @pl.when(jnp.logical_not(even))
    def _():
        others = Queries(q2_ref, g2_ref, stat2_ref, theirs_low, stat_t)
        others.high_keys(theirs_high, dq_h, high_total, True)
        send_whole(stat2_ref, x_dq, dq_h, send)
        back[:T, :] = (low_total[...] + x_low[...]).astype(BF16)

    back[T:, :] = high_total[...].astype(BF16)


def query_kernel(dq_ref, got_ref, out_ref):
    out_ref[...] = ((dq_ref[...] + got_ref[...].astype(F32)) * SCALE).astype(BF16)


def key_kernel(own_low, low_total, high_total, got_ref, dk_ref, dv_ref):
    ql = low_row(piece_of(own_low))
    qh = pl.multiple_of(HALF - ql, HALF)
    for total, rows, at in ((low_total, ql, 0), (high_total, qh, T)):
        for out, n in ((dk_ref, 0), (dv_ref, HALF)):
            got = got_ref[at + n : at + n + HALF, :].astype(F32)
            out[pl.ds(rows, HALF), :] = (total[n : n + HALF, :] + got).astype(BF16)


def vmem():
    return pl.BlockSpec(memory_space=pltpu.VMEM)


def cost(quadrants, size):
    return pl.CostEstimate(
        flops=int(quadrants * H * 10 * HALF * HALF * D),
        bytes_accessed=size,
        transcendentals=int(quadrants * H * HALF * HALF),
    )


def hbm():
    return pl.BlockSpec(memory_space=pltpu.HBM)


def pack(k, v, positions):
    return pl.pallas_call(
        pack_kernel,
        in_specs=[hbm()] * 3,
        out_specs=vmem(),
        out_shape=jax.ShapeDtypeStruct((2 * T + IDS, D), BF16),
        scratch_shapes=[pltpu.SMEM(positions.shape, jnp.int32), pltpu.SemaphoreType.DMA((3,))],
        name="pack",
    )(k, v, positions)


def hbm():
    return pl.BlockSpec(memory_space=pltpu.HBM)


def in_vmem(value):
    return pltpu.with_memory_space_constraint(value, pltpu.VMEM)


def array(shape, dtype):
    return jax.ShapeDtypeStruct(shape, dtype)


def call(kernel, name, ins, outs, scratch=(), quadrants=0, from_hbm=0):
    size = sum(x.size * x.dtype.itemsize for x in list(ins) + list(outs))
    return pl.pallas_call(
        kernel,
        in_specs=[hbm()] * from_hbm + [vmem()] * (len(ins) - from_hbm),
        out_specs=[vmem()] * len(outs),
        out_shape=list(outs),
        scratch_shapes=list(scratch),
        compiler_params=pltpu.CompilerParams(vmem_limit_bytes=24 << 20),
        cost_estimate=cost(quadrants, size),
        name=name,
    )(*ins)


def passed_along(value, steps):
    count = lax.axis_size("blk")
    pairs = [(source, (source + steps) % count) for source in range(count)]
    return lax.ppermute(value, "blk", pairs)


def swapped(value):
    count = lax.axis_size("blk")
    return lax.ppermute(value, "blk", [(source, source ^ 1) for source in range(count)])


def on_device(q_in, k, v, o, g_in, log_total, positions):
    q_in, k, v, o, g_in, log_total, positions = (
        pltpu.with_memory_space_constraint(x, pltpu.HBM)
        for x in (q_in, k, v, o, g_in, log_total, positions)
    )
    rows, half_rows = array((T, H * D), BF16), array((HALF, H * D), BF16)
    stat_t = pltpu.VMEM((T, 3 * H), F32)
    terms, half_terms = array((2 * T, D), F32), array((T, D), F32)
    low, high = call(
        pack_kernel,
        "pack",
        (k, v, positions),
        (array((T + IDS, D), BF16), array((T, D), BF16)),
        (
            pltpu.SMEM(positions.shape, jnp.int32),
            pltpu.VMEM((T, D), BF16),
            pltpu.VMEM((T, D), BF16),
            pltpu.SemaphoreType.DMA((3,)),
        ),
        from_hbm=3,
    )
    theirs_low = in_vmem(passed_along(low, 2))
    low, q_swap, g_swap = lax.optimization_barrier((low, q_in, g_in))
    q2, g2 = in_vmem(swapped(q_swap)), in_vmem(swapped(g_swap))
    q, g, stat = call(
        stat_kernel,
        "stat",
        (q_in, g_in, o, log_total, low),
        (rows, rows, array((3 * H, T), F32)),
        (pltpu.VMEM((T, H * D), BF16), pltpu.VMEM((H, T), F32), pltpu.SemaphoreType.DMA((2, 3))),
        from_hbm=4,
    )
    high, stat = lax.optimization_barrier((high, stat))
    theirs_high = in_vmem(passed_along(high, 2))
    stat2 = in_vmem(swapped(stat))
    keep, low_total = call(
        first_kernel,
        "first",
        (q, g, stat, theirs_low),
        (rows, half_terms),
        (stat_t,),
        quadrants=1.5,
    )
    x_dq, x_dq_h, x_low, x_high = call(
        second_kernel,
        "second",
        (q2, g2, stat2, low, high, theirs_low),
        (rows, half_rows, half_terms, half_terms),
        (stat_t,),
        quadrants=2,
    )
    theirs_high, x_dq = lax.optimization_barrier((theirs_high, x_dq))
    keep_h, send, message_back = call(
        third_kernel,
        "third",
        (q, g, stat, q2, g2, stat2, theirs_low, theirs_high, low_total, x_low, x_dq, x_dq_h),
        (half_rows, rows, array((2 * T, D), BF16)),
        (pltpu.VMEM((T, D), F32), pltpu.VMEM((HALF, H * D), BF16), stat_t),
        quadrants=0.5,
    )
    back = passed_along(message_back, -2)
    got = in_vmem(swapped(send))
    dq, own_low, own_high = call(
        own_kernel,
        "own",
        (q, g, stat, low, high, keep, keep_h, x_low, x_high),
        (array((T, H * D), F32), half_terms, half_terms),
        (stat_t,),
        quadrants=3,
    )
    (dq,) = call(query_kernel, "query_sum", (dq, got), (rows,))
    back, dq = lax.optimization_barrier((back, dq))
    dk, dv = call(
        key_kernel, "key_sum", (low, own_low, own_high, back), (array((T, D), BF16),) * 2
    )
    return dq, dk, dv


def solution(mesh):
    in_specs = (
        P("blk", "tp"),
        P("blk", "tp"),
        P("blk", "tp"),
        P("blk", "tp"),
        P("blk", "tp"),
        P("tp", "blk"),
        P(("blk", "tp")),
    )
    out_specs = (P("blk", "tp"), P("blk", "tp"), P("blk", "tp"))
    return jax.shard_map(
        on_device, mesh=mesh, in_specs=in_specs, out_specs=out_specs, check_vma=False
    )
```

time: 37.3 us -> 33.5 us (0.90)
  waiting for transfers between devices: 11.1 us -> 5.58 us
  starting transfers between devices: 8.48 us -> 10.5 us
  local copies, waits for them, and re-layouts: 1.7 us -> 0 us
  Pallas kernels: 15.1 us -> 16.6 us
    ppermute x3, waiting for transfers between devices: 11.1 us -> 5.57 us  [passed_along(): return lax.ppermute(value, 'blk', pairs)]
    ppermute x1 -> x4, starting transfers between devices: 1.32 us -> 5.03 us  [swapped(): lax.ppermute(value, 'blk', [(source, source ^ 1) for source in range(coun...]
    ppermute x3, starting transfers between devices: 7.17 us -> 5.45 us  [passed_along(): return lax.ppermute(value, 'blk', pairs)]
    pallas_call x4 -> x8, Pallas kernels: 15.1 us -> 16.6 us  [call(): pl.pallas_call(kernel, in_specs=[hbm()] * from_hbm + [vmem()] * (len(ins)...]
    unnamed x4 -> x0, local copies, waits for them, and re-layouts: 0.99 us -> none
    slice x1 -> x0, local copies, waits for them, and re-layouts: 0.72 us -> none  [on_device(): return (dq, total[:T], total[T:])]
  transfers between devices with their start and end apart: 4 -> 7, of which waited for: 3 -> 2; matrix products, arithmetic and copies ran while one was open for 0% -> 0% of each run, Pallas kernels for 36% -> 38%
where the time goes in v3:
time: 33.5 us; the launch traced here: 33.4 us
  Pallas kernels  16.6 us (50%)
  starting transfers between devices  10.5 us (31%)
  waiting for transfers between devices  5.58 us (17%)
  between operations  0.72 us (2%)
    pallas_call x8, Pallas kernels, call(): pl.pallas_call(kernel, in_specs=[hbm()] * from_hbm + [vmem()] * (len(ins)...  16.6 us
    ppermute x3, waiting for transfers between devices, passed_along(): return lax.ppermute(value, 'blk', pairs)  5.57 us
    ppermute x3, starting transfers between devices, passed_along(): return lax.ppermute(value, 'blk', pairs)  5.45 us
    ppermute x4, starting transfers between devices, swapped(): lax.ppermute(value, 'blk', [(source, source ^ 1) for source in range(coun...  5.03 us
  transfers between devices with their start and end apart: 7, of which 2 were waited for; matrix products, arithmetic and copies ran while one was open for 0% of the time, Pallas kernels for 38%

profile of v3, /device:TPU:1, one launch (start us, length us, event | category | flops | bytes accessed | tf_op | source)
XLA Modules:
  0.0 33.4 jit_solution(14881575001896485168)
XLA Ops:
  0.6 1.0 %pack.1 = (bf16[528,128]{1,0:T(8,128)(2,1)S(1)}, bf16[512,128]{1,0:T(8,128)(2,1)S(1)}) custom-call(bf16[512,128]{1,0:T(8,128)(2,1)} %k_hbm.1, bf16[512,128]{1,0:T(8,128)(2,1)} %v_hbm.1, s32[64]{0:T(128)} %pos_hbm.1), custom_call_target="tpu_custom_call" | custom-call | bytes 528640 | tf_op jit(solution)/shard_map/pack/pallas_call | solution.py:337
  1.6 3.3 %collective-permute-start = (bf16[512,1024]{1,0:T(8,128)(2,1)}, bf16[512,1024]{1,0:T(8,128)(2,1)S(1)}, u32[]{:S(2)}, u32[]{:S(2)}) collective-permute-start(bf16[512,1024]{1,0:T(8,128)(2,1)} %q_hbm.1), channel_id=1, source_target_pairs={{0,8},{8,0},{16,24},{24,16},{32,40},{40,32},{48,56},{56,48},{64,72... | collective-permute-start | bytes 3145736 | tf_op jit(solution)/shard_map/ppermute | solution.py:357
  5.0 0.1 collective-permute-start.1
  5.1 1.0 %collective-permute-start.3 = (bf16[528,128]{1,0:T(8,128)(2,1)S(1)}, bf16[528,128]{1,0:T(8,128)(2,1)S(1)}, u32[]{:S(2)}, u32[]{:S(2)}) collective-permute-start(bf16[528,128]{1,0:T(8,128)(2,1)S(1)} %get-tuple-element.32.message.own_low.low_ref), channel_id=1, source_target_pairs={{0,16},{8,24},{16,32},{24,40},{32,48},{40,56},{48,64},{56,72},{64,... | collective-permute-start | bytes 405512 | tf_op jit(solution)/shard_map/ppermute | solution.py:352
  6.1 2.1 %stat.1 = (bf16[512,1024]{1,0:T(8,128)(2,1)S(1)}, bf16[512,1024]{1,0:T(8,128)(2,1)S(1)}, f32[24,512]{1,0:T(8,128)S(1)}) custom-call(bf16[512,1024]{1,0:T(8,128)(2,1)} %q_hbm.1, bf16[512,1024]{1,0:T(8,128)(2,1)} %g_hbm.1, bf16[512,1024]{1,0:T(8,128)(2,1)} %o_hbm.1, f32[8,512]{1,0:T(8,128)} %l_hbm.1, bf16[528,128]{1,0:T(8,128)(2,1)S(1)} %get-tuple-element.32.message.own_low.low_ref), custom_call_target="tpu_custom_call" | custom-call | bytes 5443584 | tf_op jit(solution)/shard_map/stat/pallas_call | solution.py:337
  8.2 0.8 %collective-permute-start.2 = (f32[24,512]{1,0:T(8,128)S(1)}, f32[24,512]{1,0:T(8,128)S(1)}, u32[]{:S(2)}, u32[]{:S(2)}) collective-permute-start(f32[24,512]{1,0:T(8,128)S(1)} %get-tuple-element.37.stat_ref), channel_id=1, source_target_pairs={{0,8},{8,0},{16,24},{24,16},{32,40},{40,32},{48,56},{56,48},{64,72... | collective-permute-start | bytes 147464 | tf_op jit(solution)/shard_map/ppermute | solution.py:357
  9.0 1.6 %collective-permute-start.4 = (bf16[512,128]{1,0:T(8,128)(2,1)S(1)}, bf16[512,128]{1,0:T(8,128)(2,1)S(1)}, u32[]{:S(2)}, u32[]{:S(2)}) collective-permute-start(bf16[512,128]{1,0:T(8,128)(2,1)S(1)} %get-tuple-element.40.own_high.high_ref), channel_id=1, source_target_pairs={{0,16},{8,24},{16,32},{24,40},{32,48},{40,56},{48,64},{56,72},{64,... | collective-permute-start | bytes 393224 | tf_op jit(solution)/shard_map/ppermute | solution.py:352
  10.6 4.4 %collective-permute-done.3.theirs_low = bf16[528,128]{1,0:T(8,128)(2,1)S(1)} collective-permute-done((bf16[528,128]{1,0:T(8,128)(2,1)S(1)}, bf16[528,128]{1,0:T(8,128)(2,1)S(1)}, u32[]{:S(2)}, u32[]{:S(2)}) %collective-permute-start.3) | collective-permute-done | bytes 135200 | tf_op jit(solution)/shard_map/ppermute | solution.py:352
  15.0 1.6 %first.1 = (bf16[512,1024]{1,0:T(8,128)(2,1)S(1)}, f32[512,128]{1,0:T(8,128)S(1)}) custom-call(bf16[512,1024]{1,0:T(8,128)(2,1)S(1)} %get-tuple-element.33.q_ref, bf16[512,1024]{1,0:T(8,128)(2,1)S(1)} %get-tuple-element.34.g_ref, f32[24,512]{1,0:T(8,128)S(1)} %get-tuple-element.37.stat_ref, bf16[528,128]{1,0:T(8,128)(2,1)S(1)} %collective-permute-done.3.theirs_low), custom_call_target="tpu_custom_call" | custom-call | flops 1006632960 | bytes 3592192 | tf_op jit(solution)/shard_map/first/pallas_call | solution.py:337
  16.6 0.0 collective-permute-done.2.stat2_ref
  16.6 0.0 collective-permute-done.q2_ref
  16.6 0.0 collective-permute-done.1.g2_ref
  16.6 3.5 %second.1 = (bf16[512,1024]{1,0:T(8,128)(2,1)S(1)}, bf16[256,1024]{1,0:T(8,128)(2,1)S(1)}, f32[512,128]{1,0:T(8,128)S(1)}, f32[512,128]{1,0:T(8,128)S(1)}) custom-call(bf16[512,1024]{1,0:T(8,128)(2,1)S(1)} %collective-permute-done.q2_ref, bf16[512,1024]{1,0:T(8,128)(2,1)S(1)} %collective-permute-done.1.g2_ref, ...), custom_call_target="tpu_custom_call" | custom-call | flops 1342177280 | bytes 4644864 | tf_op jit(solution)/shard_map/second/pallas_call | solution.py:337
  20.1 0.0 collective-permute-done.4.theirs_high
  20.1 2.2 %third.1 = (bf16[256,1024]{1,0:T(8,128)(2,1)S(1)}, bf16[512,1024]{1,0:T(8,128)(2,1)S(1)}, bf16[1024,128]{1,0:T(8,128)(2,1)S(1)}) custom-call(bf16[512,1024]{1,0:T(8,128)(2,1)S(1)} %get-tuple-element.33.q_ref, bf16[512,1024]{1,0:T(8,128)(2,1)S(1)} %get-tuple-element.34.g_ref, f32[24,512]{1,0:T(8,128)S(1)} %get-tuple-element.37.stat_ref, ...), custom_call_target="tpu_custom_call" | custom-call | flops 335544320 | bytes 8491008 | tf_op jit(solution)/shard_map/third/pallas_call | solution.py:337
  22.3 0.8 %collective-permute-start.6 = (bf16[512,1024]{1,0:T(8,128)(2,1)S(1)}, bf16[512,1024]{1,0:T(8,128)(2,1)S(1)}, u32[]{:S(2)}, u32[]{:S(2)}) collective-permute-start(bf16[512,1024]{1,0:T(8,128)(2,1)S(1)} %get-tuple-element.52), channel_id=1, source_target_pairs={{0,8},{8,0},{16,24},{24,16},{32,40},{40,32},{48,56},{56,48},{64,72... | collective-permute-start | bytes 3145736 | tf_op jit(solution)/shard_map/ppermute | solution.py:357
  23.2 2.8 %collective-permute-start.5 = (bf16[1024,128]{1,0:T(8,128)(2,1)S(1)}, bf16[1024,128]{1,0:T(8,128)(2,1)S(1)}, u32[]{:S(2)}, u32[]{:S(2)}) collective-permute-start(bf16[1024,128]{1,0:T(8,128)(2,1)S(1)} %get-tuple-element.47), channel_id=1, source_target_pairs={{0,240},{8,248},{16,0},{24,8},{32,16},{40,24},{48,32},{56,40},{64,... | collective-permute-start | bytes 786440 | tf_op jit(solution)/shard_map/ppermute | solution.py:352
  26.0 4.2 %own.1 = (f32[512,1024]{1,0:T(8,128)S(1)}, f32[512,128]{1,0:T(8,128)S(1)}, f32[512,128]{1,0:T(8,128)S(1)}) custom-call(bf16[512,1024]{1,0:T(8,128)(2,1)S(1)} %get-tuple-element.33.q_ref, bf16[512,1024]{1,0:T(8,128)(2,1)S(1)} %get-tuple-element.34.g_ref, f32[24,512]{1,0:T(8,128)S(1)} %get-tuple-element.37.stat_ref, ...), custom_call_target="tpu_custom_call" | custom-call | flops 2013265920 | bytes 7131136 | tf_op jit(solution)/shard_map/own/pallas_call | solution.py:337
  30.2 0.0 collective-permute-done.6.got_ref
  30.2 1.2 %query_sum.1 = bf16[512,1024]{1,0:T(8,128)(2,1)} custom-call(f32[512,1024]{1,0:T(8,128)S(1)} %get-tuple-element.51.dq_ref, bf16[512,1024]{1,0:T(8,128)(2,1)S(1)} %collective-permute-done.6.got_ref), custom_call_target="tpu_custom_call" | custom-call | bytes 4194304 | tf_op jit(solution)/shard_map/query_sum/pallas_call | solution.py:337
  31.4 1.1 %collective-permute-done.5.got_ref = bf16[1024,128]{1,0:T(8,128)(2,1)S(1)} collective-permute-done((bf16[1024,128]{1,0:T(8,128)(2,1)S(1)}, bf16[1024,128]{1,0:T(8,128)(2,1)S(1)}, u32[]{:S(2)}, u32[]{:S(2)}) %collective-permute-start.5) | collective-permute-done | bytes 262176 | tf_op jit(solution)/shard_map/ppermute | solution.py:352
  32.5 0.8 %key_sum.1 = (bf16[512,128]{1,0:T(8,128)(2,1)}, bf16[512,128]{1,0:T(8,128)(2,1)}) custom-call(bf16[528,128]{1,0:T(8,128)(2,1)S(1)} %get-tuple-element.32.message.own_low.low_ref, f32[512,128]{1,0:T(8,128)S(1)} %get-tuple-element.54.low_total, f32[512,128]{1,0:T(8,128)S(1)} %get-tuple-element.55.high_total, bf16[1024,128]{1,0:T(8,128)(2,1)S(1)} %collective-permute-done.5.got_ref), custom_call_target="tpu_custom_call" | custom-call | bytes 1183744 | tf_op jit(solution)/shard_map/key_sum/pallas_call | solution.py:337
Async XLA Ops:
  1.6 15.0 %collective-permute-start = (bf16[512,1024]{1,0:T(8,128)(2,1)}, bf16[512,1024]{1,0:T(8,128)(2,1)S(1)}, u32[]{:S(2)}, u32[]{:S(2)}) collective-permute-start(bf16[512,1024]{1,0:T(8,128)(2,1)} %q_hbm.1), channel_id=1, source_target_pairs={{0,8},{8,0},{16,24},{24,16},{32,40},{40,32},{48,56},{56,48},{64,72... | collective-permute-start | bytes 3145736 | tf_op jit(solution)/shard_map/ppermute | solution.py:357
  5.0 11.7 %collective-permute-start.1 = (bf16[512,1024]{1,0:T(8,128)(2,1)}, bf16[512,1024]{1,0:T(8,128)(2,1)S(1)}, u32[]{:S(2)}, u32[]{:S(2)}) collective-permute-start(bf16[512,1024]{1,0:T(8,128)(2,1)} %g_hbm.1), channel_id=1, source_target_pairs={{0,8},{8,0},{16,24},{24,16},{32,40},{40,32},{48,56},{56,48},{64,72... | collective-permute-start | bytes 3145736 | tf_op jit(solution)/shard_map/ppermute | solution.py:357
  5.1 9.9 %collective-permute-start.3 = (bf16[528,128]{1,0:T(8,128)(2,1)S(1)}, bf16[528,128]{1,0:T(8,128)(2,1)S(1)}, u32[]{:S(2)}, u32[]{:S(2)}) collective-permute-start(bf16[528,128]{1,0:T(8,128)(2,1)S(1)} %get-tuple-element.32.message.own_low.low_ref), channel_id=1, source_target_pairs={{0,16},{8,24},{16,32},{24,40},{32,48},{40,56},{48,64},{56,72},{64,... | collective-permute-start | bytes 405512 | tf_op jit(solution)/shard_map/ppermute | solution.py:352
  8.2 8.4 %collective-permute-start.2 = (f32[24,512]{1,0:T(8,128)S(1)}, f32[24,512]{1,0:T(8,128)S(1)}, u32[]{:S(2)}, u32[]{:S(2)}) collective-permute-start(f32[24,512]{1,0:T(8,128)S(1)} %get-tuple-element.37.stat_ref), channel_id=1, source_target_pairs={{0,8},{8,0},{16,24},{24,16},{32,40},{40,32},{48,56},{56,48},{64,72... | collective-permute-start | bytes 147464 | tf_op jit(solution)/shard_map/ppermute | solution.py:357
  9.0 11.1 %collective-permute-start.4 = (bf16[512,128]{1,0:T(8,128)(2,1)S(1)}, bf16[512,128]{1,0:T(8,128)(2,1)S(1)}, u32[]{:S(2)}, u32[]{:S(2)}) collective-permute-start(bf16[512,128]{1,0:T(8,128)(2,1)S(1)} %get-tuple-element.40.own_high.high_ref), channel_id=1, source_target_pairs={{0,16},{8,24},{16,32},{24,40},{32,48},{40,56},{48,64},{56,72},{64,... | collective-permute-start | bytes 393224 | tf_op jit(solution)/shard_map/ppermute | solution.py:352
  22.3 7.9 %collective-permute-start.6 = (bf16[512,1024]{1,0:T(8,128)(2,1)S(1)}, bf16[512,1024]{1,0:T(8,128)(2,1)S(1)}, u32[]{:S(2)}, u32[]{:S(2)}) collective-permute-start(bf16[512,1024]{1,0:T(8,128)(2,1)S(1)} %get-tuple-element.52), channel_id=1, source_target_pairs={{0,8},{8,0},{16,24},{24,16},{32,40},{40,32},{48,56},{56,48},{64,72... | collective-permute-start | bytes 3145736 | tf_op jit(solution)/shard_map/ppermute | solution.py:357
  23.2 9.4 %collective-permute-start.5 = (bf16[1024,128]{1,0:T(8,128)(2,1)S(1)}, bf16[1024,128]{1,0:T(8,128)(2,1)S(1)}, u32[]{:S(2)}, u32[]{:S(2)}) collective-permute-start(bf16[1024,128]{1,0:T(8,128)(2,1)S(1)} %get-tuple-element.47), channel_id=1, source_target_pairs={{0,240},{8,248},{16,0},{24,8},{32,16},{40,24},{48,32},{56,40},{64,... | collective-permute-start | bytes 786440 | tf_op jit(solution)/shard_map/ppermute | solution.py:352

commit v4 on v3

--- a/solution.py
+++ b/solution.py
@@ -122,7 +122,7 @@
     load_q.wait()
 
 
-def own_kernel(q_ref, g_ref, stat_ref, low_ref, high_ref, keep_ref, keep_h, x_low, x_high, dq_ref, low_total, high_total, stat_t):
+def own_kernel(q_ref, g_ref, stat_ref, low_ref, high_ref, keep_ref, x_low, x_high, dq_ref, low_total, high_total, stat_t):
     transposed_stat(stat_ref, stat_t)
     ql = low_row(piece_of(low_ref))
     qh = pl.multiple_of(HALF - ql, HALF)
@@ -154,7 +154,7 @@
         )
         for n, cols in enumerate(heads):
             dq_ref[pl.ds(ql, HALF), cols] = keep_ref[pl.ds(ql, HALF), cols].astype(F32) + lows[n]
-            kept = keep_ref[pl.ds(qh, HALF), cols].astype(F32) + keep_h[:, cols].astype(F32)
+            kept = keep_ref[pl.ds(qh, HALF), cols].astype(F32)
             dq_ref[pl.ds(qh, HALF), cols] = kept + highs[n]
         g0_t, g1_t = cat([g.T for g in g0], 1), cat([g.T for g in g1], 1)
         q0_t, q1_t = cat([q.T for q in q0], 1), cat([q.T for q in q1], 1)
@@ -179,53 +179,54 @@
         self.high = pl.multiple_of(HALF - self.low, HALF)
         self.lows = low_piece(first) > low_piece(piece_of(theirs_low))
 
-    def quadrant(self, rows, keys, dq_ref, at):
+    def quadrants(self, runs, keys, dq_ref, adds):
         k, v = keys[:HALF, :], keys[HALF:T, :]
         k_t, v_t = k.T, v.T
         heads = [slice(h * D, (h + 1) * D) for h in range(H)]
-        qs = [self.q_ref[pl.ds(rows, HALF), cols] for cols in heads]
-        gs = [self.g_ref[pl.ds(rows, HALF), cols] for cols in heads]
-        scores, grads = products(qs, k_t), products(gs, v_t)
-        ps, ds = [], []
-        for h in range(H):
-            p, d = weights_of(scores[h], grads[h], *stat_of(self.stat_t, rows, h), None)
-            ps, ds = ps + [p], ds + [d]
-        for h, x in enumerate(products(ds, k)):
-            dq_ref[pl.ds(at, HALF), heads[h]] = x.astype(BF16)
-        dv = dot(cat([g.T for g in gs], 1), cat(ps, 0))
-        dk = dot(cat([q.T for q in qs], 1), cat(ds, 0))
+        q_t, g_t, ps, ds = [], [], [], []
+        for rows in runs:
+            qs = [self.q_ref[pl.ds(rows, HALF), cols] for cols in heads]
+            gs = [self.g_ref[pl.ds(rows, HALF), cols] for cols in heads]
+            scores, grads = products(qs, k_t), products(gs, v_t)
+            for h in range(H):
+                p, d = weights_of(scores[h], grads[h], *stat_of(self.stat_t, rows, h), None)
+                ps, ds = ps + [p], ds + [d]
+            q_t, g_t = q_t + [q.T for q in qs], g_t + [g.T for g in gs]
+            for cols, x in zip(heads, products(ds[-H:], k)):
+                if adds:
+                    x += dq_ref[pl.ds(rows, HALF), cols].astype(F32)
+                dq_ref[pl.ds(rows, HALF), cols] = x.astype(BF16)
+        dv = dot(cat(g_t, 1), cat(ps, 0))
+        dk = dot(cat(q_t, 1), cat(ds, 0))
         return (dk * SCALE).T, dv.T
 
     def low_keys(self, keys, dq_ref, total):
-        dk, dv = self.quadrant(self.high, keys, dq_ref, self.high)
-        total[:HALF, :] = dk
-        total[HALF:, :] = dv
-
         @pl.when(self.lows)
         def _():
-            dk, dv = self.quadrant(self.low, keys, dq_ref, self.low)
-            total[:HALF, :] += dk
-            total[HALF:, :] += dv
+            dk, dv = self.quadrants((self.high, self.low), keys, dq_ref, False)
+            total[:HALF, :] = dk
+            total[HALF:, :] = dv
 
         @pl.when(jnp.logical_not(self.lows))
         def _():
             dq_ref[pl.ds(self.low, HALF), :] = jnp.zeros((HALF, H * D), BF16)
+            dk, dv = self.quadrants((self.high,), keys, dq_ref, False)
+            total[:HALF, :] = dk
+            total[HALF:, :] = dv
 
     def high_keys(self, keys, dq_ref, total, adds):
         @pl.when(jnp.logical_not(self.lows))
         def _():
-            dk, dv = self.quadrant(self.high, keys, dq_ref, 0)
+            dk, dv = self.quadrants((self.high,), keys, dq_ref, True)
             if adds:
-                total[:HALF, :] += dk
-                total[HALF:, :] += dv
-            else:
-                total[:HALF, :] = dk
-                total[HALF:, :] = dv
-
-        @pl.when(self.lows)
-        def _():
-            dq_ref[...] = jnp.zeros((HALF, H * D), BF16)
-            if not adds:
+                dk, dv = dk + total[:HALF, :], dv + total[HALF:, :]
+            total[:HALF, :] = dk
+            total[HALF:, :] = dv
+
+        if not adds:
+
+            @pl.when(self.lows)
+            def _():
                 total[...] = jnp.zeros((T, D), F32)
 
 
@@ -238,44 +239,35 @@
     queries.low_keys(theirs_low, dq_ref, low_total)
 
 
-def second_kernel(q2_ref, g2_ref, stat2_ref, own_low, own_high, theirs_low, dq_ref, dq_h, x_low, x_high, stat_t):
+def second_kernel(q2_ref, g2_ref, stat2_ref, own_low, own_high, theirs_low, dq_ref, x_low, x_high, stat_t):
     even = is_even()
 
     @pl.when(even)
     def _():
         queries = Queries(q2_ref, g2_ref, stat2_ref, own_low, stat_t)
         queries.low_keys(own_low, dq_ref, x_low)
-        queries.high_keys(own_high, dq_h, x_high, False)
+        queries.high_keys(own_high, dq_ref, x_high, False)
 
     @pl.when(jnp.logical_not(even))
     def _():
         Queries(q2_ref, g2_ref, stat2_ref, theirs_low, stat_t).low_keys(theirs_low, dq_ref, x_low)
 
 
-def send_whole(stat2_ref, dq_ref, dq_h, out_ref):
-    high = pl.multiple_of(HALF - low_row(jnp.max(stat2_ref[2 * H :, :]).astype(jnp.int32)), HALF)
-    low = pl.multiple_of(HALF - high, HALF)
-    total = dq_ref[pl.ds(high, HALF), :].astype(F32) + dq_h[...].astype(F32)
-    out_ref[pl.ds(high, HALF), :] = total.astype(BF16)
-    out_ref[pl.ds(low, HALF), :] = dq_ref[pl.ds(low, HALF), :]
-
-
-def third_kernel(q_ref, g_ref, stat_ref, q2_ref, g2_ref, stat2_ref, theirs_low, theirs_high, low_total, x_low, x_dq, x_dq_h, keep_h, send, back, high_total, dq_h, stat_t):
+def third_kernel(q_ref, g_ref, stat_ref, q2_ref, g2_ref, stat2_ref, theirs_low, theirs_high, low_total, x_low, _, __, keep, send, back, high_total, stat_t):
     even = is_even()
-    queries = Queries(q_ref, g_ref, stat_ref, theirs_low, stat_t)
-    queries.high_keys(theirs_high, keep_h, high_total, False)
+    Queries(q_ref, g_ref, stat_ref, theirs_low, stat_t).high_keys(
+        theirs_high, keep, high_total, False
+    )
 
     @pl.when(even)
     def _():
-        send_whole(stat2_ref, x_dq, x_dq_h, send)
         back[:T, :] = low_total[...].astype(BF16)
 
     @pl.when(jnp.logical_not(even))
     def _():
+        back[:T, :] = (low_total[...] + x_low[...]).astype(BF16)
         others = Queries(q2_ref, g2_ref, stat2_ref, theirs_low, stat_t)
-        others.high_keys(theirs_high, dq_h, high_total, True)
-        send_whole(stat2_ref, x_dq, dq_h, send)
-        back[:T, :] = (low_total[...] + x_low[...]).astype(BF16)
+        others.high_keys(theirs_high, send, high_total, True)
 
     back[T:, :] = high_total[...].astype(BF16)
 
@@ -332,7 +324,7 @@
     return jax.ShapeDtypeStruct(shape, dtype)
 
 
-def call(kernel, name, ins, outs, scratch=(), quadrants=0, from_hbm=0):
+def call(kernel, name, ins, outs, scratch=(), quadrants=0, from_hbm=0, aliases=None):
     size = sum(x.size * x.dtype.itemsize for x in list(ins) + list(outs))
     return pl.pallas_call(
         kernel,
@@ -340,6 +332,7 @@
         out_specs=[vmem()] * len(outs),
         out_shape=list(outs),
         scratch_shapes=list(scratch),
+        input_output_aliases=aliases or {},
         compiler_params=pltpu.CompilerParams(vmem_limit_bytes=24 << 20),
         cost_estimate=cost(quadrants, size),
         name=name,
@@ -362,7 +355,7 @@
         pltpu.with_memory_space_constraint(x, pltpu.HBM)
         for x in (q_in, k, v, o, g_in, log_total, positions)
     )
-    rows, half_rows = array((T, H * D), BF16), array((HALF, H * D), BF16)
+    rows = array((T, H * D), BF16)
     stat_t = pltpu.VMEM((T, 3 * H), F32)
     terms, half_terms = array((2 * T, D), F32), array((T, D), F32)
     low, high = call(
@@ -387,6 +380,7 @@
         (q_in, g_in, o, log_total, low),
         (rows, rows, array((3 * H, T), F32)),
         (pltpu.VMEM((T, H * D), BF16), pltpu.VMEM((H, T), F32), pltpu.SemaphoreType.DMA((2, 3))),
+        quadrants=30,
         from_hbm=4,
     )
     high, stat = lax.optimization_barrier((high, stat))
@@ -400,32 +394,33 @@
         (stat_t,),
         quadrants=1.5,
     )
-    x_dq, x_dq_h, x_low, x_high = call(
+    send, x_low, x_high = call(
         second_kernel,
         "second",
         (q2, g2, stat2, low, high, theirs_low),
-        (rows, half_rows, half_terms, half_terms),
+        (rows, half_terms, half_terms),
         (stat_t,),
         quadrants=2,
     )
-    theirs_high, x_dq = lax.optimization_barrier((theirs_high, x_dq))
-    keep_h, send, message_back = call(
+    theirs_high, send = lax.optimization_barrier((theirs_high, send))
+    keep, send, message_back = call(
         third_kernel,
         "third",
-        (q, g, stat, q2, g2, stat2, theirs_low, theirs_high, low_total, x_low, x_dq, x_dq_h),
-        (half_rows, rows, array((2 * T, D), BF16)),
-        (pltpu.VMEM((T, D), F32), pltpu.VMEM((HALF, H * D), BF16), stat_t),
+        (q, g, stat, q2, g2, stat2, theirs_low, theirs_high, low_total, x_low, keep, send),
+        (rows, rows, array((2 * T, D), BF16)),
+        (pltpu.VMEM((T, D), F32), stat_t),
         quadrants=0.5,
+        aliases={10: 0, 11: 1},
     )
     back = passed_along(message_back, -2)
     got = in_vmem(swapped(send))
     dq, own_low, own_high = call(
         own_kernel,
         "own",
-        (q, g, stat, low, high, keep, keep_h, x_low, x_high),
+        (q, g, stat, low, high, keep, x_low, x_high),
         (array((T, H * D), F32), half_terms, half_terms),
         (stat_t,),
-        quadrants=3,
+        quadrants=60,
     )
     (dq,) = call(query_kernel, "query_sum", (dq, got), (rows,))
     back, dq = lax.optimization_barrier((back, dq))

time: 33.5 us -> 31.3 us (0.934)
  waiting for transfers between devices: 5.58 us -> 3.37 us
  Pallas kernels: 16.6 us -> 15.8 us
  starting transfers between devices: 10.5 us -> 11.2 us
    ppermute x3, starting transfers between devices: 5.45 us -> 7.96 us  [passed_along(): return lax.ppermute(value, 'blk', pairs)]
    ppermute x3, waiting for transfers between devices: 5.57 us -> 3.36 us  [passed_along(): return lax.ppermute(value, 'blk', pairs)]
    ppermute x4, starting transfers between devices: 5.03 us -> 3.23 us  [swapped(): lax.ppermute(value, 'blk', [(source, source ^ 1) for source in range(coun...]
    pallas_call x8, Pallas kernels: 16.6 us -> 15.8 us  [call(): pl.pallas_call(kernel, in_specs=[hbm()] * from_hbm + [vmem()] * (len(ins)...]
  transfers between devices with their start and end apart: 7 -> 7, of which waited for: 2 -> 1; matrix products, arithmetic and copies ran while one was open for 0% -> 0% of each run, Pallas kernels for 38% -> 39%
where the time goes in v4:
time: 31.3 us; the launch traced here: 31.1 us
  Pallas kernels  15.8 us (50%)
  starting transfers between devices  11.2 us (36%)
  waiting for transfers between devices  3.37 us (11%)
  between operations  0.72 us (2%)
    pallas_call x8, Pallas kernels, call(): pl.pallas_call(kernel, in_specs=[hbm()] * from_hbm + [vmem()] * (len(ins)...  15.8 us
    ppermute x3, starting transfers between devices, passed_along(): return lax.ppermute(value, 'blk', pairs)  7.96 us
    ppermute x3, waiting for transfers between devices, passed_along(): return lax.ppermute(value, 'blk', pairs)  3.36 us
    ppermute x4, starting transfers between devices, swapped(): lax.ppermute(value, 'blk', [(source, source ^ 1) for source in range(coun...  3.23 us
  transfers between devices with their start and end apart: 7, of which 1 were waited for; matrix products, arithmetic and copies ran while one was open for 0% of the time, Pallas kernels for 39%

profile of v4, /device:TPU:1, one launch (start us, length us, event | category | flops | bytes accessed | tf_op | source)
XLA Modules:
  0.0 31.1 jit_solution(17995918919874869066)
XLA Ops:
  0.6 1.0 %pack.1 = (bf16[528,128]{1,0:T(8,128)(2,1)S(1)}, bf16[512,128]{1,0:T(8,128)(2,1)S(1)}) custom-call(bf16[512,128]{1,0:T(8,128)(2,1)} %k_hbm.1, bf16[512,128]{1,0:T(8,128)(2,1)} %v_hbm.1, s32[64]{0:T(128)} %pos_hbm.1), custom_call_target="tpu_custom_call" | custom-call | bytes 528640 | tf_op jit(solution)/shard_map/pack/pallas_call | solution.py:329
  1.6 3.7 %collective-permute-start.3 = (bf16[528,128]{1,0:T(8,128)(2,1)S(1)}, bf16[528,128]{1,0:T(8,128)(2,1)S(1)}, u32[]{:S(2)}, u32[]{:S(2)}) collective-permute-start(bf16[528,128]{1,0:T(8,128)(2,1)S(1)} %get-tuple-element.31.message.own_low.low_ref), channel_id=1, source_target_pairs={{0,16},{8,24},{16,32},{24,40},{32,48},{40,56},{48,64},{56,72},{64,... | collective-permute-start | bytes 405512 | tf_op jit(solution)/shard_map/ppermute | solution.py:345
  5.3 1.0 %collective-permute-start = (bf16[512,1024]{1,0:T(8,128)(2,1)}, bf16[512,1024]{1,0:T(8,128)(2,1)S(1)}, u32[]{:S(2)}, u32[]{:S(2)}) collective-permute-start(bf16[512,1024]{1,0:T(8,128)(2,1)} %q_hbm.1), channel_id=1, source_target_pairs={{0,8},{8,0},{16,24},{24,16},{32,40},{40,32},{48,56},{56,48},{64,72... | collective-permute-start | bytes 3145736 | tf_op jit(solution)/shard_map/ppermute | solution.py:350
  6.2 0.0 collective-permute-start.1
  6.3 2.1 %stat.1 = (bf16[512,1024]{1,0:T(8,128)(2,1)S(1)}, bf16[512,1024]{1,0:T(8,128)(2,1)S(1)}, f32[24,512]{1,0:T(8,128)S(1)}) custom-call(bf16[512,1024]{1,0:T(8,128)(2,1)} %q_hbm.1, bf16[512,1024]{1,0:T(8,128)(2,1)} %g_hbm.1, bf16[512,1024]{1,0:T(8,128)(2,1)} %o_hbm.1, f32[8,512]{1,0:T(8,128)} %l_hbm.1, bf16[528,128]{1,0:T(8,128)(2,1)S(1)} %get-tuple-element.31.message.own_low.low_ref), custom_call_target="tpu_custom_call" | custom-call | flops 20132659200 | bytes 5443584 | tf_op jit(solution)/shard_map/stat/pallas_call | solution.py:329
  8.4 0.6 %collective-permute-start.2 = (f32[24,512]{1,0:T(8,128)S(1)}, f32[24,512]{1,0:T(8,128)S(1)}, u32[]{:S(2)}, u32[]{:S(2)}) collective-permute-start(f32[24,512]{1,0:T(8,128)S(1)} %get-tuple-element.36.stat_ref), channel_id=1, source_target_pairs={{0,8},{8,0},{16,24},{24,16},{32,40},{40,32},{48,56},{56,48},{64,72... | collective-permute-start | bytes 147464 | tf_op jit(solution)/shard_map/ppermute | solution.py:350
  8.9 1.6 %collective-permute-start.4 = (bf16[512,128]{1,0:T(8,128)(2,1)S(1)}, bf16[512,128]{1,0:T(8,128)(2,1)S(1)}, u32[]{:S(2)}, u32[]{:S(2)}) collective-permute-start(bf16[512,128]{1,0:T(8,128)(2,1)S(1)} %get-tuple-element.39.own_high.high_ref), channel_id=1, source_target_pairs={{0,16},{8,24},{16,32},{24,40},{32,48},{40,56},{48,64},{56,72},{64,... | collective-permute-start | bytes 393224 | tf_op jit(solution)/shard_map/ppermute | solution.py:345
  10.5 3.4 %collective-permute-done.3.theirs_low = bf16[528,128]{1,0:T(8,128)(2,1)S(1)} collective-permute-done((bf16[528,128]{1,0:T(8,128)(2,1)S(1)}, bf16[528,128]{1,0:T(8,128)(2,1)S(1)}, u32[]{:S(2)}, u32[]{:S(2)}) %collective-permute-start.3) | collective-permute-done | bytes 135200 | tf_op jit(solution)/shard_map/ppermute | solution.py:345
  13.9 1.7 %first.1 = (bf16[512,1024]{1,0:T(8,128)(2,1)S(1)}, f32[512,128]{1,0:T(8,128)S(1)}) custom-call(bf16[512,1024]{1,0:T(8,128)(2,1)S(1)} %get-tuple-element.32.q_ref, bf16[512,1024]{1,0:T(8,128)(2,1)S(1)} %get-tuple-element.33.g_ref, f32[24,512]{1,0:T(8,128)S(1)} %get-tuple-element.36.stat_ref, bf16[528,128]{1,0:T(8,128)(2,1)S(1)} %collective-permute-done.3.theirs_low), custom_call_target="tpu_custom_call" | custom-call | flops 1006632960 | bytes 3592192 | tf_op jit(solution)/shard_map/first/pallas_call | solution.py:329
  15.6 0.0 collective-permute-done.2.stat2_ref
  15.6 0.0 collective-permute-done.q2_ref
  15.6 0.0 collective-permute-done.1.g2_ref
  15.6 3.1 %second.1 = (bf16[512,1024]{1,0:T(8,128)(2,1)S(1)}, f32[512,128]{1,0:T(8,128)S(1)}, f32[512,128]{1,0:T(8,128)S(1)}) custom-call(bf16[512,1024]{1,0:T(8,128)(2,1)S(1)} %collective-permute-done.q2_ref, bf16[512,1024]{1,0:T(8,128)(2,1)S(1)} %collective-permute-done.1.g2_ref, f32[24,512]{1,0:T(8,128)S(1)} %collective-permute-done.2.stat2_ref, ...), custom_call_target="tpu_custom_call" | custom-call | flops 1342177280 | bytes 4120576 | tf_op jit(solution)/shard_map/second/pallas_call | solution.py:329
  18.7 0.0 collective-permute-done.4.theirs_high
  18.7 1.9 %third.1 = (bf16[512,1024]{1,0:T(8,128)(2,1)S(1)}, bf16[512,1024]{1,0:T(8,128)(2,1)S(1)}, bf16[1024,128]{1,0:T(8,128)(2,1)S(1)}) custom-call(bf16[512,1024]{1,0:T(8,128)(2,1)S(1)} %get-tuple-element.32.q_ref, bf16[512,1024]{1,0:T(8,128)(2,1)S(1)} %get-tuple-element.33.g_ref, ...), custom_call_target="tpu_custom_call", output_to_operand_aliasing={{0}: (10, {}), {1}: (11, {})} | custom-call | flops 335544320 | bytes 9539584 | tf_op jit(solution)/shard_map/third/pallas_call | solution.py:329
  20.6 2.7 %collective-permute-start.5 = (bf16[1024,128]{1,0:T(8,128)(2,1)S(1)}, bf16[1024,128]{1,0:T(8,128)(2,1)S(1)}, u32[]{:S(2)}, u32[]{:S(2)}) collective-permute-start(bf16[1024,128]{1,0:T(8,128)(2,1)S(1)} %get-tuple-element.46), channel_id=1, source_target_pairs={{0,240},{8,248},{16,0},{24,8},{32,16},{40,24},{48,32},{56,40},{64,... | collective-permute-start | bytes 786440 | tf_op jit(solution)/shard_map/ppermute | solution.py:345
  23.3 1.7 %collective-permute-start.6 = (bf16[512,1024]{1,0:T(8,128)(2,1)S(1)}, bf16[512,1024]{1,0:T(8,128)(2,1)S(1)}, u32[]{:S(2)}, u32[]{:S(2)}) collective-permute-start(bf16[512,1024]{1,0:T(8,128)(2,1)S(1)} %get-tuple-element.50), channel_id=1, source_target_pairs={{0,8},{8,0},{16,24},{24,16},{32,40},{40,32},{48,56},{56,48},{64,72... | collective-permute-start | bytes 3145736 | tf_op jit(solution)/shard_map/ppermute | solution.py:350
  25.0 4.1 %own.1 = (f32[512,1024]{1,0:T(8,128)S(1)}, f32[512,128]{1,0:T(8,128)S(1)}, f32[512,128]{1,0:T(8,128)S(1)}) custom-call(bf16[512,1024]{1,0:T(8,128)(2,1)S(1)} %get-tuple-element.32.q_ref, bf16[512,1024]{1,0:T(8,128)(2,1)S(1)} %get-tuple-element.33.g_ref, f32[24,512]{1,0:T(8,128)S(1)} %get-tuple-element.36.stat_ref, ...), custom_call_target="tpu_custom_call" | custom-call | flops 40265318400 | bytes 6606848 | tf_op jit(solution)/shard_map/own/pallas_call | solution.py:329
  29.1 0.0 collective-permute-done.6.got_ref
  29.1 1.2 %query_sum.1 = bf16[512,1024]{1,0:T(8,128)(2,1)} custom-call(f32[512,1024]{1,0:T(8,128)S(1)} %get-tuple-element.49.dq_ref, bf16[512,1024]{1,0:T(8,128)(2,1)S(1)} %collective-permute-done.6.got_ref), custom_call_target="tpu_custom_call" | custom-call | bytes 4194304 | tf_op jit(solution)/shard_map/query_sum/pallas_call | solution.py:329
  30.3 0.0 collective-permute-done.5.got_ref
  30.3 0.8 %key_sum.1 = (bf16[512,128]{1,0:T(8,128)(2,1)}, bf16[512,128]{1,0:T(8,128)(2,1)}) custom-call(bf16[528,128]{1,0:T(8,128)(2,1)S(1)} %get-tuple-element.31.message.own_low.low_ref, f32[512,128]{1,0:T(8,128)S(1)} %get-tuple-element.52.low_total, f32[512,128]{1,0:T(8,128)S(1)} %get-tuple-element.53.high_total, bf16[1024,128]{1,0:T(8,128)(2,1)S(1)} %collective-permute-done.5.got_ref), custom_call_target="tpu_custom_call" | custom-call | bytes 1183744 | tf_op jit(solution)/shard_map/key_sum/pallas_call | solution.py:329
Async XLA Ops:
  1.6 12.3 %collective-permute-start.3 = (bf16[528,128]{1,0:T(8,128)(2,1)S(1)}, bf16[528,128]{1,0:T(8,128)(2,1)S(1)}, u32[]{:S(2)}, u32[]{:S(2)}) collective-permute-start(bf16[528,128]{1,0:T(8,128)(2,1)S(1)} %get-tuple-element.31.message.own_low.low_ref), channel_id=1, source_target_pairs={{0,16},{8,24},{16,32},{24,40},{32,48},{40,56},{48,64},{56,72},{64,... | collective-permute-start | bytes 405512 | tf_op jit(solution)/shard_map/ppermute | solution.py:345
  5.3 10.3 %collective-permute-start = (bf16[512,1024]{1,0:T(8,128)(2,1)}, bf16[512,1024]{1,0:T(8,128)(2,1)S(1)}, u32[]{:S(2)}, u32[]{:S(2)}) collective-permute-start(bf16[512,1024]{1,0:T(8,128)(2,1)} %q_hbm.1), channel_id=1, source_target_pairs={{0,8},{8,0},{16,24},{24,16},{32,40},{40,32},{48,56},{56,48},{64,72... | collective-permute-start | bytes 3145736 | tf_op jit(solution)/shard_map/ppermute | solution.py:350
  6.2 9.3 %collective-permute-start.1 = (bf16[512,1024]{1,0:T(8,128)(2,1)}, bf16[512,1024]{1,0:T(8,128)(2,1)S(1)}, u32[]{:S(2)}, u32[]{:S(2)}) collective-permute-start(bf16[512,1024]{1,0:T(8,128)(2,1)} %g_hbm.1), channel_id=1, source_target_pairs={{0,8},{8,0},{16,24},{24,16},{32,40},{40,32},{48,56},{56,48},{64,72... | collective-permute-start | bytes 3145736 | tf_op jit(solution)/shard_map/ppermute | solution.py:350
  8.4 7.2 %collective-permute-start.2 = (f32[24,512]{1,0:T(8,128)S(1)}, f32[24,512]{1,0:T(8,128)S(1)}, u32[]{:S(2)}, u32[]{:S(2)}) collective-permute-start(f32[24,512]{1,0:T(8,128)S(1)} %get-tuple-element.36.stat_ref), channel_id=1, source_target_pairs={{0,8},{8,0},{16,24},{24,16},{32,40},{40,32},{48,56},{56,48},{64,72... | collective-permute-start | bytes 147464 | tf_op jit(solution)/shard_map/ppermute | solution.py:350
  8.9 9.8 %collective-permute-start.4 = (bf16[512,128]{1,0:T(8,128)(2,1)S(1)}, bf16[512,128]{1,0:T(8,128)(2,1)S(1)}, u32[]{:S(2)}, u32[]{:S(2)}) collective-permute-start(bf16[512,128]{1,0:T(8,128)(2,1)S(1)} %get-tuple-element.39.own_high.high_ref), channel_id=1, source_target_pairs={{0,16},{8,24},{16,32},{24,40},{32,48},{40,56},{48,64},{56,72},{64,... | collective-permute-start | bytes 393224 | tf_op jit(solution)/shard_map/ppermute | solution.py:345
  20.6 9.7 %collective-permute-start.5 = (bf16[1024,128]{1,0:T(8,128)(2,1)S(1)}, bf16[1024,128]{1,0:T(8,128)(2,1)S(1)}, u32[]{:S(2)}, u32[]{:S(2)}) collective-permute-start(bf16[1024,128]{1,0:T(8,128)(2,1)S(1)} %get-tuple-element.46), channel_id=1, source_target_pairs={{0,240},{8,248},{16,0},{24,8},{32,16},{40,24},{48,32},{56,40},{64,... | collective-permute-start | bytes 786440 | tf_op jit(solution)/shard_map/ppermute | solution.py:345
  23.3 5.8 %collective-permute-start.6 = (bf16[512,1024]{1,0:T(8,128)(2,1)S(1)}, bf16[512,1024]{1,0:T(8,128)(2,1)S(1)}, u32[]{:S(2)}, u32[]{:S(2)}) collective-permute-start(bf16[512,1024]{1,0:T(8,128)(2,1)S(1)} %get-tuple-element.50), channel_id=1, source_target_pairs={{0,8},{8,0},{16,24},{24,16},{32,40},{40,32},{48,56},{56,48},{64,72... | collective-permute-start | bytes 3145736 | tf_op jit(solution)/shard_map/ppermute | solution.py:350

commit v5 on v4

--- a/solution.py
+++ b/solution.py
@@ -11,6 +11,7 @@
 D = 128
 H = 8
 T = 512
+STEPS = 2
 HALF = T // 2
 PIECES = 64
 IDS = 16
@@ -122,8 +123,7 @@
     load_q.wait()
 
 
-def own_kernel(q_ref, g_ref, stat_ref, low_ref, high_ref, keep_ref, x_low, x_high, dq_ref, low_total, high_total, stat_t):
-    transposed_stat(stat_ref, stat_t)
+def own_half(h0, q_ref, g_ref, stat_t, low_ref, high_ref, dq_ref, low_total, high_total):
     ql = low_row(piece_of(low_ref))
     qh = pl.multiple_of(HALF - ql, HALF)
     mask = lax.broadcasted_iota(jnp.int32, (HALF, HALF), 1) <= lax.broadcasted_iota(
@@ -131,42 +131,64 @@
     )
     kl, vl = low_ref[:HALF, :], low_ref[HALF:T, :]
     kh, vh = high_ref[:HALF, :], high_ref[HALF:, :]
-    sums = None
-    for h0 in (0, GROUP):
-        heads = [slice(h * D, (h + 1) * D) for h in range(h0, h0 + GROUP)]
-        q0, q1 = ([q_ref[pl.ds(rows, HALF), cols] for cols in heads] for rows in (ql, qh))
-        g0, g1 = ([g_ref[pl.ds(rows, HALF), cols] for cols in heads] for rows in (ql, qh))
-        scores_l, grads_l = products(q0 + q1, kl.T), products(g0 + g1, vl.T)
-        scores_h, grads_h = products(q1, kh.T), products(g1, vh.T)
-        p_l, d_l, p_h, d_h = [], [], [], []
-        for n in range(2 * GROUP):
-            rows, masked = (ql, mask) if n < GROUP else (qh, None)
-            stat = stat_of(stat_t, rows, h0 + n % GROUP)
-            p, d = weights_of(scores_l[n], grads_l[n], *stat, masked)
-            p_l, d_l = p_l + [p], d_l + [d]
-        for n in range(GROUP):
-            p, d = weights_of(scores_h[n], grads_h[n], *stat_of(stat_t, qh, h0 + n), mask)
-            p_h, d_h = p_h + [p], d_h + [d]
-        lows = products(d_l[:GROUP], kl)
-        highs = products(
-            [jnp.concatenate([d_l[GROUP + n], d_h[n]], 1) for n in range(GROUP)],
-            jnp.concatenate([kl, kh], 0),
-        )
-        for n, cols in enumerate(heads):
-            dq_ref[pl.ds(ql, HALF), cols] = keep_ref[pl.ds(ql, HALF), cols].astype(F32) + lows[n]
-            kept = keep_ref[pl.ds(qh, HALF), cols].astype(F32)
-            dq_ref[pl.ds(qh, HALF), cols] = kept + highs[n]
-        g0_t, g1_t = cat([g.T for g in g0], 1), cat([g.T for g in g1], 1)
-        q0_t, q1_t = cat([q.T for q in q0], 1), cat([q.T for q in q1], 1)
-        dv_l, dv_h = dot(cat([g0_t, g1_t], 1), cat(p_l, 0)), dot(g1_t, cat(p_h, 0))
-        dk_l, dk_h = dot(cat([q0_t, q1_t], 1), cat(d_l, 0)), dot(q1_t, cat(d_h, 0))
-        part = (dk_l, dv_l, dk_h, dv_h)
-        sums = part if sums is None else tuple(x + y for x, y in zip(sums, part))
-    dk_l, dv_l, dk_h, dv_h = sums
-    even = is_even()
-    for total, more, dk, dv in ((low_total, x_low, dk_l, dv_l), (high_total, x_high, dk_h, dv_h)):
-        total[:HALF, :] = (dk * SCALE).T + jnp.where(even, more[:HALF, :], 0.0)
-        total[HALF:, :] = dv.T + jnp.where(even, more[HALF:, :], 0.0)
+    heads = [slice(h * D, (h + 1) * D) for h in range(h0, h0 + GROUP)]
+    q0, q1 = ([q_ref[pl.ds(rows, HALF), cols] for cols in heads] for rows in (ql, qh))
+    g0, g1 = ([g_ref[pl.ds(rows, HALF), cols] for cols in heads] for rows in (ql, qh))
+    scores_l, grads_l = products(q0 + q1, kl.T), products(g0 + g1, vl.T)
+    scores_h, grads_h = products(q1, kh.T), products(g1, vh.T)
+    p_l, d_l, p_h, d_h = [], [], [], []
+    for n in range(2 * GROUP):
+        rows, masked = (ql, mask) if n < GROUP else (qh, None)
+        stat = stat_of(stat_t, rows, h0 + n % GROUP)
+        p, d = weights_of(scores_l[n], grads_l[n], *stat, masked)
+        p_l, d_l = p_l + [p], d_l + [d]
+    for n in range(GROUP):
+        p, d = weights_of(scores_h[n], grads_h[n], *stat_of(stat_t, qh, h0 + n), mask)
+        p_h, d_h = p_h + [p], d_h + [d]
+    lows = products(d_l[:GROUP], kl)
+    highs = products(
+        [jnp.concatenate([d_l[GROUP + n], d_h[n]], 1) for n in range(GROUP)],
+        jnp.concatenate([kl, kh], 0),
+    )
+    for n, cols in enumerate(heads):
+        dq_ref[pl.ds(ql, HALF), cols] = lows[n]
+        dq_ref[pl.ds(qh, HALF), cols] = highs[n]
+    g0_t, g1_t = cat([g.T for g in g0], 1), cat([g.T for g in g1], 1)
+    q0_t, q1_t = cat([q.T for q in q0], 1), cat([q.T for q in q1], 1)
+    dv_l, dv_h = dot(cat([g0_t, g1_t], 1), cat(p_l, 0)), dot(g1_t, cat(p_h, 0))
+    dk_l, dk_h = dot(cat([q0_t, q1_t], 1), cat(d_l, 0)), dot(q1_t, cat(d_h, 0))
+    for total, dk, dv in ((low_total, dk_l, dv_l), (high_total, dk_h, dv_h)):
+        total[:HALF, :] += (dk * SCALE).T
+        total[HALF:, :] += dv.T
+
+
+def waits_long():
+    return lax.axis_index("blk") < STEPS
+
+
+def own_ahead_kernel(q_ref, g_ref, stat_ref, low_ref, high_ref, dq_ref, low_total, high_total, stat_t):
+    low_total[...] = jnp.zeros((T, D), F32)
+    high_total[...] = jnp.zeros((T, D), F32)
+
+    @pl.when(waits_long())
+    def _():
+        transposed_stat(stat_ref, stat_t)
+        own_half(0, q_ref, g_ref, stat_t, low_ref, high_ref, dq_ref, low_total, high_total)
+
+
+def own_kernel(q_ref, g_ref, stat_ref, low_ref, high_ref, x_low, x_high, _, __, ___, dq_ref, low_total, high_total, stat_t):
+    transposed_stat(stat_ref, stat_t)
+
+    @pl.when(jnp.logical_not(waits_long()))
+    def _():
+        own_half(0, q_ref, g_ref, stat_t, low_ref, high_ref, dq_ref, low_total, high_total)
+
+    own_half(GROUP, q_ref, g_ref, stat_t, low_ref, high_ref, dq_ref, low_total, high_total)
+
+    @pl.when(is_even())
+    def _():
+        low_total[...] += x_low[...]
+        high_total[...] += x_high[...]
 
 
 class Queries:
@@ -234,26 +256,22 @@
     return lax.axis_index("blk") % 2 == 0
 
 
-def first_kernel(q_ref, g_ref, stat_ref, theirs_low, dq_ref, low_total, stat_t):
-    queries = Queries(q_ref, g_ref, stat_ref, theirs_low, stat_t)
-    queries.low_keys(theirs_low, dq_ref, low_total)
-
-
-def second_kernel(q2_ref, g2_ref, stat2_ref, own_low, own_high, theirs_low, dq_ref, x_low, x_high, stat_t):
+def low_kernel(q_ref, g_ref, stat_ref, q2_ref, g2_ref, stat2_ref, own_low, own_high, theirs_low, keep, send, low_total, x_low, x_high, stat_t):
+    Queries(q_ref, g_ref, stat_ref, theirs_low, stat_t).low_keys(theirs_low, keep, low_total)
     even = is_even()
 
     @pl.when(even)
     def _():
         queries = Queries(q2_ref, g2_ref, stat2_ref, own_low, stat_t)
-        queries.low_keys(own_low, dq_ref, x_low)
-        queries.high_keys(own_high, dq_ref, x_high, False)
+        queries.low_keys(own_low, send, x_low)
+        queries.high_keys(own_high, send, x_high, False)
 
     @pl.when(jnp.logical_not(even))
     def _():
-        Queries(q2_ref, g2_ref, stat2_ref, theirs_low, stat_t).low_keys(theirs_low, dq_ref, x_low)
-
-
-def third_kernel(q_ref, g_ref, stat_ref, q2_ref, g2_ref, stat2_ref, theirs_low, theirs_high, low_total, x_low, _, __, keep, send, back, high_total, stat_t):
+        Queries(q2_ref, g2_ref, stat2_ref, theirs_low, stat_t).low_keys(theirs_low, send, x_low)
+
+
+def high_kernel(q_ref, g_ref, stat_ref, q2_ref, g2_ref, stat2_ref, theirs_low, theirs_high, low_total, x_low, _, __, keep, send, back, high_total, stat_t):
     even = is_even()
     Queries(q_ref, g_ref, stat_ref, theirs_low, stat_t).high_keys(
         theirs_high, keep, high_total, False
@@ -272,8 +290,16 @@
     back[T:, :] = high_total[...].astype(BF16)
 
 
-def query_kernel(dq_ref, got_ref, out_ref):
-    out_ref[...] = ((dq_ref[...] + got_ref[...].astype(F32)) * SCALE).astype(BF16)
+def query_kernel(dq_ref, keep_ref, got_ref, out_hbm, out_ref, sems):
+    copies = []
+    for n in range(4):
+        rows = pl.ds(n * T // 4, T // 4)
+        total = dq_ref[rows, :] + keep_ref[rows, :].astype(F32) + got_ref[rows, :].astype(F32)
+        out_ref[rows, :] = (total * SCALE).astype(BF16)
+        copies.append(pltpu.make_async_copy(out_ref.at[rows, :], out_hbm.at[rows, :], sems.at[n]))
+        copies[n].start()
+    for copy in copies:
+        copy.wait()
 
 
 def key_kernel(own_low, low_total, high_total, got_ref, dk_ref, dv_ref):
@@ -324,12 +350,12 @@
     return jax.ShapeDtypeStruct(shape, dtype)
 
 
-def call(kernel, name, ins, outs, scratch=(), quadrants=0, from_hbm=0, aliases=None):
+def call(kernel, name, ins, outs, scratch=(), quadrants=0, from_hbm=0, to_hbm=0, aliases=None):
     size = sum(x.size * x.dtype.itemsize for x in list(ins) + list(outs))
     return pl.pallas_call(
         kernel,
         in_specs=[hbm()] * from_hbm + [vmem()] * (len(ins) - from_hbm),
-        out_specs=[vmem()] * len(outs),
+        out_specs=[hbm()] * to_hbm + [vmem()] * (len(outs) - to_hbm),
         out_shape=list(outs),
         scratch_shapes=list(scratch),
         input_output_aliases=aliases or {},
@@ -386,26 +412,27 @@
     high, stat = lax.optimization_barrier((high, stat))
     theirs_high = in_vmem(passed_along(high, 2))
     stat2 = in_vmem(swapped(stat))
-    keep, low_total = call(
-        first_kernel,
-        "first",
-        (q, g, stat, theirs_low),
-        (rows, half_terms),
+    own_out = (array((T, H * D), F32), half_terms, half_terms)
+    dq, own_low, own_high = call(
+        own_ahead_kernel,
+        "own_ahead",
+        (q, g, stat, low, high),
+        own_out,
         (stat_t,),
-        quadrants=1.5,
-    )
-    send, x_low, x_high = call(
-        second_kernel,
-        "second",
-        (q2, g2, stat2, low, high, theirs_low),
-        (rows, half_terms, half_terms),
+    )
+    theirs_low, dq = lax.optimization_barrier((theirs_low, dq))
+    keep, send, low_total, x_low, x_high = call(
+        low_kernel,
+        "low_keys",
+        (q, g, stat, q2, g2, stat2, low, high, theirs_low),
+        (rows, rows, half_terms, half_terms, half_terms),
         (stat_t,),
-        quadrants=2,
+        quadrants=3.5,
     )
     theirs_high, send = lax.optimization_barrier((theirs_high, send))
     keep, send, message_back = call(
-        third_kernel,
-        "third",
+        high_kernel,
+        "high_keys",
         (q, g, stat, q2, g2, stat2, theirs_low, theirs_high, low_total, x_low, keep, send),
         (rows, rows, array((2 * T, D), BF16)),
         (pltpu.VMEM((T, D), F32), stat_t),
@@ -417,12 +444,20 @@
     dq, own_low, own_high = call(
         own_kernel,
         "own",
-        (q, g, stat, low, high, keep, x_low, x_high),
-        (array((T, H * D), F32), half_terms, half_terms),
+        (q, g, stat, low, high, x_low, x_high, dq, own_low, own_high),
+        own_out,
         (stat_t,),
         quadrants=60,
-    )
-    (dq,) = call(query_kernel, "query_sum", (dq, got), (rows,))
+        aliases={7: 0, 8: 1, 9: 2},
+    )
+    (dq,) = call(
+        query_kernel,
+        "query_sum",
+        (dq, keep, got),
+        (rows,),
+        (pltpu.VMEM((T, H * D), BF16), pltpu.SemaphoreType.DMA((4,))),
+        to_hbm=1,
+    )
     back, dq = lax.optimization_barrier((back, dq))
     dk, dv = call(
         key_kernel, "key_sum", (low, own_low, own_high, back), (array((T, D), BF16),) * 2

time: 31.3 us -> 30.7 us (0.981)
  waiting for transfers between devices: 3.37 us -> 2.02 us
  Pallas kernels: 15.8 us -> 16.9 us
  starting transfers between devices: 11.2 us -> 10.8 us
    ppermute x3, waiting for transfers between devices: 3.36 us -> 2.01 us  [passed_along(): return lax.ppermute(value, 'blk', pairs)]
    pallas_call x8, Pallas kernels: 15.8 us -> 16.9 us  [call(): pl.pallas_call(kernel, in_specs=[hbm()] * from_hbm + [vmem()] * (len(ins)...]
    ppermute x3, starting transfers between devices: 7.96 us -> 7.24 us  [passed_along(): return lax.ppermute(value, 'blk', pairs)]
  transfers between devices with their start and end apart: 7 -> 7, of which waited for: 1 -> 3; matrix products, arithmetic and copies ran while one was open for 0% -> 0% of each run, Pallas kernels for 39% -> 39%
where the time goes in v5:
time: 30.7 us; the launch traced here: 30.4 us
  Pallas kernels  16.9 us (55%)
  starting transfers between devices  10.8 us (35%)
  waiting for transfers between devices  2.02 us (7%)
  between operations  0.71 us (2%)
    pallas_call x8, Pallas kernels, call(): pl.pallas_call(kernel, in_specs=[hbm()] * from_hbm + [vmem()] * (len(ins)...  16.9 us
    ppermute x3, starting transfers between devices, passed_along(): return lax.ppermute(value, 'blk', pairs)  7.24 us
    ppermute x4, starting transfers between devices, swapped(): lax.ppermute(value, 'blk', [(source, source ^ 1) for source in range(coun...  3.52 us
    ppermute x3, waiting for transfers between devices, passed_along(): return lax.ppermute(value, 'blk', pairs)  2.01 us
  transfers between devices with their start and end apart: 7, of which 3 were waited for; matrix products, arithmetic and copies ran while one was open for 0% of the time, Pallas kernels for 39%

profile of v5, /device:TPU:1, one launch (start us, length us, event | category | flops | bytes accessed | tf_op | source)
XLA Modules:
  0.0 30.4 jit_solution(8970723260584488099)
XLA Ops:
  0.6 1.0 %pack.1 = (bf16[528,128]{1,0:T(8,128)(2,1)S(1)}, bf16[512,128]{1,0:T(8,128)(2,1)S(1)}) custom-call(bf16[512,128]{1,0:T(8,128)(2,1)} %k_hbm.1, bf16[512,128]{1,0:T(8,128)(2,1)} %v_hbm.1, s32[64]{0:T(128)} %pos_hbm.1), custom_call_target="tpu_custom_call" | custom-call | bytes 528640 | tf_op jit(solution)/shard_map/pack/pallas_call | solution.py:355
  1.6 3.7 %collective-permute-start.3 = (bf16[528,128]{1,0:T(8,128)(2,1)S(1)}, bf16[528,128]{1,0:T(8,128)(2,1)S(1)}, u32[]{:S(2)}, u32[]{:S(2)}) collective-permute-start(bf16[528,128]{1,0:T(8,128)(2,1)S(1)} %get-tuple-element.36.message.low_ref.own_low), channel_id=1, source_target_pairs={{0,16},{8,24},{16,32},{24,40},{32,48},{40,56},{48,64},{56,72},{64,... | collective-permute-start | bytes 405512 | tf_op jit(solution)/shard_map/ppermute | solution.py:371
  5.3 1.0 %collective-permute-start = (bf16[512,1024]{1,0:T(8,128)(2,1)}, bf16[512,1024]{1,0:T(8,128)(2,1)S(1)}, u32[]{:S(2)}, u32[]{:S(2)}) collective-permute-start(bf16[512,1024]{1,0:T(8,128)(2,1)} %q_hbm.1), channel_id=1, source_target_pairs={{0,8},{8,0},{16,24},{24,16},{32,40},{40,32},{48,56},{56,48},{64,72... | collective-permute-start | bytes 3145736 | tf_op jit(solution)/shard_map/ppermute | solution.py:376
  6.2 0.0 collective-permute-start.1
  6.3 2.1 %stat.1 = (bf16[512,1024]{1,0:T(8,128)(2,1)S(1)}, bf16[512,1024]{1,0:T(8,128)(2,1)S(1)}, f32[24,512]{1,0:T(8,128)S(1)}) custom-call(bf16[512,1024]{1,0:T(8,128)(2,1)} %q_hbm.1, bf16[512,1024]{1,0:T(8,128)(2,1)} %g_hbm.1, bf16[512,1024]{1,0:T(8,128)(2,1)} %o_hbm.1, f32[8,512]{1,0:T(8,128)} %l_hbm.1, bf16[528,128]{1,0:T(8,128)(2,1)S(1)} %get-tuple-element.36.message.low_ref.own_low), custom_call_target="tpu_custom_call" | custom-call | flops 20132659200 | bytes 5443584 | tf_op jit(solution)/shard_map/stat/pallas_call | solution.py:355
  8.4 0.6 %collective-permute-start.2 = (f32[24,512]{1,0:T(8,128)S(1)}, f32[24,512]{1,0:T(8,128)S(1)}, u32[]{:S(2)}, u32[]{:S(2)}) collective-permute-start(f32[24,512]{1,0:T(8,128)S(1)} %get-tuple-element.41.stat_ref), channel_id=1, source_target_pairs={{0,8},{8,0},{16,24},{24,16},{32,40},{40,32},{48,56},{56,48},{64,72... | collective-permute-start | bytes 147464 | tf_op jit(solution)/shard_map/ppermute | solution.py:376
  8.9 1.6 %collective-permute-start.4 = (bf16[512,128]{1,0:T(8,128)(2,1)S(1)}, bf16[512,128]{1,0:T(8,128)(2,1)S(1)}, u32[]{:S(2)}, u32[]{:S(2)}) collective-permute-start(bf16[512,128]{1,0:T(8,128)(2,1)S(1)} %get-tuple-element.44.high_ref.own_high), channel_id=1, source_target_pairs={{0,16},{8,24},{16,32},{24,40},{32,48},{40,56},{48,64},{56,72},{64,... | collective-permute-start | bytes 393224 | tf_op jit(solution)/shard_map/ppermute | solution.py:371
  10.5 2.3 %own_ahead.1 = (f32[512,1024]{1,0:T(8,128)S(1)}, f32[512,128]{1,0:T(8,128)S(1)}, f32[512,128]{1,0:T(8,128)S(1)}) custom-call(bf16[512,1024]{1,0:T(8,128)(2,1)S(1)} %get-tuple-element.37.q_ref, bf16[512,1024]{1,0:T(8,128)(2,1)S(1)} %get-tuple-element.38.g_ref, f32[24,512]{1,0:T(8,128)S(1)} %get-tuple-element.41.stat_ref, ...), custom_call_target="tpu_custom_call" | custom-call | bytes 5033984 | tf_op jit(solution)/shard_map/own_ahead/pallas_call | solution.py:355
  12.9 1.0 %collective-permute-done.3.theirs_low = bf16[528,128]{1,0:T(8,128)(2,1)S(1)} collective-permute-done((bf16[528,128]{1,0:T(8,128)(2,1)S(1)}, bf16[528,128]{1,0:T(8,128)(2,1)S(1)}, u32[]{:S(2)}, u32[]{:S(2)}) %collective-permute-start.3) | collective-permute-done | bytes 135200 | tf_op jit(solution)/shard_map/ppermute | solution.py:371
  13.9 0.0 collective-permute-done.2.stat2_ref
  13.9 0.0 collective-permute-done.q2_ref
  13.9 0.0 collective-permute-done.1.g2_ref
  13.9 3.6 %low_keys.1 = (bf16[512,1024]{1,0:T(8,128)(2,1)S(1)}, bf16[512,1024]{1,0:T(8,128)(2,1)S(1)}, f32[512,128]{1,0:T(8,128)S(1)}, f32[512,128]{1,0:T(8,128)S(1)}, f32[512,128]{1,0:T(8,128)S(1)}) custom-call(bf16[512,1024]{1,0:T(8,128)(2,1)S(1)} %get-tuple-element.37.q_ref, bf16[512,1024]{1,0:T(8,128)(2,1)S(1)} %get-tuple-element.38.g_ref, ...), custom_call_target="tpu_custom_call" | custom-call | flops 2348810240 | bytes 7577600 | tf_op jit(solution)/shard_map/low_keys/pallas_call | solution.py:355
  17.5 0.2 collective-permute-done.4.theirs_high
  17.7 3.3 %high_keys.1 = (bf16[512,1024]{1,0:T(8,128)(2,1)S(1)}, bf16[512,1024]{1,0:T(8,128)(2,1)S(1)}, bf16[1024,128]{1,0:T(8,128)(2,1)S(1)}) custom-call(bf16[512,1024]{1,0:T(8,128)(2,1)S(1)} %get-tuple-element.37.q_ref, bf16[512,1024]{1,0:T(8,128)(2,1)S(1)} %get-tuple-element.38.g_ref, ...), custom_call_target="tpu_custom_call", output_to_operand_aliasing={{0}: (10, {}), {1}: (11, {})} | custom-call | flops 335544320 | bytes 9539584 | tf_op jit(solution)/shard_map/high_keys/pallas_call | solution.py:355
  21.0 2.0 %collective-permute-start.5 = (bf16[1024,128]{1,0:T(8,128)(2,1)S(1)}, bf16[1024,128]{1,0:T(8,128)(2,1)S(1)}, u32[]{:S(2)}, u32[]{:S(2)}) collective-permute-start(bf16[1024,128]{1,0:T(8,128)(2,1)S(1)} %get-tuple-element.53), channel_id=1, source_target_pairs={{0,240},{8,248},{16,0},{24,8},{32,16},{40,24},{48,32},{56,40},{64,... | collective-permute-start | bytes 786440 | tf_op jit(solution)/shard_map/ppermute | solution.py:371
  23.0 2.0 %collective-permute-start.6 = (bf16[512,1024]{1,0:T(8,128)(2,1)S(1)}, bf16[512,1024]{1,0:T(8,128)(2,1)S(1)}, u32[]{:S(2)}, u32[]{:S(2)}) collective-permute-start(bf16[512,1024]{1,0:T(8,128)(2,1)S(1)} %get-tuple-element.60), channel_id=1, source_target_pairs={{0,8},{8,0},{16,24},{24,16},{32,40},{40,32},{48,56},{56,48},{64,72... | collective-permute-start | bytes 3145736 | tf_op jit(solution)/shard_map/ppermute | solution.py:376
  25.0 2.6 %own.1 = (f32[512,1024]{1,0:T(8,128)S(1)}, f32[512,128]{1,0:T(8,128)S(1)}, f32[512,128]{1,0:T(8,128)S(1)}) custom-call(bf16[512,1024]{1,0:T(8,128)(2,1)S(1)} %get-tuple-element.37.q_ref, bf16[512,1024]{1,0:T(8,128)(2,1)S(1)} %get-tuple-element.38.g_ref, ...), custom_call_target="tpu_custom_call", output_to_operand_aliasing={{0}: (7, {}), {1}: (8, {}), {2}: (9, {})} | custom-call | flops 40265318400 | bytes 8179712 | tf_op jit(solution)/shard_map/own/pallas_call | solution.py:355
  27.6 0.0 collective-permute-done.6.got_ref
  27.6 1.1 %query_sum.1 = bf16[512,1024]{1,0:T(8,128)(2,1)} custom-call(f32[512,1024]{1,0:T(8,128)S(1)} %get-tuple-element.58.dq_ref, bf16[512,1024]{1,0:T(8,128)(2,1)S(1)} %get-tuple-element.59.keep_ref, bf16[512,1024]{1,0:T(8,128)(2,1)S(1)} %collective-permute-done.6.got_ref), custom_call_target="tpu_custom_call" | custom-call | bytes 5242880 | tf_op jit(solution)/shard_map/query_sum/pallas_call | solution.py:355
  28.8 0.8 %collective-permute-done.5.got_ref = bf16[1024,128]{1,0:T(8,128)(2,1)S(1)} collective-permute-done((bf16[1024,128]{1,0:T(8,128)(2,1)S(1)}, bf16[1024,128]{1,0:T(8,128)(2,1)S(1)}, u32[]{:S(2)}, u32[]{:S(2)}) %collective-permute-start.5) | collective-permute-done | bytes 262176 | tf_op jit(solution)/shard_map/ppermute | solution.py:371
  29.6 0.8 %key_sum.1 = (bf16[512,128]{1,0:T(8,128)(2,1)}, bf16[512,128]{1,0:T(8,128)(2,1)}) custom-call(bf16[528,128]{1,0:T(8,128)(2,1)S(1)} %get-tuple-element.36.message.low_ref.own_low, f32[512,128]{1,0:T(8,128)S(1)} %get-tuple-element.62.low_total, f32[512,128]{1,0:T(8,128)S(1)} %get-tuple-element.63.high_total, bf16[1024,128]{1,0:T(8,128)(2,1)S(1)} %collective-permute-done.5.got_ref), custom_call_target="tpu_custom_call" | custom-call | bytes 1183744 | tf_op jit(solution)/shard_map/key_sum/pallas_call | solution.py:355
Async XLA Ops:
  1.6 12.3 %collective-permute-start.3 = (bf16[528,128]{1,0:T(8,128)(2,1)S(1)}, bf16[528,128]{1,0:T(8,128)(2,1)S(1)}, u32[]{:S(2)}, u32[]{:S(2)}) collective-permute-start(bf16[528,128]{1,0:T(8,128)(2,1)S(1)} %get-tuple-element.36.message.low_ref.own_low), channel_id=1, source_target_pairs={{0,16},{8,24},{16,32},{24,40},{32,48},{40,56},{48,64},{56,72},{64,... | collective-permute-start | bytes 405512 | tf_op jit(solution)/shard_map/ppermute | solution.py:371
  5.3 8.6 %collective-permute-start = (bf16[512,1024]{1,0:T(8,128)(2,1)}, bf16[512,1024]{1,0:T(8,128)(2,1)S(1)}, u32[]{:S(2)}, u32[]{:S(2)}) collective-permute-start(bf16[512,1024]{1,0:T(8,128)(2,1)} %q_hbm.1), channel_id=1, source_target_pairs={{0,8},{8,0},{16,24},{24,16},{32,40},{40,32},{48,56},{56,48},{64,72... | collective-permute-start | bytes 3145736 | tf_op jit(solution)/shard_map/ppermute | solution.py:376
  6.2 7.7 %collective-permute-start.1 = (bf16[512,1024]{1,0:T(8,128)(2,1)}, bf16[512,1024]{1,0:T(8,128)(2,1)S(1)}, u32[]{:S(2)}, u32[]{:S(2)}) collective-permute-start(bf16[512,1024]{1,0:T(8,128)(2,1)} %g_hbm.1), channel_id=1, source_target_pairs={{0,8},{8,0},{16,24},{24,16},{32,40},{40,32},{48,56},{56,48},{64,72... | collective-permute-start | bytes 3145736 | tf_op jit(solution)/shard_map/ppermute | solution.py:376
  8.4 5.5 %collective-permute-start.2 = (f32[24,512]{1,0:T(8,128)S(1)}, f32[24,512]{1,0:T(8,128)S(1)}, u32[]{:S(2)}, u32[]{:S(2)}) collective-permute-start(f32[24,512]{1,0:T(8,128)S(1)} %get-tuple-element.41.stat_ref), channel_id=1, source_target_pairs={{0,8},{8,0},{16,24},{24,16},{32,40},{40,32},{48,56},{56,48},{64,72... | collective-permute-start | bytes 147464 | tf_op jit(solution)/shard_map/ppermute | solution.py:376
  8.9 8.7 %collective-permute-start.4 = (bf16[512,128]{1,0:T(8,128)(2,1)S(1)}, bf16[512,128]{1,0:T(8,128)(2,1)S(1)}, u32[]{:S(2)}, u32[]{:S(2)}) collective-permute-start(bf16[512,128]{1,0:T(8,128)(2,1)S(1)} %get-tuple-element.44.high_ref.own_high), channel_id=1, source_target_pairs={{0,16},{8,24},{16,32},{24,40},{32,48},{40,56},{48,64},{56,72},{64,... | collective-permute-start | bytes 393224 | tf_op jit(solution)/shard_map/ppermute | solution.py:371
  21.0 8.6 %collective-permute-start.5 = (bf16[1024,128]{1,0:T(8,128)(2,1)S(1)}, bf16[1024,128]{1,0:T(8,128)(2,1)S(1)}, u32[]{:S(2)}, u32[]{:S(2)}) collective-permute-start(bf16[1024,128]{1,0:T(8,128)(2,1)S(1)} %get-tuple-element.53), channel_id=1, source_target_pairs={{0,240},{8,248},{16,0},{24,8},{32,16},{40,24},{48,32},{56,40},{64,... | collective-permute-start | bytes 786440 | tf_op jit(solution)/shard_map/ppermute | solution.py:371
  23.0 4.6 %collective-permute-start.6 = (bf16[512,1024]{1,0:T(8,128)(2,1)S(1)}, bf16[512,1024]{1,0:T(8,128)(2,1)S(1)}, u32[]{:S(2)}, u32[]{:S(2)}) collective-permute-start(bf16[512,1024]{1,0:T(8,128)(2,1)S(1)} %get-tuple-element.60), channel_id=1, source_target_pairs={{0,8},{8,0},{16,24},{24,16},{32,40},{40,32},{48,56},{56,48},{64,72... | collective-permute-start | bytes 3145736 | tf_op jit(solution)/shard_map/ppermute | solution.py:376

commit v6 on v5

--- a/solution.py
+++ b/solution.py
@@ -187,8 +187,9 @@
 
     @pl.when(is_even())
     def _():
-        low_total[...] += x_low[...]
-        high_total[...] += x_high[...]
+        for total, more in ((low_total, x_low), (high_total, x_high)):
+            total[:HALF, :] += more[:D, :].T
+            total[HALF:, :] += more[D:, :].T
 
 
 class Queries:
@@ -220,36 +221,36 @@
                 dq_ref[pl.ds(rows, HALF), cols] = x.astype(BF16)
         dv = dot(cat(g_t, 1), cat(ps, 0))
         dk = dot(cat(q_t, 1), cat(ds, 0))
-        return (dk * SCALE).T, dv.T
+        return dk * SCALE, dv
 
     def low_keys(self, keys, dq_ref, total):
         @pl.when(self.lows)
         def _():
             dk, dv = self.quadrants((self.high, self.low), keys, dq_ref, False)
-            total[:HALF, :] = dk
-            total[HALF:, :] = dv
+            total[:D, :] = dk
+            total[D:, :] = dv
 
         @pl.when(jnp.logical_not(self.lows))
         def _():
             dq_ref[pl.ds(self.low, HALF), :] = jnp.zeros((HALF, H * D), BF16)
             dk, dv = self.quadrants((self.high,), keys, dq_ref, False)
-            total[:HALF, :] = dk
-            total[HALF:, :] = dv
+            total[:D, :] = dk
+            total[D:, :] = dv
 
     def high_keys(self, keys, dq_ref, total, adds):
         @pl.when(jnp.logical_not(self.lows))
         def _():
             dk, dv = self.quadrants((self.high,), keys, dq_ref, True)
             if adds:
-                dk, dv = dk + total[:HALF, :], dv + total[HALF:, :]
-            total[:HALF, :] = dk
-            total[HALF:, :] = dv
+                dk, dv = dk + total[:D, :], dv + total[D:, :]
+            total[:D, :] = dk
+            total[D:, :] = dv
 
         if not adds:
 
             @pl.when(self.lows)
             def _():
-                total[...] = jnp.zeros((T, D), F32)
+                total[...] = jnp.zeros((2 * D, HALF), F32)
 
 
 def is_even():
@@ -269,6 +270,11 @@
     @pl.when(jnp.logical_not(even))
     def _():
         Queries(q2_ref, g2_ref, stat2_ref, theirs_low, stat_t).low_keys(theirs_low, send, x_low)
+
+
+def write_back(back, at, total):
+    back[at : at + HALF, :] = total[:D, :].T.astype(BF16)
+    back[at + HALF : at + T, :] = total[D:, :].T.astype(BF16)
 
 
 def high_kernel(q_ref, g_ref, stat_ref, q2_ref, g2_ref, stat2_ref, theirs_low, theirs_high, low_total, x_low, _, __, keep, send, back, high_total, stat_t):
@@ -279,15 +285,15 @@
 
     @pl.when(even)
     def _():
-        back[:T, :] = low_total[...].astype(BF16)
+        write_back(back, 0, low_total[...])
 
     @pl.when(jnp.logical_not(even))
     def _():
-        back[:T, :] = (low_total[...] + x_low[...]).astype(BF16)
+        write_back(back, 0, low_total[...] + x_low[...])
         others = Queries(q2_ref, g2_ref, stat2_ref, theirs_low, stat_t)
         others.high_keys(theirs_high, send, high_total, True)
 
-    back[T:, :] = high_total[...].astype(BF16)
+    write_back(back, T, high_total[...])
 
 
 def query_kernel(dq_ref, keep_ref, got_ref, out_hbm, out_ref, sems):
@@ -425,7 +431,7 @@
         low_kernel,
         "low_keys",
         (q, g, stat, q2, g2, stat2, low, high, theirs_low),
-        (rows, rows, half_terms, half_terms, half_terms),
+        (rows, rows) + (array((2 * D, HALF), F32),) * 3,
         (stat_t,),
         quadrants=3.5,
     )
@@ -435,7 +441,7 @@
         "high_keys",
         (q, g, stat, q2, g2, stat2, theirs_low, theirs_high, low_total, x_low, keep, send),
         (rows, rows, array((2 * T, D), BF16)),
-        (pltpu.VMEM((T, D), F32), stat_t),
+        (pltpu.VMEM((2 * D, HALF), F32), stat_t),
         quadrants=0.5,
         aliases={10: 0, 11: 1},
     )

time: 30.7 us -> 30.9 us (level)
  the two profiles are of different devices: /device:TPU:1 before, /device:TPU:102 now
where the time goes in v6:
time: 30.9 us; the launch traced here: 31.1 us
  Pallas kernels  16.7 us (54%)
  starting transfers between devices  8.17 us (26%)
  waiting for transfers between devices  5.5 us (18%)
  between operations  0.73 us (2%)
    pallas_call x8, Pallas kernels, call(): pl.pallas_call(kernel, in_specs=[hbm()] * from_hbm + [vmem()] * (len(ins)...  16.7 us
    ppermute x3, starting transfers between devices, passed_along(): return lax.ppermute(value, 'blk', pairs)  7.42 us
    ppermute x3, waiting for transfers between devices, passed_along(): return lax.ppermute(value, 'blk', pairs)  5.48 us
    ppermute x4, starting transfers between devices, swapped(): lax.ppermute(value, 'blk', [(source, source ^ 1) for source in range(coun...  0.75 us
  transfers between devices with their start and end apart: 7, of which 2 were waited for; matrix products, arithmetic and copies ran while one was open for 0% of the time, Pallas kernels for 42%

profile of v6, /device:TPU:102, one launch (start us, length us, event | category | flops | bytes accessed | tf_op | source)
XLA Modules:
  0.0 31.1 jit_solution(7019202612689138156)
XLA Ops:
  0.6 1.0 %pack.1 = (bf16[528,128]{1,0:T(8,128)(2,1)S(1)}, bf16[512,128]{1,0:T(8,128)(2,1)S(1)}) custom-call(bf16[512,128]{1,0:T(8,128)(2,1)} %k_hbm.1, bf16[512,128]{1,0:T(8,128)(2,1)} %v_hbm.1, s32[64]{0:T(128)} %pos_hbm.1), custom_call_target="tpu_custom_call" | custom-call | bytes 528640 | tf_op jit(solution)/shard_map/pack/pallas_call | solution.py:361
  1.6 4.0 %collective-permute-start.3 = (bf16[528,128]{1,0:T(8,128)(2,1)S(1)}, bf16[528,128]{1,0:T(8,128)(2,1)S(1)}, u32[]{:S(2)}, u32[]{:S(2)}) collective-permute-start(bf16[528,128]{1,0:T(8,128)(2,1)S(1)} %get-tuple-element.36.message.low_ref.own_low), channel_id=1, source_target_pairs={{0,16},{8,24},{16,32},{24,40},{32,48},{40,56},{48,64},{56,72},{64,... | collective-permute-start | bytes 405512 | tf_op jit(solution)/shard_map/ppermute | solution.py:377
  5.7 0.0 collective-permute-start
  5.7 0.5 %collective-permute-start.1 = (bf16[512,1024]{1,0:T(8,128)(2,1)}, bf16[512,1024]{1,0:T(8,128)(2,1)S(1)}, u32[]{:S(2)}, u32[]{:S(2)}) collective-permute-start(bf16[512,1024]{1,0:T(8,128)(2,1)} %g_hbm.1), channel_id=1, source_target_pairs={{0,8},{8,0},{16,24},{24,16},{32,40},{40,32},{48,56},{56,48},{64,72... | collective-permute-start | bytes 3145736 | tf_op jit(solution)/shard_map/ppermute | solution.py:382
  6.2 2.1 %stat.1 = (bf16[512,1024]{1,0:T(8,128)(2,1)S(1)}, bf16[512,1024]{1,0:T(8,128)(2,1)S(1)}, f32[24,512]{1,0:T(8,128)S(1)}) custom-call(bf16[512,1024]{1,0:T(8,128)(2,1)} %q_hbm.1, bf16[512,1024]{1,0:T(8,128)(2,1)} %g_hbm.1, bf16[512,1024]{1,0:T(8,128)(2,1)} %o_hbm.1, f32[8,512]{1,0:T(8,128)} %l_hbm.1, bf16[528,128]{1,0:T(8,128)(2,1)S(1)} %get-tuple-element.36.message.low_ref.own_low), custom_call_target="tpu_custom_call" | custom-call | flops 20132659200 | bytes 5443584 | tf_op jit(solution)/shard_map/stat/pallas_call | solution.py:361
  8.3 0.1 collective-permute-start.2
  8.4 2.2 %collective-permute-start.4 = (bf16[512,128]{1,0:T(8,128)(2,1)S(1)}, bf16[512,128]{1,0:T(8,128)(2,1)S(1)}, u32[]{:S(2)}, u32[]{:S(2)}) collective-permute-start(bf16[512,128]{1,0:T(8,128)(2,1)S(1)} %get-tuple-element.44.high_ref.own_high), channel_id=1, source_target_pairs={{0,16},{8,24},{16,32},{24,40},{32,48},{40,56},{48,64},{56,72},{64,... | collective-permute-start | bytes 393224 | tf_op jit(solution)/shard_map/ppermute | solution.py:377
  10.6 0.0 collective-permute-done.3.theirs_low
  10.7 0.0 collective-permute-done.2.stat2_ref
  10.7 0.0 collective-permute-done.q2_ref
  10.7 0.0 collective-permute-done.1.g2_ref
  10.7 4.8 %low_keys.1 = (bf16[512,1024]{1,0:T(8,128)(2,1)S(1)}, bf16[512,1024]{1,0:T(8,128)(2,1)S(1)}, f32[256,256]{1,0:T(8,128)S(1)}, f32[256,256]{1,0:T(8,128)S(1)}, f32[256,256]{1,0:T(8,128)S(1)}) custom-call(bf16[512,1024]{1,0:T(8,128)(2,1)S(1)} %get-tuple-element.37.q_ref, bf16[512,1024]{1,0:T(8,128)(2,1)S(1)} %get-tuple-element.38.g_ref, ...), custom_call_target="tpu_custom_call" | custom-call | flops 2348810240 | bytes 7577600 | tf_op jit(solution)/shard_map/low_keys/pallas_call | solution.py:361
  15.5 0.3 %collective-permute-done.4.theirs_high = bf16[512,128]{1,0:T(8,128)(2,1)S(1)} collective-permute-done((bf16[512,128]{1,0:T(8,128)(2,1)S(1)}, bf16[512,128]{1,0:T(8,128)(2,1)S(1)}, u32[]{:S(2)}, u32[]{:S(2)}) %collective-permute-start.4) | collective-permute-done | bytes 131104 | tf_op jit(solution)/shard_map/ppermute | solution.py:377
  15.8 1.8 %high_keys.1 = (bf16[512,1024]{1,0:T(8,128)(2,1)S(1)}, bf16[512,1024]{1,0:T(8,128)(2,1)S(1)}, bf16[1024,128]{1,0:T(8,128)(2,1)S(1)}) custom-call(bf16[512,1024]{1,0:T(8,128)(2,1)S(1)} %get-tuple-element.37.q_ref, bf16[512,1024]{1,0:T(8,128)(2,1)S(1)} %get-tuple-element.38.g_ref, ...), custom_call_target="tpu_custom_call", output_to_operand_aliasing={{0}: (10, {}), {1}: (11, {})} | custom-call | flops 335544320 | bytes 9539584 | tf_op jit(solution)/shard_map/high_keys/pallas_call | solution.py:361
  17.6 1.2 %collective-permute-start.5 = (bf16[1024,128]{1,0:T(8,128)(2,1)S(1)}, bf16[1024,128]{1,0:T(8,128)(2,1)S(1)}, u32[]{:S(2)}, u32[]{:S(2)}) collective-permute-start(bf16[1024,128]{1,0:T(8,128)(2,1)S(1)} %get-tuple-element.53), channel_id=1, source_target_pairs={{0,240},{8,248},{16,0},{24,8},{32,16},{40,24},{48,32},{56,40},{64,... | collective-permute-start | bytes 786440 | tf_op jit(solution)/shard_map/ppermute | solution.py:377
  18.8 0.1 collective-permute-start.6
  18.9 5.0 %own.1 = (f32[512,1024]{1,0:T(8,128)S(1)}, f32[512,128]{1,0:T(8,128)S(1)}, f32[512,128]{1,0:T(8,128)S(1)}) custom-call(bf16[512,1024]{1,0:T(8,128)(2,1)S(1)} %get-tuple-element.37.q_ref, bf16[512,1024]{1,0:T(8,128)(2,1)S(1)} %get-tuple-element.38.g_ref, ...), custom_call_target="tpu_custom_call", output_to_operand_aliasing={{0}: (7, {}), {1}: (8, {}), {2}: (9, {})} | custom-call | flops 40265318400 | bytes 8179712 | tf_op jit(solution)/shard_map/own/pallas_call | solution.py:361
  24.0 0.0 collective-permute-done.6.got_ref
  24.0 1.1 %query_sum.1 = bf16[512,1024]{1,0:T(8,128)(2,1)} custom-call(f32[512,1024]{1,0:T(8,128)S(1)} %get-tuple-element.58.dq_ref, bf16[512,1024]{1,0:T(8,128)(2,1)S(1)} %get-tuple-element.59.keep_ref, bf16[512,1024]{1,0:T(8,128)(2,1)S(1)} %collective-permute-done.6.got_ref), custom_call_target="tpu_custom_call" | custom-call | bytes 5242880 | tf_op jit(solution)/shard_map/query_sum/pallas_call | solution.py:361
  25.1 5.2 %collective-permute-done.5.got_ref = bf16[1024,128]{1,0:T(8,128)(2,1)S(1)} collective-permute-done((bf16[1024,128]{1,0:T(8,128)(2,1)S(1)}, bf16[1024,128]{1,0:T(8,128)(2,1)S(1)}, u32[]{:S(2)}, u32[]{:S(2)}) %collective-permute-start.5) | collective-permute-done | bytes 262176 | tf_op jit(solution)/shard_map/ppermute | solution.py:377
  30.3 0.8 %key_sum.1 = (bf16[512,128]{1,0:T(8,128)(2,1)}, bf16[512,128]{1,0:T(8,128)(2,1)}) custom-call(bf16[528,128]{1,0:T(8,128)(2,1)S(1)} %get-tuple-element.36.message.low_ref.own_low, f32[512,128]{1,0:T(8,128)S(1)} %get-tuple-element.62.low_total, f32[512,128]{1,0:T(8,128)S(1)} %get-tuple-element.63.high_total, bf16[1024,128]{1,0:T(8,128)(2,1)S(1)} %collective-permute-done.5.got_ref), custom_call_target="tpu_custom_call" | custom-call | bytes 1183744 | tf_op jit(solution)/shard_map/key_sum/pallas_call | solution.py:361
  (1 shorter events, 0.0 us)
Async XLA Ops:
  1.6 9.0 %collective-permute-start.3 = (bf16[528,128]{1,0:T(8,128)(2,1)S(1)}, bf16[528,128]{1,0:T(8,128)(2,1)S(1)}, u32[]{:S(2)}, u32[]{:S(2)}) collective-permute-start(bf16[528,128]{1,0:T(8,128)(2,1)S(1)} %get-tuple-element.36.message.low_ref.own_low), channel_id=1, source_target_pairs={{0,16},{8,24},{16,32},{24,40},{32,48},{40,56},{48,64},{56,72},{64,... | collective-permute-start | bytes 405512 | tf_op jit(solution)/shard_map/ppermute | solution.py:377
  5.7 5.0 %collective-permute-start = (bf16[512,1024]{1,0:T(8,128)(2,1)}, bf16[512,1024]{1,0:T(8,128)(2,1)S(1)}, u32[]{:S(2)}, u32[]{:S(2)}) collective-permute-start(bf16[512,1024]{1,0:T(8,128)(2,1)} %q_hbm.1), channel_id=1, source_target_pairs={{0,8},{8,0},{16,24},{24,16},{32,40},{40,32},{48,56},{56,48},{64,72... | collective-permute-start | bytes 3145736 | tf_op jit(solution)/shard_map/ppermute | solution.py:382
  5.7 5.0 %collective-permute-start.1 = (bf16[512,1024]{1,0:T(8,128)(2,1)}, bf16[512,1024]{1,0:T(8,128)(2,1)S(1)}, u32[]{:S(2)}, u32[]{:S(2)}) collective-permute-start(bf16[512,1024]{1,0:T(8,128)(2,1)} %g_hbm.1), channel_id=1, source_target_pairs={{0,8},{8,0},{16,24},{24,16},{32,40},{40,32},{48,56},{56,48},{64,72... | collective-permute-start | bytes 3145736 | tf_op jit(solution)/shard_map/ppermute | solution.py:382
  8.3 2.4 %collective-permute-start.2 = (f32[24,512]{1,0:T(8,128)S(1)}, f32[24,512]{1,0:T(8,128)S(1)}, u32[]{:S(2)}, u32[]{:S(2)}) collective-permute-start(f32[24,512]{1,0:T(8,128)S(1)} %get-tuple-element.41.stat_ref), channel_id=1, source_target_pairs={{0,8},{8,0},{16,24},{24,16},{32,40},{40,32},{48,56},{56,48},{64,72... | collective-permute-start | bytes 147464 | tf_op jit(solution)/shard_map/ppermute | solution.py:382
  8.4 7.4 %collective-permute-start.4 = (bf16[512,128]{1,0:T(8,128)(2,1)S(1)}, bf16[512,128]{1,0:T(8,128)(2,1)S(1)}, u32[]{:S(2)}, u32[]{:S(2)}) collective-permute-start(bf16[512,128]{1,0:T(8,128)(2,1)S(1)} %get-tuple-element.44.high_ref.own_high), channel_id=1, source_target_pairs={{0,16},{8,24},{16,32},{24,40},{32,48},{40,56},{48,64},{56,72},{64,... | collective-permute-start | bytes 393224 | tf_op jit(solution)/shard_map/ppermute | solution.py:377
  17.6 12.7 %collective-permute-start.5 = (bf16[1024,128]{1,0:T(8,128)(2,1)S(1)}, bf16[1024,128]{1,0:T(8,128)(2,1)S(1)}, u32[]{:S(2)}, u32[]{:S(2)}) collective-permute-start(bf16[1024,128]{1,0:T(8,128)(2,1)S(1)} %get-tuple-element.53), channel_id=1, source_target_pairs={{0,240},{8,248},{16,0},{24,8},{32,16},{40,24},{48,32},{56,40},{64,... | collective-permute-start | bytes 786440 | tf_op jit(solution)/shard_map/ppermute | solution.py:377
  18.8 5.2 %collective-permute-start.6 = (bf16[512,1024]{1,0:T(8,128)(2,1)S(1)}, bf16[512,1024]{1,0:T(8,128)(2,1)S(1)}, u32[]{:S(2)}, u32[]{:S(2)}) collective-permute-start(bf16[512,1024]{1,0:T(8,128)(2,1)S(1)} %get-tuple-element.60), channel_id=1, source_target_pairs={{0,8},{8,0},{16,24},{24,16},{32,40},{40,32},{48,56},{56,48},{64,72... | collective-permute-start | bytes 3145736 | tf_op jit(solution)/shard_map/ppermute | solution.py:382

commit v7 on v6

--- a/solution.py
+++ b/solution.py
@@ -308,13 +308,19 @@
         copy.wait()
 
 
-def key_kernel(own_low, low_total, high_total, got_ref, dk_ref, dv_ref):
+def key_kernel(own_low, low_total, high_total, got_ref, dk_hbm, dv_hbm, out, sems):
     ql = low_row(piece_of(own_low))
     qh = pl.multiple_of(HALF - ql, HALF)
+    copies = []
     for total, rows, at in ((low_total, ql, 0), (high_total, qh, T)):
-        for out, n in ((dk_ref, 0), (dv_ref, HALF)):
-            got = got_ref[at + n : at + n + HALF, :].astype(F32)
-            out[pl.ds(rows, HALF), :] = (total[n : n + HALF, :] + got).astype(BF16)
+        for target, n in ((dk_hbm, 0), (dv_hbm, HALF)):
+            part = pl.ds(at + n, HALF)
+            out[part, :] = (total[n : n + HALF, :] + got_ref[part, :].astype(F32)).astype(BF16)
+            to = target.at[pl.ds(rows, HALF), :]
+            copies.append(pltpu.make_async_copy(out.at[part, :], to, sems.at[len(copies)]))
+            copies[-1].start()
+    for copy in copies:
+        copy.wait()
 
 
 def vmem():
@@ -466,7 +472,12 @@
     )
     back, dq = lax.optimization_barrier((back, dq))
     dk, dv = call(
-        key_kernel, "key_sum", (low, own_low, own_high, back), (array((T, D), BF16),) * 2
+        key_kernel,
+        "key_sum",
+        (low, own_low, own_high, back),
+        (array((T, D), BF16),) * 2,
+        (pltpu.VMEM((2 * T, D), BF16), pltpu.SemaphoreType.DMA((4,))),
+        to_hbm=2,
     )
     return dq, dk, dv
 

time: 30.9 us -> 30.6 us (level)
  the two profiles are of different devices: /device:TPU:102 before, /device:TPU:116 now
where the time goes in v7:
time: 30.6 us; the launch traced here: 30.3 us
  Pallas kernels  16.6 us (54%)
  starting transfers between devices  8.74 us (29%)
  waiting for transfers between devices  4.07 us (13%)
  between operations  0.94 us (3%)
    pallas_call x8, Pallas kernels, call(): pl.pallas_call(kernel, in_specs=[hbm()] * from_hbm + [vmem()] * (len(ins)...  16.6 us
    ppermute x3, starting transfers between devices, passed_along(): return lax.ppermute(value, 'blk', pairs)  7.28 us
    ppermute x3, waiting for transfers between devices, passed_along(): return lax.ppermute(value, 'blk', pairs)  4.06 us
    ppermute x4, starting transfers between devices, swapped(): lax.ppermute(value, 'blk', [(source, source ^ 1) for source in range(coun...  1.46 us
  transfers between devices with their start and end apart: 7, of which 1 were waited for; matrix products, arithmetic and copies ran while one was open for 0% of the time, Pallas kernels for 47%

profile of v7, /device:TPU:116, one launch (start us, length us, event | category | flops | bytes accessed | tf_op | source)
XLA Modules:
  0.0 30.3 jit_solution(15237136391346023)
XLA Ops:
  0.6 1.0 %pack.1 = (bf16[528,128]{1,0:T(8,128)(2,1)S(1)}, bf16[512,128]{1,0:T(8,128)(2,1)S(1)}) custom-call(bf16[512,128]{1,0:T(8,128)(2,1)} %k_hbm.1, bf16[512,128]{1,0:T(8,128)(2,1)} %v_hbm.1, s32[64]{0:T(128)} %pos_hbm.1), custom_call_target="tpu_custom_call" | custom-call | bytes 528640 | tf_op jit(solution)/shard_map/pack/pallas_call | solution.py:367
  1.6 3.1 %collective-permute-start.3 = (bf16[528,128]{1,0:T(8,128)(2,1)S(1)}, bf16[528,128]{1,0:T(8,128)(2,1)S(1)}, u32[]{:S(2)}, u32[]{:S(2)}) collective-permute-start(bf16[528,128]{1,0:T(8,128)(2,1)S(1)} %get-tuple-element.36.message.low_ref.own_low), channel_id=1, source_target_pairs={{0,16},{8,24},{16,32},{24,40},{32,48},{40,56},{48,64},{56,72},{64,... | collective-permute-start | bytes 405512 | tf_op jit(solution)/shard_map/ppermute | solution.py:383
  4.8 0.0 collective-permute-start
  4.8 0.5 %collective-permute-start.1 = (bf16[512,1024]{1,0:T(8,128)(2,1)}, bf16[512,1024]{1,0:T(8,128)(2,1)S(1)}, u32[]{:S(2)}, u32[]{:S(2)}) collective-permute-start(bf16[512,1024]{1,0:T(8,128)(2,1)} %g_hbm.1), channel_id=1, source_target_pairs={{0,8},{8,0},{16,24},{24,16},{32,40},{40,32},{48,56},{56,48},{64,72... | collective-permute-start | bytes 3145736 | tf_op jit(solution)/shard_map/ppermute | solution.py:388
  5.3 2.1 %stat.1 = (bf16[512,1024]{1,0:T(8,128)(2,1)S(1)}, bf16[512,1024]{1,0:T(8,128)(2,1)S(1)}, f32[24,512]{1,0:T(8,128)S(1)}) custom-call(bf16[512,1024]{1,0:T(8,128)(2,1)} %q_hbm.1, bf16[512,1024]{1,0:T(8,128)(2,1)} %g_hbm.1, bf16[512,1024]{1,0:T(8,128)(2,1)} %o_hbm.1, f32[8,512]{1,0:T(8,128)} %l_hbm.1, bf16[528,128]{1,0:T(8,128)(2,1)S(1)} %get-tuple-element.36.message.low_ref.own_low), custom_call_target="tpu_custom_call" | custom-call | flops 20132659200 | bytes 5443584 | tf_op jit(solution)/shard_map/stat/pallas_call | solution.py:367
  7.4 0.1 collective-permute-start.2
  7.5 3.1 %collective-permute-start.4 = (bf16[512,128]{1,0:T(8,128)(2,1)S(1)}, bf16[512,128]{1,0:T(8,128)(2,1)S(1)}, u32[]{:S(2)}, u32[]{:S(2)}) collective-permute-start(bf16[512,128]{1,0:T(8,128)(2,1)S(1)} %get-tuple-element.44.high_ref.own_high), channel_id=1, source_target_pairs={{0,16},{8,24},{16,32},{24,40},{32,48},{40,56},{48,64},{56,72},{64,... | collective-permute-start | bytes 393224 | tf_op jit(solution)/shard_map/ppermute | solution.py:383
  10.6 0.0 collective-permute-done.3.theirs_low
  10.7 0.0 collective-permute-done.2.stat2_ref
  10.7 0.0 collective-permute-done.q2_ref
  10.7 0.0 collective-permute-done.1.g2_ref
  10.7 6.0 %low_keys.1 = (bf16[512,1024]{1,0:T(8,128)(2,1)S(1)}, bf16[512,1024]{1,0:T(8,128)(2,1)S(1)}, f32[256,256]{1,0:T(8,128)S(1)}, f32[256,256]{1,0:T(8,128)S(1)}, f32[256,256]{1,0:T(8,128)S(1)}) custom-call(bf16[512,1024]{1,0:T(8,128)(2,1)S(1)} %get-tuple-element.37.q_ref, bf16[512,1024]{1,0:T(8,128)(2,1)S(1)} %get-tuple-element.38.g_ref, ...), custom_call_target="tpu_custom_call" | custom-call | flops 2348810240 | bytes 7577600 | tf_op jit(solution)/shard_map/low_keys/pallas_call | solution.py:367
  16.7 0.0 collective-permute-done.4.theirs_high
  16.7 0.4 %high_keys.1 = (bf16[512,1024]{1,0:T(8,128)(2,1)S(1)}, bf16[512,1024]{1,0:T(8,128)(2,1)S(1)}, bf16[1024,128]{1,0:T(8,128)(2,1)S(1)}) custom-call(bf16[512,1024]{1,0:T(8,128)(2,1)S(1)} %get-tuple-element.37.q_ref, bf16[512,1024]{1,0:T(8,128)(2,1)S(1)} %get-tuple-element.38.g_ref, ...), custom_call_target="tpu_custom_call", output_to_operand_aliasing={{0}: (10, {}), {1}: (11, {})} | custom-call | flops 335544320 | bytes 9539584 | tf_op jit(solution)/shard_map/high_keys/pallas_call | solution.py:367
  17.1 1.0 %collective-permute-start.5 = (bf16[1024,128]{1,0:T(8,128)(2,1)S(1)}, bf16[1024,128]{1,0:T(8,128)(2,1)S(1)}, u32[]{:S(2)}, u32[]{:S(2)}) collective-permute-start(bf16[1024,128]{1,0:T(8,128)(2,1)S(1)} %get-tuple-element.53), channel_id=1, source_target_pairs={{0,240},{8,248},{16,0},{24,8},{32,16},{40,24},{48,32},{56,40},{64,... | collective-permute-start | bytes 786440 | tf_op jit(solution)/shard_map/ppermute | solution.py:383
  18.1 0.9 %collective-permute-start.6 = (bf16[512,1024]{1,0:T(8,128)(2,1)S(1)}, bf16[512,1024]{1,0:T(8,128)(2,1)S(1)}, u32[]{:S(2)}, u32[]{:S(2)}) collective-permute-start(bf16[512,1024]{1,0:T(8,128)(2,1)S(1)} %get-tuple-element.60), channel_id=1, source_target_pairs={{0,8},{8,0},{16,24},{24,16},{32,40},{40,32},{48,56},{56,48},{64,72... | collective-permute-start | bytes 3145736 | tf_op jit(solution)/shard_map/ppermute | solution.py:388
  19.0 5.0 %own.1 = (f32[512,1024]{1,0:T(8,128)S(1)}, f32[512,128]{1,0:T(8,128)S(1)}, f32[512,128]{1,0:T(8,128)S(1)}) custom-call(bf16[512,1024]{1,0:T(8,128)(2,1)S(1)} %get-tuple-element.37.q_ref, bf16[512,1024]{1,0:T(8,128)(2,1)S(1)} %get-tuple-element.38.g_ref, ...), custom_call_target="tpu_custom_call", output_to_operand_aliasing={{0}: (7, {}), {1}: (8, {}), {2}: (9, {})} | custom-call | flops 40265318400 | bytes 8179712 | tf_op jit(solution)/shard_map/own/pallas_call | solution.py:367
  24.0 0.0 collective-permute-done.6.got_ref
  24.1 1.1 %query_sum.1 = bf16[512,1024]{1,0:T(8,128)(2,1)} custom-call(f32[512,1024]{1,0:T(8,128)S(1)} %get-tuple-element.58.dq_ref, bf16[512,1024]{1,0:T(8,128)(2,1)S(1)} %get-tuple-element.59.keep_ref, bf16[512,1024]{1,0:T(8,128)(2,1)S(1)} %collective-permute-done.6.got_ref), custom_call_target="tpu_custom_call" | custom-call | bytes 5242880 | tf_op jit(solution)/shard_map/query_sum/pallas_call | solution.py:367
  25.2 4.1 %collective-permute-done.5.got_ref = bf16[1024,128]{1,0:T(8,128)(2,1)S(1)} collective-permute-done((bf16[1024,128]{1,0:T(8,128)(2,1)S(1)}, bf16[1024,128]{1,0:T(8,128)(2,1)S(1)}, u32[]{:S(2)}, u32[]{:S(2)}) %collective-permute-start.5) | collective-permute-done | bytes 262176 | tf_op jit(solution)/shard_map/ppermute | solution.py:383
  29.3 0.8 %key_sum.1 = (bf16[512,128]{1,0:T(8,128)(2,1)}, bf16[512,128]{1,0:T(8,128)(2,1)}) custom-call(bf16[528,128]{1,0:T(8,128)(2,1)S(1)} %get-tuple-element.36.message.low_ref.own_low, f32[512,128]{1,0:T(8,128)S(1)} %get-tuple-element.62.low_total, f32[512,128]{1,0:T(8,128)S(1)} %get-tuple-element.63.high_total, bf16[1024,128]{1,0:T(8,128)(2,1)S(1)} %collective-permute-done.5.got_ref), custom_call_target="tpu_custom_call" | custom-call | bytes 1183744 | tf_op jit(solution)/shard_map/key_sum/pallas_call | solution.py:367
  (1 shorter events, 0.0 us)
Async XLA Ops:
  1.6 9.0 %collective-permute-start.3 = (bf16[528,128]{1,0:T(8,128)(2,1)S(1)}, bf16[528,128]{1,0:T(8,128)(2,1)S(1)}, u32[]{:S(2)}, u32[]{:S(2)}) collective-permute-start(bf16[528,128]{1,0:T(8,128)(2,1)S(1)} %get-tuple-element.36.message.low_ref.own_low), channel_id=1, source_target_pairs={{0,16},{8,24},{16,32},{24,40},{32,48},{40,56},{48,64},{56,72},{64,... | collective-permute-start | bytes 405512 | tf_op jit(solution)/shard_map/ppermute | solution.py:383
  4.8 5.9 %collective-permute-start = (bf16[512,1024]{1,0:T(8,128)(2,1)}, bf16[512,1024]{1,0:T(8,128)(2,1)S(1)}, u32[]{:S(2)}, u32[]{:S(2)}) collective-permute-start(bf16[512,1024]{1,0:T(8,128)(2,1)} %q_hbm.1), channel_id=1, source_target_pairs={{0,8},{8,0},{16,24},{24,16},{32,40},{40,32},{48,56},{56,48},{64,72... | collective-permute-start | bytes 3145736 | tf_op jit(solution)/shard_map/ppermute | solution.py:388
  4.8 5.9 %collective-permute-start.1 = (bf16[512,1024]{1,0:T(8,128)(2,1)}, bf16[512,1024]{1,0:T(8,128)(2,1)S(1)}, u32[]{:S(2)}, u32[]{:S(2)}) collective-permute-start(bf16[512,1024]{1,0:T(8,128)(2,1)} %g_hbm.1), channel_id=1, source_target_pairs={{0,8},{8,0},{16,24},{24,16},{32,40},{40,32},{48,56},{56,48},{64,72... | collective-permute-start | bytes 3145736 | tf_op jit(solution)/shard_map/ppermute | solution.py:388
  7.4 3.3 %collective-permute-start.2 = (f32[24,512]{1,0:T(8,128)S(1)}, f32[24,512]{1,0:T(8,128)S(1)}, u32[]{:S(2)}, u32[]{:S(2)}) collective-permute-start(f32[24,512]{1,0:T(8,128)S(1)} %get-tuple-element.41.stat_ref), channel_id=1, source_target_pairs={{0,8},{8,0},{16,24},{24,16},{32,40},{40,32},{48,56},{56,48},{64,72... | collective-permute-start | bytes 147464 | tf_op jit(solution)/shard_map/ppermute | solution.py:388
  7.5 9.2 %collective-permute-start.4 = (bf16[512,128]{1,0:T(8,128)(2,1)S(1)}, bf16[512,128]{1,0:T(8,128)(2,1)S(1)}, u32[]{:S(2)}, u32[]{:S(2)}) collective-permute-start(bf16[512,128]{1,0:T(8,128)(2,1)S(1)} %get-tuple-element.44.high_ref.own_high), channel_id=1, source_target_pairs={{0,16},{8,24},{16,32},{24,40},{32,48},{40,56},{48,64},{56,72},{64,... | collective-permute-start | bytes 393224 | tf_op jit(solution)/shard_map/ppermute | solution.py:383
  17.1 12.2 %collective-permute-start.5 = (bf16[1024,128]{1,0:T(8,128)(2,1)S(1)}, bf16[1024,128]{1,0:T(8,128)(2,1)S(1)}, u32[]{:S(2)}, u32[]{:S(2)}) collective-permute-start(bf16[1024,128]{1,0:T(8,128)(2,1)S(1)} %get-tuple-element.53), channel_id=1, source_target_pairs={{0,240},{8,248},{16,0},{24,8},{32,16},{40,24},{48,32},{56,40},{64,... | collective-permute-start | bytes 786440 | tf_op jit(solution)/shard_map/ppermute | solution.py:383
  18.1 5.9 %collective-permute-start.6 = (bf16[512,1024]{1,0:T(8,128)(2,1)S(1)}, bf16[512,1024]{1,0:T(8,128)(2,1)S(1)}, u32[]{:S(2)}, u32[]{:S(2)}) collective-permute-start(bf16[512,1024]{1,0:T(8,128)(2,1)S(1)} %get-tuple-element.60), channel_id=1, source_target_pairs={{0,8},{8,0},{16,24},{24,16},{32,40},{40,32},{48,56},{56,48},{64,72... | collective-permute-start | bytes 3145736 | tf_op jit(solution)/shard_map/ppermute | solution.py:388
